TPU v7x, 128 devices: a whole 4x4x4 slice. The times are simulated.
128 devices in a mesh: ctx: 32 (over x, y, core), req: 4 (over z).
Axes of the slice: x: 4, y: 4, z: 4, core: 2. Of those that a mesh axis runs over, the one named last changes fastest.
Arguments:
- queries: bfloat16 [128, 4, 128, 576], P(('req', 'ctx')), may hold values from -32 to 32
- top_rows: int32 [128, 4, 2048], P(('req', 'ctx')), may hold values from 0 to 16383, as said below
- lengths: int32 [128], P(('req', 'ctx')), may hold values from 8196 to 16384, as said below
- span_map: int32 [64], replicated, may hold values from 0 to 31, as said below
- latent_cache: bfloat16 [128, 16384, 576], P('req', 'ctx'), may hold values from -5 to 5
- up_weight: bfloat16 [128, 512, 128], P('req'), may hold values from -2 to 2
- out_weight: bfloat16 [16384, 7168], P('req', 'ctx'), may hold values from -0.046875 to 0.046875
Outputs:
- attended: bfloat16 [128, 4, 7168], P('req', None, 'ctx')
Inputs may be any that keep to these rules, and one draw needn't show every extreme that they name: Each list top_rows[r, s] names 2048 distinct positions of request r, among them its newest position limit[r, s] - 1; positions at or past limit[r, s] may occur. At most 96 positions of one list are stored on one ctx device, and in every list one device stores exactly 96 of them. Step s of request r sees limit lengths[r] - 3 + s. `span_map`: entries c and 63 - c name the same device; every ctx device is named by exactly two entries, one in each half.
All inputs are finite; a program needn't handle non-finite values.
Results may differ from a plain program's by a relative error of at most 0.015.
Values may be sent and summed in bfloat16 or wider, within the bound.
A program may use at most 192 MiB of HBM per device.

v0:
```python
import jax
import jax.numpy as jnp
from jax import lax
from jax.sharding import PartitionSpec as P

score_scale = 192.0 ** (-0.5)
far_slot = 2**30


def locate(positions, span_map, width):
    devices = span_map.shape[0] // 2
    blocks = positions // width
    marks = blocks[..., None] == jnp.arange(span_map.shape[0], dtype=jnp.int32)
    holder = jnp.sum(jnp.where(marks, span_map, 0), axis=-1)
    local = jnp.where(blocks >= devices, width, 0) + positions % width
    return (holder, local)


def bucket(positions, holder, local, devices, capacity):
    lead = positions.shape[:-1]
    picks = positions.shape[-1]
    marks = (holder[..., None] == jnp.arange(devices, dtype=jnp.int32)).astype(jnp.int32)
    before = jnp.cumsum(marks, axis=-2) - marks
    rank = jnp.sum(before * marks, axis=-1)
    slot = (holder * capacity + rank).reshape(-1, picks)
    count = slot.shape[0]
    line = jnp.arange(count, dtype=jnp.int32)[:, None]
    wanted = (
        jnp.full((count, devices * capacity), -1, jnp.int32)
        .at[line, slot]
        .set(local.reshape(-1, picks))
    )
    places = (
        jnp.full((count, devices * capacity), far_slot, jnp.int32)
        .at[line, slot]
        .set(positions.reshape(-1, picks))
    )
    return (
        wanted.reshape(lead + (devices, capacity)),
        places.reshape(lead + (devices * capacity,)),
    )


def collect(latent_cache, wanted):
    owned, block_steps, owners, capacity = wanted.shape
    local_rows = latent_cache.shape[1]
    request = (
        jnp.arange(owners, dtype=jnp.int32)[None, None, :, None] * owned
        + jnp.arange(owned, dtype=jnp.int32)[:, None, None, None]
    )
    flat = request * local_rows + jnp.maximum(wanted, 0)
    table = latent_cache.reshape(-1, latent_cache.shape[2])
    return jnp.take(table, flat, axis=0)


def attend(queries, keys, places, limits, latent):
    scores = (
        jnp.einsum("rbhd,rbmd->rbhm", queries, keys, preferred_element_type=jnp.float32)
        * score_scale
    )
    valid = places < limits[..., None]
    scores = jnp.where(valid[:, :, None, :], scores, -jnp.inf)
    top = jnp.max(scores, axis=-1, keepdims=True)
    weights = jnp.exp(scores - top)
    probs = (weights / jnp.sum(weights, axis=-1, keepdims=True)).astype(jnp.bfloat16)
    mixed = jnp.einsum(
        "rbhm,rbmc->rbhc", probs, keys[..., :latent], preferred_element_type=jnp.float32
    )
    return mixed.astype(jnp.bfloat16)


def per_device(queries, top_rows, lengths, span_map, latent_cache, up_weight, out_weight):
    devices = lax.axis_size("ctx")
    groups = lax.axis_size("req")
    owned, steps, heads, depth = queries.shape
    latent = up_weight.shape[1]
    local_rows = latent_cache.shape[1]
    width = local_rows // 2
    capacity = 3 * top_rows.shape[2] // (2 * devices)
    ahead = jnp.arange(steps, dtype=jnp.int32) - steps + 1
    limits = lengths[:, None] + ahead[None, :]
    holder, local = locate(top_rows, span_map, width)
    pieces = []
    for step in range(steps):
        wanted, places = bucket(
            top_rows[:, step : step + 1],
            holder[:, step : step + 1],
            local[:, step : step + 1],
            devices,
            capacity,
        )
        asked = lax.all_to_all(wanted, "ctx", split_axis=2, concat_axis=2, tiled=True)
        found = lax.all_to_all(
            collect(latent_cache, asked), "ctx", split_axis=2, concat_axis=2, tiled=True
        )
        keys = found.reshape(owned, 1, devices * capacity, depth)
        pieces.append(
            attend(queries[:, step : step + 1], keys, places, limits[:, step : step + 1], latent)
        )
    latent_out = jnp.concatenate(pieces, axis=1)
    regrouped = lax.all_to_all(latent_out, "req", split_axis=2, concat_axis=0, tiled=True)
    head_values = jnp.einsum(
        "rshl,hle->rshe", regrouped, up_weight, preferred_element_type=jnp.float32
    ).astype(jnp.bfloat16)
    head_values = head_values.reshape(
        groups, owned * steps, head_values.shape[2] * head_values.shape[3]
    )
    terms = jnp.einsum(
        "gmf,fd->gmd",
        lax.all_gather(head_values, "ctx", axis=1, tiled=True),
        out_weight,
        preferred_element_type=jnp.float32,
    )
    summed = lax.psum_scatter(
        terms.astype(jnp.bfloat16), "req", scatter_dimension=0, tiled=True
    ).astype(jnp.float32)
    return summed.reshape(-1, steps, out_weight.shape[1]).astype(jnp.bfloat16)


def solution(mesh):
    return jax.shard_map(
        per_device,
        mesh=mesh,
        in_specs=(
            P(("req", "ctx"), None, None, None),
            P(("req", "ctx"), None, None),
            P(("req", "ctx")),
            P(),
            P("req", "ctx", None),
            P("req", None, None),
            P("req", "ctx"),
        ),
        out_specs=P("req", None, "ctx"),
        check_vma=False,
    )
```

profile of v0, /device:TPU:0, one launch (start us, length us, event | category | flops | bytes accessed | tf_op | source)
XLA Modules:
  0.0 530.2 jit_solution(17175584054882200860)
XLA Ops:
  8.7 9.1 %reduce-window.34 = s32[1,1,32,16,128]{4,3,2,1,0:T(8,128)S(1)} reduce-window(s32[1,1,32,16,128]{4,3,2,1,0:T(8,128)S(1)} %bitcast.232, s32[]{:T(128)} %constant.61.clone.1), window={size=1x1x1x1x128 pad=0_0x0_0x0_0x0_0x127_0}, to_apply=%region_15.17 | reduce-window | flops 8323072 | bytes 524292 | tf_op jit(solution)/shard_map/reduce-window.4
  18.7 9.1 %reduce-window.36 = s32[1,1,32,16,128]{4,3,2,1,0:T(8,128)S(1)} reduce-window(s32[1,1,32,16,128]{4,3,2,1,0:T(8,128)S(1)} %bitcast.233, s32[]{:T(128)} %constant.61.clone.1), window={size=1x1x1x1x128 pad=0_0x0_0x0_0x0_0x127_0}, to_apply=%region_22.24 | reduce-window | flops 8323072 | bytes 524292 | tf_op jit(solution)/shard_map/reduce-window.6
  28.8 9.1 %reduce-window.30 = s32[1,1,32,16,128]{4,3,2,1,0:T(8,128)S(1)} reduce-window(s32[1,1,32,16,128]{4,3,2,1,0:T(8,128)S(1)} %bitcast.234, s32[]{:T(128)} %constant.61.clone.1), window={size=1x1x1x1x128 pad=0_0x0_0x0_0x0_0x127_0}, to_apply=%region_8.10 | reduce-window | flops 8323072 | bytes 524292 | tf_op jit(solution)/shard_map/reduce-window.2
  38.9 9.1 %reduce-window.26 = s32[1,1,32,16,128]{4,3,2,1,0:T(8,128)S(1)} reduce-window(s32[1,1,32,16,128]{4,3,2,1,0:T(8,128)S(1)} %bitcast.235, s32[]{:T(128)} %constant.61.clone.1), window={size=1x1x1x1x128 pad=0_0x0_0x0_0x0_0x127_0}, to_apply=%region_1.2 | reduce-window | flops 8323072 | bytes 524292 | tf_op jit(solution)/shard_map/reduce-window
  50.4 1.7 reshape.926
  54.4 1.7 reshape.939
  57.4 1.7 reshape.913
  60.4 1.7 reshape.899
  64.7 8.1 %scatter_custom_fusion.1 = s32[3072]{0:T(1024)S(1)} fusion(s32[2048]{0:T(1024)S(1)} %get-tuple-element.61, s32[2048]{0:T(1024)S(1)} %bitcast.262, s32[]{:T(128)} %constant.64.clone.1), kind=kCustom, calls=%fused_computation.152 | custom fusion | bytes 12292
  73.5 7.4 %all-to-all-start = ((s32[1,1,32,96]{3,1,0,2:T(1,128)}), s32[1,1,32,96]{3,1,0,2:T(1,128)S(1)}, u32[]{:S(2)}, u32[]{:S(2)}) async-start(s32[1,1,32,96]{3,1,0,2:T(1,128)} %reshape.904), calls=%async_computation | async-start | bytes 32768 | tf_op jit(solution)/shard_map/all_to_all | solution.py:92
  80.9 8.1 %scatter_custom_fusion.3 = s32[3072]{0:T(1024)S(1)} fusion(s32[2048]{0:T(1024)S(1)} %get-tuple-element.60, s32[2048]{0:T(1024)S(1)} %bitcast.261, s32[]{:T(128)} %constant.64.clone.1), kind=kCustom, calls=%fused_computation.150 | custom fusion | bytes 12292
  89.7 7.4 %all-to-all-start.2 = ((s32[1,1,32,96]{3,1,0,2:T(1,128)}), s32[1,1,32,96]{3,1,0,2:T(1,128)S(1)}, u32[]{:S(2)}, u32[]{:S(2)}) async-start(s32[1,1,32,96]{3,1,0,2:T(1,128)} %reshape.917), calls=%async_computation.2 | async-start | bytes 32768 | tf_op jit(solution)/shard_map/all_to_all | solution.py:92
  97.1 8.1 %scatter_custom_fusion.5 = s32[3072]{0:T(1024)S(1)} fusion(s32[2048]{0:T(1024)S(1)} %get-tuple-element.59, s32[2048]{0:T(1024)S(1)} %bitcast.260, s32[]{:T(128)} %constant.64.clone.1), kind=kCustom, calls=%fused_computation.148 | custom fusion | bytes 12292
  105.8 7.4 %all-to-all-start.4 = ((s32[1,1,32,96]{3,1,0,2:T(1,128)}), s32[1,1,32,96]{3,1,0,2:T(1,128)S(1)}, u32[]{:S(2)}, u32[]{:S(2)}) async-start(s32[1,1,32,96]{3,1,0,2:T(1,128)} %reshape.930), calls=%async_computation.4 | async-start | bytes 32768 | tf_op jit(solution)/shard_map/all_to_all | solution.py:92
  113.2 8.1 %scatter_custom_fusion.7 = s32[3072]{0:T(1024)S(1)} fusion(s32[2048]{0:T(1024)S(1)} %get-tuple-element.58, s32[2048]{0:T(1024)S(1)} %bitcast.259, s32[]{:T(128)} %constant.64.clone.1), kind=kCustom, calls=%fused_computation.146 | custom fusion | bytes 12292
  122.0 7.9 %all-to-all-start.6 = ((s32[1,1,32,96]{3,1,0,2:T(1,128)}), s32[1,1,32,96]{3,1,0,2:T(1,128)S(1)}, u32[]{:S(2)}, u32[]{:S(2)}) async-start(s32[1,1,32,96]{3,1,0,2:T(1,128)} %reshape.943), calls=%async_computation.6 | async-start | bytes 32768 | tf_op jit(solution)/shard_map/all_to_all | solution.py:92
  129.9 28.2 %copy.68 = bf16[32,512,576]{2,1,0:T(8,128)(2,1)} copy(bf16[32,512,576]{1,2,0:T(8,128)(2,1)} %param.13) | data formatting | bytes 37748736 | tf_op args[4]
  158.3 23.4 %gather_fusion.3 = bf16[3072,576]{1,0:T(8,128)(2,1)} fusion(bf16[16384,576]{1,0:T(8,128)(2,1)} %bitcast.224, s32[3072]{0:T(1024)S(1)} %broadcast_clamp_fusion), kind=kCustom, calls=%fused_computation.3.clone | custom fusion | bytes 7090176 | tf_op jit(solution)/shard_map/jit(_take)/gather | solution.py:53
  181.7 3.9 broadcast_select_fusion
  185.5 7.6 %all-to-all-start.7 = ((bf16[1,1,32,96,576]{4,3,1,0,2:T(8,128)(2,1)}), bf16[1,1,32,96,576]{4,3,1,0,2:T(8,128)(2,1)}, u32[]{:S(2)}, u32[]{:S(2)}) async-start(bf16[1,1,32,96,576]{4,3,1,0,2:T(8,128)(2,1)} %broadcast_select_fusion), calls=%async_computation.7 | async-start | bytes 7864320 | tf_op jit(solution)/shard_map/all_to_all | solution.py:93
  193.2 23.4 %gather_fusion.2 = bf16[3072,576]{1,0:T(8,128)(2,1)} fusion(bf16[16384,576]{1,0:T(8,128)(2,1)} %bitcast.225, s32[3072]{0:T(1024)S(1)} %broadcast_clamp_fusion.1), kind=kCustom, calls=%fused_computation.2.clone | custom fusion | bytes 7090176 | tf_op jit(solution)/shard_map/jit(_take)/gather | solution.py:53
  216.7 3.8 broadcast_select_fusion.1
  220.5 22.4 %all-to-all-done.7 = bf16[1,1,32,96,576]{4,3,1,0,2:T(8,128)(2,1)} async-done(((bf16[1,1,32,96,576]{4,3,1,0,2:T(8,128)(2,1)}), bf16[1,1,32,96,576]{4,3,1,0,2:T(8,128)(2,1)}, u32[]{:S(2)}, u32[]{:S(2)}) %all-to-all-start.7) | async-done | bytes 3538976 | tf_op jit(solution)/shard_map/all_to_all | solution.py:93
  242.8 6.6 %all-to-all-start.5 = ((bf16[1,1,32,96,576]{4,3,1,0,2:T(8,128)(2,1)}), bf16[1,1,32,96,576]{4,3,1,0,2:T(8,128)(2,1)}, u32[]{:S(2)}, u32[]{:S(2)}) async-start(bf16[1,1,32,96,576]{4,3,1,0,2:T(8,128)(2,1)} %broadcast_select_fusion.1), calls=%async_computation.5 | async-start | bytes 7864320 | tf_op jit(solution)/shard_map/all_to_all | solution.py:93
  249.6 23.4 %gather_fusion = bf16[3072,576]{1,0:T(8,128)(2,1)} fusion(bf16[16384,576]{1,0:T(8,128)(2,1)} %bitcast.226, s32[3072]{0:T(1024)S(1)} %broadcast_clamp_fusion.3), kind=kCustom, calls=%fused_computation.clone | custom fusion | bytes 7090176 | tf_op jit(solution)/shard_map/jit(_take)/gather | solution.py:53
  273.0 3.8 broadcast_select_fusion.3
  276.7 22.4 %all-to-all-done.5 = bf16[1,1,32,96,576]{4,3,1,0,2:T(8,128)(2,1)} async-done(((bf16[1,1,32,96,576]{4,3,1,0,2:T(8,128)(2,1)}), bf16[1,1,32,96,576]{4,3,1,0,2:T(8,128)(2,1)}, u32[]{:S(2)}, u32[]{:S(2)}) %all-to-all-start.5) | async-done | bytes 3538976 | tf_op jit(solution)/shard_map/all_to_all | solution.py:93
  299.2 6.4 %all-to-all-start.1 = ((bf16[1,1,32,96,576]{4,3,1,0,2:T(8,128)(2,1)}), bf16[1,1,32,96,576]{4,3,1,0,2:T(8,128)(2,1)}, u32[]{:S(2)}, u32[]{:S(2)}) async-start(bf16[1,1,32,96,576]{4,3,1,0,2:T(8,128)(2,1)} %broadcast_select_fusion.3), calls=%async_computation.1 | async-start | bytes 7864320 | tf_op jit(solution)/shard_map/all_to_all | solution.py:93
  306.3 8.1 %scatter_custom_fusion.2 = s32[3072]{0:T(1024)S(1)} fusion(s32[2048]{0:T(1024)S(1)} %get-tuple-element.60, s32[2048]{0:T(1024)S(1)} %bitcast.266, s32[]{:T(128)} %constant.59.clone.1), kind=kCustom, calls=%fused_computation.158 | custom fusion | bytes 12292
  314.4 8.1 %scatter_custom_fusion = s32[3072]{0:T(1024)S(1)} fusion(s32[2048]{0:T(1024)S(1)} %get-tuple-element.61, s32[2048]{0:T(1024)S(1)} %bitcast.265, s32[]{:T(128)} %constant.59.clone.1), kind=kCustom, calls=%fused_computation.160 | custom fusion | bytes 12292
  322.4 8.1 %scatter_custom_fusion.6 = s32[3072]{0:T(1024)S(1)} fusion(s32[2048]{0:T(1024)S(1)} %get-tuple-element.58, s32[2048]{0:T(1024)S(1)} %bitcast.264, s32[]{:T(128)} %constant.59.clone.1), kind=kCustom, calls=%fused_computation.154 | custom fusion | bytes 12292
  330.5 8.1 %scatter_custom_fusion.4 = s32[3072]{0:T(1024)S(1)} fusion(s32[2048]{0:T(1024)S(1)} %get-tuple-element.59, s32[2048]{0:T(1024)S(1)} %bitcast.263, s32[]{:T(128)} %constant.59.clone.1), kind=kCustom, calls=%fused_computation.156 | custom fusion | bytes 12292
  340.6 23.4 %gather_fusion.1 = bf16[3072,576]{1,0:T(8,128)(2,1)} fusion(bf16[16384,576]{1,0:T(8,128)(2,1)} %bitcast.227, s32[3072]{0:T(1024)S(1)} %broadcast_clamp_fusion.2), kind=kCustom, calls=%fused_computation.1.clone | custom fusion | bytes 7090176 | tf_op jit(solution)/shard_map/jit(_take)/gather | solution.py:53
  364.0 3.8 broadcast_select_fusion.2
  367.8 7.8 %all-to-all-start.3 = ((bf16[1,1,32,96,576]{4,3,1,0,2:T(8,128)(2,1)}), bf16[1,1,32,96,576]{4,3,1,0,2:T(8,128)(2,1)}, u32[]{:S(2)}, u32[]{:S(2)}) async-start(bf16[1,1,32,96,576]{4,3,1,0,2:T(8,128)(2,1)} %broadcast_select_fusion.2), calls=%async_computation.3 | async-start | bytes 7864320 | tf_op jit(solution)/shard_map/all_to_all | solution.py:93
  376.9 3.8 fusion.89
  381.2 3.8 fusion.90
  385.4 3.8 fusion.92
  389.7 2.6 fusion.32
  392.3 2.6 fusion.33
  394.9 2.6 fusion.35
  397.6 27.7 %all-to-all-done.3 = bf16[1,1,32,96,576]{4,3,1,0,2:T(8,128)(2,1)} async-done(((bf16[1,1,32,96,576]{4,3,1,0,2:T(8,128)(2,1)}), bf16[1,1,32,96,576]{4,3,1,0,2:T(8,128)(2,1)}, u32[]{:S(2)}, u32[]{:S(2)}) %all-to-all-start.3) | async-done | bytes 3538976 | tf_op jit(solution)/shard_map/all_to_all | solution.py:93
  425.2 3.8 fusion.91
  429.5 2.8 fusion.34
  432.8 14.4 %all_to_all.58 = bf16[1,4,128,512]{3,1,0,2:T(4,128)(2,1)S(1)} all-to-all(bf16[1,4,128,512]{3,1,0,2:T(4,128)(2,1)S(1)} %copy.82), channel_id=1, replica_groups=mesh['ctx'=32,'req'=4] {'req'}, dimensions={2} | all-to-all | bytes 1048576 | tf_op jit(solution)/shard_map/all_to_all | solution.py:101
  449.0 44.3 %all-gather.2.cloned.1.call-done = bf16[4,128,4096]{2,0,1:T(4,128)(2,1)} async-done(((bf16[4,4,4096]{2,0,1:T(4,128)(2,1)}), bf16[4,128,4096]{2,0,1:T(4,128)(2,1)}) %all-gather.2.cloned.1.call-update) | async-done | bytes 4194320 | tf_op jit(solution)/shard_map/all_gather | solution.py:110
  493.3 7.6 %fusion.17 = bf16[4,128,224]{1,2,0:T(8,128)(2,1)} fusion(bf16[4096,224]{0,1:T(8,128)(2,1)S(1)} %copy-done, bf16[4,128,4096]{2,0,1:T(4,128)(2,1)} %all-gather.2.cloned.1.call-done), kind=kOutput, calls=%fused_computation.51 | convolution fusion | flops 939638784 | bytes 6258688 | tf_op jit(solution)/shard_map/gmf,fd->gmd/dot_general | solution.py:108
  501.0 20.4 %reduce-scatter.2.cloned.1.call-done = bf16[1,128,224]{1,2,0:T(8,128)(2,1)} async-done(((bf16[4,128,224]{1,2,0:T(8,128)(2,1)}), bf16[1,128,224]{1,2,0:T(8,128)(2,1)}) %reduce-scatter.2.cloned.1.call-update) | async-done | bytes 57360 | tf_op jit(solution)/shard_map/reduce_scatter | solution.py:114
  (108 shorter events, 27.0 us)
Async XLA Ops:
  6.5 486.8 %copy-start = (bf16[4096,224]{0,1:T(8,128)(2,1)S(1)}, bf16[4096,224]{0,1:T(8,128)(2,1)}, u32[]{:S(2)}) copy-start(bf16[4096,224]{0,1:T(8,128)(2,1)} %param.15) | copy-start | bytes 5505028
  48.1 7.9 %copy-start.1 = (s32[1,1,32,16,1]{4,3,2,1,0:T(8,128)S(1)}, s32[1,1,32,16,1]{4,3,2,1,0:T(8,128)}, u32[]{:S(2)}) copy-start(s32[1,1,32,16,1]{4,3,2,1,0:T(8,128)} %slice.154) | copy-start | bytes 6148
  56.2 5.8 %copy-start.2 = (s32[1,1,32,2048]{3,2,1,0:T(8,128)S(1)}, s32[1,1,32,2048]{3,2,1,0:T(8,128)}, u32[]{:S(2)}) copy-start(s32[1,1,32,2048]{3,2,1,0:T(8,128)} %reshape.926) | copy-start | bytes 786436
  56.5 7.8 %copy-start.6 = (s32[2]{0:T(128)S(1)}, s32[2]{0:T(128)}, u32[]{:S(2)}) copy-start(s32[2]{0:T(128)} %constant.88) | copy-start | bytes 28
  56.5 8.1 %copy-start.5 = (s32[2]{0:T(128)S(1)}, s32[2]{0:T(128)}, u32[]{:S(2)}) copy-start(s32[2]{0:T(128)} %constant.85) | copy-start | bytes 28
  59.2 3.9 copy-start.3
  73.5 16.2 %all-to-all-start = ((s32[1,1,32,96]{3,1,0,2:T(1,128)}), s32[1,1,32,96]{3,1,0,2:T(1,128)S(1)}, u32[]{:S(2)}, u32[]{:S(2)}) async-start(s32[1,1,32,96]{3,1,0,2:T(1,128)} %reshape.904), calls=%async_computation | async-start | bytes 32768 | tf_op jit(solution)/shard_map/all_to_all | solution.py:92
  89.7 16.2 %all-to-all-start.2 = ((s32[1,1,32,96]{3,1,0,2:T(1,128)}), s32[1,1,32,96]{3,1,0,2:T(1,128)S(1)}, u32[]{:S(2)}, u32[]{:S(2)}) async-start(s32[1,1,32,96]{3,1,0,2:T(1,128)} %reshape.917), calls=%async_computation.2 | async-start | bytes 32768 | tf_op jit(solution)/shard_map/all_to_all | solution.py:92
  105.8 16.2 %all-to-all-start.4 = ((s32[1,1,32,96]{3,1,0,2:T(1,128)}), s32[1,1,32,96]{3,1,0,2:T(1,128)S(1)}, u32[]{:S(2)}, u32[]{:S(2)}) async-start(s32[1,1,32,96]{3,1,0,2:T(1,128)} %reshape.930), calls=%async_computation.4 | async-start | bytes 32768 | tf_op jit(solution)/shard_map/all_to_all | solution.py:92
  122.0 36.1 %all-to-all-start.6 = ((s32[1,1,32,96]{3,1,0,2:T(1,128)}), s32[1,1,32,96]{3,1,0,2:T(1,128)S(1)}, u32[]{:S(2)}, u32[]{:S(2)}) async-start(s32[1,1,32,96]{3,1,0,2:T(1,128)} %reshape.943), calls=%async_computation.6 | async-start | bytes 32768 | tf_op jit(solution)/shard_map/all_to_all | solution.py:92
  185.5 57.3 %all-to-all-start.7 = ((bf16[1,1,32,96,576]{4,3,1,0,2:T(8,128)(2,1)}), bf16[1,1,32,96,576]{4,3,1,0,2:T(8,128)(2,1)}, u32[]{:S(2)}, u32[]{:S(2)}) async-start(bf16[1,1,32,96,576]{4,3,1,0,2:T(8,128)(2,1)} %broadcast_select_fusion), calls=%async_computation.7 | async-start | bytes 7864320 | tf_op jit(solution)/shard_map/all_to_all | solution.py:93
  242.8 56.3 %all-to-all-start.5 = ((bf16[1,1,32,96,576]{4,3,1,0,2:T(8,128)(2,1)}), bf16[1,1,32,96,576]{4,3,1,0,2:T(8,128)(2,1)}, u32[]{:S(2)}, u32[]{:S(2)}) async-start(bf16[1,1,32,96,576]{4,3,1,0,2:T(8,128)(2,1)} %broadcast_select_fusion.1), calls=%async_computation.5 | async-start | bytes 7864320 | tf_op jit(solution)/shard_map/all_to_all | solution.py:93
  276.7 29.5 %copy-start.4 = (s32[1,4,2048]{2,1,0:T(4,128)S(1)}, s32[1,4,2048]{2,1,0:T(4,128)}, u32[]{:S(2)}) copy-start(s32[1,4,2048]{2,1,0:T(4,128)} %param.10) | copy-start | bytes 98308
  299.2 68.6 %all-to-all-start.1 = ((bf16[1,1,32,96,576]{4,3,1,0,2:T(8,128)(2,1)}), bf16[1,1,32,96,576]{4,3,1,0,2:T(8,128)(2,1)}, u32[]{:S(2)}, u32[]{:S(2)}) async-start(bf16[1,1,32,96,576]{4,3,1,0,2:T(8,128)(2,1)} %broadcast_select_fusion.3), calls=%async_computation.1 | async-start | bytes 7864320 | tf_op jit(solution)/shard_map/all_to_all | solution.py:93
  367.8 9.1 %copy-start.8 = (bf16[1,4,128,576]{2,3,1,0:T(8,128)(2,1)S(1)}, bf16[1,4,128,576]{2,3,1,0:T(8,128)(2,1)}, u32[]{:S(2)}) copy-start(bf16[1,4,128,576]{2,3,1,0:T(8,128)(2,1)} %param.9) | copy-start | bytes 1769476
  367.8 57.4 %all-to-all-start.3 = ((bf16[1,1,32,96,576]{4,3,1,0,2:T(8,128)(2,1)}), bf16[1,1,32,96,576]{4,3,1,0,2:T(8,128)(2,1)}, u32[]{:S(2)}, u32[]{:S(2)}) async-start(bf16[1,1,32,96,576]{4,3,1,0,2:T(8,128)(2,1)} %broadcast_select_fusion.2), calls=%async_computation.3 | async-start | bytes 7864320 | tf_op jit(solution)/shard_map/all_to_all | solution.py:93
  375.6 117.8 %all-gather.2.cloned.1.call-start = ((), (), s32[]{:S(2)}) async-start(), calls=%async_computation.10 | async-start | bytes 4325376 | tf_op jit(solution)/shard_map/all_gather | solution.py:110
  429.5 17.7 %copy-start.7 = (bf16[32,512,128]{2,1,0:T(8,128)(2,1)S(1)}, bf16[32,512,128]{2,1,0:T(8,128)(2,1)}, u32[]{:S(2)}) copy-start(bf16[32,512,128]{2,1,0:T(8,128)(2,1)} %param.14) | copy-start | bytes 12582916
  448.7 72.6 %reduce-scatter.2.cloned.1.call-start = ((), (), s32[]{:S(2)}) async-start(), calls=%async_computation.11 | async-start | bytes 286720 | tf_op jit(solution)/shard_map/reduce_scatter | solution.py:114
Sparse Core Ops, SparseCore 0:
  448.8 44.4 all-gather.1
  501.1 20.2 reduce-scatter.1
where the time goes:
time: 539 us; the launch traced here: 530 us
  local copies, waits for them, and re-layouts  209 us (39%)
  waiting for transfers between devices  137 us (25%)
  other arithmetic  61.4 us (11%)
  starting transfers between devices  58.9 us (11%)
  matrix products  34.3 us (6%)
  between operations  15 us (3%)
  blocking collectives  14.4 us (3%)
    gather x4, local copies, waits for them, and re-layouts, collect(): return jnp.take(table, flat, axis=0)  93.7 us
    unnamed x31, local copies, waits for them, and re-layouts  92.9 us
    all_to_all x4, waiting for transfers between devices, per_device(): lax.all_to_all(collect(latent_cache, asked), 'ctx', split_axis=2, concat_...  72.5 us
    all_gather x1, waiting for transfers between devices, per_device(): lax.all_gather(head_values, 'ctx', axis=1, tiled=True)  44.3 us
    another operation x8, other arithmetic  37 us
    all_to_all x4, starting transfers between devices, per_device(): lax.all_to_all(wanted, 'ctx', split_axis=2, concat_axis=2, tiled=True)  30.1 us
    all_to_all x4, starting transfers between devices, per_device(): lax.all_to_all(collect(latent_cache, asked), 'ctx', split_axis=2, concat_...  28.4 us
    reduce_scatter x1, waiting for transfers between devices, per_device(): lax.psum_scatter(terms.astype(jnp.bfloat16), 'req', scatter_dimension=0,...  20.4 us
  transfers between devices with their start and end apart: 10, of which 5 were waited for; matrix products, arithmetic and copies ran while one was open for 36% of the time, Pallas kernels for 0%

commit v1 on v0

v1 whole, which is shorter than its diff:
```python
import functools

import jax
import jax.numpy as jnp
from jax import lax
from jax.experimental import pallas as pl
from jax.experimental.pallas import tpu as pltpu
from jax.sharding import PartitionSpec as P

score_scale = 192.0 ** (-0.5)
log2_scale = score_scale * 1.4426950408889634
masked = -1e30
lowest = -16384.0


def stored_index(top_rows, limits, span_map, width):
    spans = span_map.shape[0]
    blocks = top_rows // width
    marks = blocks[..., None] == jnp.arange(spans, dtype=jnp.int32)
    holder = jnp.sum(jnp.where(marks, span_map, 0), axis=-1)
    local = jnp.where(blocks >= spans // 2, width, 0) + top_rows % width
    stored = holder * (2 * width) + local
    return jnp.where(top_rows < limits[..., None], stored, -1)


def mask_kernel(stored_ref, bias_ref):
    steps, picks = stored_ref.shape
    rows, lanes = bias_ref.shape[1:]
    for step in range(steps):
        line = stored_ref[step : step + 1, :]
        high = jnp.where(line < 0, -1, line // lanes)
        low = line % lanes
        row_hot = lax.broadcasted_iota(jnp.int32, (rows, picks), 0) == high
        lane_hot = lax.broadcasted_iota(jnp.int32, (lanes, picks), 0) == low
        count = lax.dot_general(
            row_hot.astype(jnp.float32).astype(jnp.bfloat16),
            lane_hot.astype(jnp.float32).astype(jnp.bfloat16),
            (((1,), (1,)), ((), ())),
            preferred_element_type=jnp.float32,
        )
        bias_ref[step] = jnp.where(count > 0.5, 0.0, masked).astype(jnp.bfloat16)


def unit(cache_t, bias, query_t, hot):
    latent = 512
    left = jnp.concatenate([cache_t, bias], axis=0)
    right = jnp.concatenate([query_t, hot], axis=0)
    scores = lax.dot_general(
        left, right, (((0,), (0,)), ((), ())), preferred_element_type=jnp.float32
    )
    top = jnp.max(scores, axis=0, keepdims=True) * log2_scale
    top = jnp.maximum(top, lowest).astype(jnp.bfloat16).astype(jnp.float32)
    weights = jnp.exp2(scores * log2_scale - top)
    total = jnp.sum(weights, axis=0, keepdims=True)
    mixed = jnp.dot(
        cache_t[:latent], weights.astype(jnp.bfloat16), preferred_element_type=jnp.float32
    )
    return mixed, top, total


def hot_rows(columns):
    row = lax.broadcasted_iota(jnp.int32, (16, columns), 0)
    col = lax.broadcasted_iota(jnp.int32, (16, columns), 1)
    return row, col // 128


def attend_kernel(cache_ref, bias_ref, query_ref, out_ref, stat_ref):
    pair = pl.program_id(1)
    row, step = hot_rows(256)
    hot = jnp.where(row == step + 2 * pair, 1.0, 0.0).astype(jnp.bfloat16)
    mixed, top, total = unit(cache_ref[0], bias_ref[0], query_ref[0, 0], hot)
    out_ref[0, 0] = mixed.astype(jnp.bfloat16)
    stat_ref[0, 0, 0:1] = top
    stat_ref[0, 0, 1:2] = total


def per_device(queries, top_rows, lengths, span_map, latent_cache, up_weight, out_weight):
    devices = lax.axis_size("ctx")
    groups = lax.axis_size("req")
    owned, steps, heads, depth = queries.shape
    latent = up_weight.shape[1]
    local_rows = latent_cache.shape[1]
    width = local_rows // 2
    requests = latent_cache.shape[0]
    ahead = jnp.arange(steps, dtype=jnp.int32) - steps + 1
    limits = lengths[:, None] + ahead[None, :]
    stored = stored_index(top_rows, limits, span_map, width)[0]
    bias = pl.pallas_call(
        mask_kernel,
        out_shape=jax.ShapeDtypeStruct((steps, 128, 128), jnp.bfloat16),
    )(stored)
    bias = bias.reshape(steps, devices, local_rows).transpose(1, 0, 2)
    bias = lax.all_to_all(bias, "ctx", split_axis=0, concat_axis=0, tiled=True)
    bias = jnp.pad(bias, ((0, 0), (0, 12), (0, 0)))

    query_t = jnp.swapaxes(queries, 2, 3).reshape(2, 2, depth, heads)
    query_t = query_t.transpose(0, 2, 1, 3).reshape(1, 2, depth, 2 * heads)
    query_t = lax.all_gather(query_t, "ctx", axis=0, tiled=True)
    cache_t = jnp.swapaxes(latent_cache, 1, 2)
    mixed, stats = pl.pallas_call(
        attend_kernel,
        grid=(requests, 2),
        in_specs=[
            pl.BlockSpec((1, depth, local_rows), lambda r, p: (r, 0, 0)),
            pl.BlockSpec((1, 16, local_rows), lambda r, p: (r, 0, 0)),
            pl.BlockSpec((1, 1, depth, 256), lambda r, p: (r, p, 0, 0)),
        ],
        out_specs=[
            pl.BlockSpec((1, 1, latent, 256), lambda r, p: (r, p, 0, 0)),
            pl.BlockSpec((1, 1, 2, 256), lambda r, p: (r, p, 0, 0)),
        ],
        out_shape=[
            jax.ShapeDtypeStruct((requests, 2, latent, 256), jnp.bfloat16),
            jax.ShapeDtypeStruct((requests, 2, 2, 256), jnp.float32),
        ],
    )(cache_t, bias, query_t)
    top = lax.pmax(stats[:, :, 0], "ctx")
    factor = jnp.exp2(stats[:, :, 0] - top)
    total = lax.psum_scatter(stats[:, :, 1] * factor, "ctx", scatter_dimension=0, tiled=True)
    mixed = (mixed.astype(jnp.float32) * factor[:, :, None, :]).astype(jnp.bfloat16)
    mixed = lax.psum_scatter(mixed, "ctx", scatter_dimension=0, tiled=True)
    latent_t = (mixed.astype(jnp.float32) / total[:, :, None, :]).astype(jnp.bfloat16)
    latent_out = latent_t.reshape(1, 2, latent, 2, heads).transpose(0, 1, 3, 4, 2)
    latent_out = latent_out.reshape(1, steps, heads, latent)

    regrouped = lax.all_to_all(latent_out, "req", split_axis=2, concat_axis=0, tiled=True)
    head_values = jnp.einsum(
        "rshl,hle->rshe", regrouped, up_weight, preferred_element_type=jnp.float32
    ).astype(jnp.bfloat16)
    head_values = head_values.reshape(
        groups, owned * steps, head_values.shape[2] * head_values.shape[3]
    )
    terms = jnp.einsum(
        "gmf,fd->gmd",
        lax.all_gather(head_values, "ctx", axis=1, tiled=True),
        out_weight,
        preferred_element_type=jnp.float32,
    )
    summed = lax.psum_scatter(
        terms.astype(jnp.bfloat16), "req", scatter_dimension=0, tiled=True
    ).astype(jnp.float32)
    return summed.reshape(-1, steps, out_weight.shape[1]).astype(jnp.bfloat16)


def solution(mesh):
    return jax.shard_map(
        per_device,
        mesh=mesh,
        in_specs=(
            P(("req", "ctx"), None, None, None),
            P(("req", "ctx"), None, None),
            P(("req", "ctx")),
            P(),
            P("req", "ctx", None),
            P("req", None, None),
            P("req", "ctx"),
        ),
        out_specs=P("req", None, "ctx"),
        check_vma=False,
    )
```

time: 539 us -> 577 us (1.071); the launches traced: 530 us -> 576 us
  waiting for transfers between devices: 137 us -> 412 us
  local copies, waits for them, and re-layouts: 209 us -> 12.9 us
  Pallas kernels: 0 us -> 76.4 us
  starting transfers between devices: 58.9 us -> 0.21 us
  other arithmetic: 61.4 us -> 20.5 us
  matrix products: 34.3 us -> 10.6 us
  blocking collectives: 14.4 us -> 28.6 us
    reduce_scatter x0 -> x1, waiting for transfers between devices: none -> 117 us  [per_device(): mixed = lax.psum_scatter(mixed, 'ctx', scatter_dimension=0, tiled=True)]
    pmax x0 -> x1, waiting for transfers between devices: none -> 94.1 us  [per_device(): top = lax.pmax(stats[:, :, 0], 'ctx')]
    gather x4 -> x0, local copies, waits for them, and re-layouts: 93.7 us -> none  [collect(): return jnp.take(table, flat, axis=0)]
    unnamed x31 -> x5, local copies, waits for them, and re-layouts: 92.9 us -> 1.17 us
    unnamed x2 -> x7, waiting for transfers between devices: 0.03 us -> 80.3 us
    pallas_call x0 -> x2, Pallas kernels: none -> 76.4 us  [the longest x1 74.1 us: per_device(): pl.pallas_call(attend_kernel, grid=(requests, 2), in_specs=[pl.BlockSpec(...]
    all_to_all x8 -> x0, waiting for transfers between devices: 72.5 us -> none  [the longest x4 72.5 us: per_device(): lax.all_to_all(collect(latent_cache, asked), 'ctx', split_axis=2, concat_...]
    all_to_all x8 -> x0, starting transfers between devices: 58.5 us -> none  [the longest x4 30.1 us: per_device(): lax.all_to_all(wanted, 'ctx', split_axis=2, concat_axis=2, tiled=True)]
  transfers between devices with their start and end apart: 10 -> 6, of which waited for: 5 -> 6; matrix products, arithmetic and copies ran while one was open for 36% -> 4% of each run, Pallas kernels for 0% -> 0%
where the time goes in v1:
time: 577 us; the launch traced here: 576 us
  waiting for transfers between devices  412 us (71%)
  Pallas kernels  76.4 us (13%)
  blocking collectives  28.6 us (5%)
  other arithmetic  20.5 us (4%)
  between operations  14.2 us (2%)
  local copies, waits for them, and re-layouts  12.9 us (2%)
  matrix products  10.6 us (2%)
    reduce_scatter x1, waiting for transfers between devices, per_device(): mixed = lax.psum_scatter(mixed, 'ctx', scatter_dimension=0, tiled=True)  117 us
    pmax x1, waiting for transfers between devices, per_device(): top = lax.pmax(stats[:, :, 0], 'ctx')  94.1 us
    unnamed x7, waiting for transfers between devices  80.3 us
    pallas_call x1, Pallas kernels, per_device(): pl.pallas_call(attend_kernel, grid=(requests, 2), in_specs=[pl.BlockSpec(...  74.1 us
    all_gather x1, waiting for transfers between devices, per_device(): query_t = lax.all_gather(query_t, 'ctx', axis=0, tiled=True)  56.6 us
    all_gather x1, waiting for transfers between devices, per_device(): lax.all_gather(head_values, 'ctx', axis=1, tiled=True)  43.6 us
    reduce_scatter x1, waiting for transfers between devices, per_device(): lax.psum_scatter(terms.astype(jnp.bfloat16), 'req', scatter_dimension=0,...  20.4 us
    all_to_all x1, blocking collectives, per_device(): bias = lax.all_to_all(bias, 'ctx', split_axis=0, concat_axis=0, tiled=True)  16.1 us
  transfers between devices with their start and end apart: 6, of which 6 were waited for; matrix products, arithmetic and copies ran while one was open for 4% of the time, Pallas kernels for 0%

profile of v1, /device:TPU:0, one launch (start us, length us, event | category | flops | bytes accessed | tf_op | source)
XLA Modules:
  0.0 575.6 jit_solution(6753949650158026571)
XLA Ops:
  6.5 0.0 copy-start
  6.5 0.0 all-gather.3.cloned.1.call-start
  6.5 1.8 copy.58
  8.3 1.2 reshape.64
  9.5 0.0 all-gather.3.cloned.1.call-update
  9.6 0.0 all-reduce.5.cloned.1.call-start
  10.3 0.8 fusion.24
  11.1 1.1 select_reduce_fusion
  12.1 1.5 fusion.21.stored_ref
  13.6 2.3 shard_map.73
  15.9 1.0 reshape.62
  16.9 0.1 copy.59
  17.0 16.1 %all_to_all.23 = bf16[32,4,512]{2,1,0:T(4,128)(2,1)S(1)} all-to-all(bf16[32,4,512]{2,1,0:T(4,128)(2,1)S(1)} %bitcast.64), channel_id=1, replica_groups=mesh['ctx'=32,'req'=4] {'ctx'}, dimensions={0} | all-to-all | bytes 262144 | tf_op jit(solution)/shard_map/all_to_all | solution.py:93
  33.1 0.9 pad.4.bias_ref
  34.0 56.6 %all-gather.3.cloned.1.call-done.query_ref = bf16[32,2,576,256]{3,2,1,0:T(8,128)(2,1)} async-done(((bf16[1,2,576,256]{3,2,1,0:T(8,128)(2,1)}), bf16[32,2,576,256]{3,2,1,0:T(8,128)(2,1)}) %all-gather.3.cloned.1.call-update) | async-done | bytes 18874384 | tf_op jit(solution)/shard_map/all_gather | solution.py:98
  90.6 74.1 %shard_map.74 = (bf16[32,2,512,256]{3,2,1,0:T(8,128)(2,1)}, f32[32,2,2,256]{3,2,1,0:T(2,128)}) custom-call(bf16[32,576,512]{2,1,0:T(8,128)(2,1)} %bitcast.59, bf16[32,16,512]{2,1,0:T(8,128)(2,1)} %pad.4.bias_ref, bf16[32,2,576,256]{3,2,1,0:T(8,128)(2,1)} %all-gather.3.cloned.1.call-done.query_ref), custom_call_target="tpu_custom_call" | custom-call | tf_op jit(solution)/shard_map/pallas_call | solution.py:100
  164.8 1.0 copy.31
  165.7 0.6 slice_bitcast_fusion
  166.4 0.0 all-reduce.5.cloned.1.call-update
  166.4 0.0 all-reduce.7.cloned.1.call-start
  166.5 1.0 slice.8
  167.4 94.1 %all-reduce.5.cloned.1.call-done = f32[32,2,256]{2,1,0:T(2,128)} async-done(((f32[32,2,256]{2,1,0:T(2,128)}), f32[32,2,256]{2,1,0:T(2,128)}) %all-reduce.5.cloned.1.call-update) | async-done | bytes 65552 | tf_op jit(solution)/shard_map/pmax | solution.py:117
  261.5 1.6 bitcast_multiply_fusion
  263.1 0.0 all-reduce.7.cloned.1.call-update
  263.1 0.0 reduce-scatter.3.cloned.1.call-start
  263.2 14.5 %multiply_convert_fusion = bf16[32,2,512,256]{3,2,1,0:T(8,128)(2,1)} fusion(bf16[32,2,512,256]{3,2,1,0:T(8,128)(2,1)} %get-tuple-element.7, f32[32,2,256]{2,1,0:T(2,128)S(1)} %get-tuple-element.10), kind=kLoop, calls=%fused_computation | loop fusion | flops 25165824 | bytes 33619968 | tf_op jit(solution)/shard_map/convert_element_type | solution.py:120
  277.7 0.0 reduce-scatter.3.cloned.1.call-update
  277.7 0.0 all-gather.5.cloned.1.call-start
  277.8 0.6 copy-done.1
  278.3 0.6 dynamic-slice
  278.9 80.2 %all-reduce.7.cloned.1.call-done = f32[32,2,256]{2,1,0:T(2,128)} async-done(((f32[32,2,256]{2,1,0:T(2,128)}), f32[32,2,256]{2,1,0:T(2,128)}) %all-reduce.7.cloned.1.call-update) | async-done | bytes 65552
  359.2 1.3 dynamic-slice_bitcast_fusion
  360.5 117.1 %reduce-scatter.3.cloned.1.call-done = bf16[1,2,512,256]{3,2,1,0:T(8,128)(2,1)} async-done(((bf16[32,2,512,256]{3,2,1,0:T(8,128)(2,1)}), bf16[1,2,512,256]{3,2,1,0:T(8,128)(2,1)}) %reduce-scatter.3.cloned.1.call-update) | async-done | bytes 524304 | tf_op jit(solution)/shard_map/reduce_scatter | solution.py:121
  477.5 1.1 divide_convert_fusion
  478.7 0.2 copy.41
  478.9 0.4 copy.33
  479.3 12.5 %all_to_all.24 = bf16[1,4,128,512]{3,1,0,2:T(4,128)(2,1)S(1)} all-to-all(bf16[1,4,128,512]{3,1,0,2:T(4,128)(2,1)S(1)} %copy.33), channel_id=1, replica_groups=mesh['ctx'=32,'req'=4] {'req'}, dimensions={2} | all-to-all | bytes 1048576 | tf_op jit(solution)/shard_map/all_to_all | solution.py:126
  491.8 3.0 fusion.13
  494.9 0.7 reshape.70
  495.5 0.0 all-gather.5.cloned.1.call-update
  495.5 0.0 reduce-scatter.5.cloned.1.call-start
  495.6 43.6 %all-gather.5.cloned.1.call-done = bf16[4,128,4096]{2,0,1:T(4,128)(2,1)} async-done(((bf16[4,4,4096]{2,0,1:T(4,128)(2,1)}), bf16[4,128,4096]{2,0,1:T(4,128)(2,1)}) %all-gather.5.cloned.1.call-update) | async-done | bytes 4194320 | tf_op jit(solution)/shard_map/all_gather | solution.py:135
  539.2 0.0 copy-done
  539.2 7.6 %fusion.5 = bf16[4,128,224]{1,2,0:T(8,128)(2,1)} fusion(bf16[4096,224]{0,1:T(8,128)(2,1)S(1)} %copy-done, bf16[4,128,4096]{2,0,1:T(4,128)(2,1)} %all-gather.5.cloned.1.call-done), kind=kOutput, calls=%fused_computation.8 | convolution fusion | flops 939638784 | bytes 6258688 | tf_op jit(solution)/shard_map/gmf,fd->gmd/dot_general | solution.py:133
  546.8 0.0 reduce-scatter.5.cloned.1.call-update
  546.8 20.4 %reduce-scatter.5.cloned.1.call-done = bf16[1,128,224]{1,2,0:T(8,128)(2,1)} async-done(((bf16[4,128,224]{1,2,0:T(8,128)(2,1)}), bf16[1,128,224]{1,2,0:T(8,128)(2,1)}) %reduce-scatter.5.cloned.1.call-update) | async-done | bytes 57360 | tf_op jit(solution)/shard_map/reduce_scatter | solution.py:139
  567.2 0.9 copy.39
  568.1 0.7 convert_element_type.35
  (3 shorter events, 0.0 us)
Async XLA Ops:
  6.5 532.6 %copy-start = (bf16[4096,224]{0,1:T(8,128)(2,1)S(1)}, bf16[4096,224]{0,1:T(8,128)(2,1)}, u32[]{:S(2)}) copy-start(bf16[4096,224]{0,1:T(8,128)(2,1)} %param.13) | copy-start | bytes 5505028
  6.5 84.1 %all-gather.3.cloned.1.call-start = ((), (), s32[]{:S(2)}) async-start(), calls=%async_computation.4 | async-start | bytes 19464192 | tf_op jit(solution)/shard_map/all_gather | solution.py:98
  9.6 252.0 %all-reduce.5.cloned.1.call-start = ((), (), s32[]{:S(2)}) async-start(), calls=%async_computation.5 | async-start | bytes 131072 | tf_op jit(solution)/shard_map/pmax | solution.py:117
  166.4 192.8 %all-reduce.7.cloned.1.call-start = ((), (), s32[]{:S(2)}) async-start(), calls=%async_computation.9 | async-start | bytes 131072
  263.1 214.4 %reduce-scatter.3.cloned.1.call-start = ((), (), s32[]{:S(2)}) async-start(), calls=%async_computation.6 | async-start | bytes 17301504 | tf_op jit(solution)/shard_map/reduce_scatter | solution.py:121
  277.7 0.7 copy-start.1
  277.7 261.4 %all-gather.5.cloned.1.call-start = ((), (), s32[]{:S(2)}) async-start(), calls=%async_computation.7 | async-start | bytes 4325376 | tf_op jit(solution)/shard_map/all_gather | solution.py:135
  495.5 71.6 %reduce-scatter.5.cloned.1.call-start = ((), (), s32[]{:S(2)}) async-start(), calls=%async_computation.8 | async-start | bytes 286720 | tf_op jit(solution)/shard_map/reduce_scatter | solution.py:139
Sparse Core Ops, SparseCore 0:
  9.7 80.8 all-gather.2
  166.5 94.9 all-reduce.4
  264.8 94.3 all-reduce.6
  363.4 114.0 reduce-scatter.2
  495.7 43.4 all-gather.4
  546.9 20.2 reduce-scatter.4

commit v2 on v1

v2 whole, which is shorter than its diff:
```python
import functools

import jax
import jax.numpy as jnp
from jax import lax
from jax.experimental import pallas as pl
from jax.experimental.pallas import tpu as pltpu
from jax.sharding import PartitionSpec as P

score_scale = 192.0 ** (-0.5)
log2_scale = score_scale * 1.4426950408889634
masked = -1e30
lowest = -16384.0


def stored_index(top_rows, limits, span_map, width):
    spans = span_map.shape[0]
    blocks = top_rows // width
    marks = blocks[..., None] == jnp.arange(spans, dtype=jnp.int32)
    holder = jnp.sum(jnp.where(marks, span_map, 0), axis=-1)
    local = jnp.where(blocks >= spans // 2, width, 0) + top_rows % width
    stored = holder * (2 * width) + local
    return jnp.where(top_rows < limits[..., None], stored, -1)


def mask_kernel(stored_ref, bias_ref):
    steps, picks = stored_ref.shape
    rows, lanes = bias_ref.shape[1:]
    for step in range(steps):
        line = stored_ref[step : step + 1, :]
        high = jnp.where(line < 0, -1, line // lanes)
        low = line % lanes
        row_hot = lax.broadcasted_iota(jnp.int32, (rows, picks), 0) == high
        lane_hot = lax.broadcasted_iota(jnp.int32, (lanes, picks), 0) == low
        count = lax.dot_general(
            row_hot.astype(jnp.float32).astype(jnp.bfloat16),
            lane_hot.astype(jnp.float32).astype(jnp.bfloat16),
            (((1,), (1,)), ((), ())),
            preferred_element_type=jnp.float32,
        )
        bias_ref[step] = jnp.where(count > 0.5, 0.0, masked).astype(jnp.bfloat16)


MESH = pl.DeviceIdType.MESH
side = 4
slots = side * side
key_rows = 592
latent_rows = 512
part_rows = 528


def attend_unit(keys, query):
    scores = lax.dot_general(
        query, keys, (((0,), (0,)), ((), ())), preferred_element_type=jnp.float32
    )
    top = jnp.max(scores, axis=1, keepdims=True) * log2_scale
    top = jnp.maximum(top, lowest).astype(jnp.bfloat16).astype(jnp.float32)
    weights = jnp.exp2(scores * log2_scale - top)
    total = jnp.sum(weights, axis=1, keepdims=True)
    mixed = lax.dot_general(
        weights.astype(jnp.bfloat16),
        keys[:latent_rows],
        (((1,), (1,)), ((), ())),
        preferred_element_type=jnp.float32,
    )
    mixed = jnp.swapaxes(mixed.astype(jnp.bfloat16), 0, 1)
    top = jnp.swapaxes(jnp.broadcast_to(top, (256, 128)), 0, 1)[0:16]
    total = jnp.swapaxes(jnp.broadcast_to(total, (256, 128)), 0, 1)[0:16]
    return mixed, stat_rows(top, total)


def stat_rows(top, total):
    row = lax.broadcasted_iota(jnp.int32, (16, 256), 0)
    high = total.astype(jnp.bfloat16).astype(jnp.float32)
    rows = jnp.where(row == 0, top, jnp.where(row == 1, high, total - high))
    return jnp.where(row < 3, rows, 0.0).astype(jnp.bfloat16)


def merge_weights(refs):
    stats = [ref[latent_rows:part_rows].astype(jnp.float32) for ref in refs]
    top = functools.reduce(jnp.maximum, [stat[0:1] for stat in stats])
    factors = [jnp.exp2(stat[0:1] - top) for stat in stats]
    total = sum(f * (stat[1:2] + stat[2:3]) for f, stat in zip(factors, stats))
    return top, factors, total


def merge(refs, out):
    top, factors, total = merge_weights(refs)

    def chunk(i, carry):
        rows = pl.ds(pl.multiple_of(i * 64, 64), 64)
        parts = [f * ref[rows].astype(jnp.float32) for f, ref in zip(factors, refs)]
        out[rows] = sum(parts[1:], parts[0]).astype(jnp.bfloat16)
        return carry

    lax.fori_loop(0, latent_rows // 64, chunk, 0)
    shape = (16, 256)
    out[latent_rows:part_rows] = stat_rows(
        jnp.broadcast_to(top, shape), jnp.broadcast_to(total, shape)
    )


def gather_attend_kernel(
    query_ref, bias_ref, cache_ref, out_ref,
    own, sib, kept, from_sib, ring_in, last_in, keys,
    load_sem, key_sem, own_recv, sib_recv, a_send, b_send, sib_send,
    part_send, part_recv, ring_send, ring_recv, last_send, last_recv,
):
    me = lax.axis_index("ctx")
    core = me % 2
    chip = me // 2
    a_step = 4 - 3 * core
    b_step = 1 + 3 * core
    a = (chip // a_step) % 4
    b = (chip // b_step) % 4

    def device(da, db):
        return (((a + da + 4) % 4) * a_step + ((b + db + 4) % 4) * b_step) * 2 + core

    sibling = chip * 2 + 1 - core
    barrier = pltpu.get_barrier_semaphore()
    partners = [device(1, 0), device(3, 0), device(2, 0), device(0, 1), device(0, 3), sibling]
    for partner in partners:
        pl.semaphore_signal(barrier, inc=1, device_id={"ctx": partner}, device_id_type=MESH)

    def own_request(flow, slot):
        da, db = slot % 4, slot // 4
        if flow == 0:
            da, db = 4 - da, 4 - db
        return (((a + da) % 4) * a_step + ((b + db) % 4) * b_step) * 2 + core

    def sib_request(flow, slot):
        da, db = slot % 4, slot // 4
        if flow == 0:
            da, db = 4 - da, 4 - db
        return (((b + da) % 4) * b_step + ((a + db) % 4) * a_step) * 2 + 1 - core

    def key_copies(slot, place):
        copies = []
        for flow in range(2):
            for which, request in ((0, own_request(flow, slot)), (1, sib_request(flow, slot))):
                at = 2 * which + flow
                copies.append(pltpu.make_async_copy(
                    cache_ref.at[request], keys.at[place, at, pl.ds(0, 576)],
                    key_sem.at[place, at, 0]))
                copies.append(pltpu.make_async_copy(
                    bias_ref.at[request], keys.at[place, at, pl.ds(576, 16)],
                    key_sem.at[place, at, 1]))
        return copies

    def remote(src, dst, send, recv, target):
        return pltpu.make_async_remote_copy(
            src_ref=src, dst_ref=dst, send_sem=send, recv_sem=recv,
            device_id={"ctx": target}, device_id_type=MESH)

    body = pl.ds(0, 576)

    def a_copy(flow, slot):
        return remote(own.at[flow, slot, body], own.at[flow, slot + 1, body],
                      a_send.at[flow, slot], own_recv.at[flow, slot + 1],
                      device(1 - 2 * flow, 0))

    def b_copy(flow, slot):
        return remote(own.at[flow, slot, body], own.at[flow, slot + 4, body],
                      b_send.at[flow, slot], own_recv.at[flow, slot + 4],
                      device(0, 1 - 2 * flow))

    def sib_copy(flow, slot):
        return remote(own.at[flow, slot, body], sib.at[flow, slot, body],
                      sib_send.at[flow, slot], sib_recv.at[flow, slot], sibling)

    part = pl.ds(0, part_rows)

    def part_copy(flow, slot):
        return remote(sib.at[flow, slot, part], from_sib.at[flow, slot],
                      part_send.at[flow, slot], part_recv.at[flow, slot], sibling)

    def ring_copy(flow, slot):
        return remote(kept.at[flow, slot], ring_in.at[flow, slot - 4],
                      ring_send.at[flow, slot - 4], ring_recv.at[flow, slot - 4],
                      device(0, 1 - 2 * flow))

    def last_copy(flow, da):
        return remote(kept.at[flow, da], last_in.at[flow, da - 1],
                      last_send.at[flow, da - 1], last_recv.at[flow, da - 1],
                      device(-da if flow == 0 else da - 4, 0))

    loads = [
        pltpu.make_async_copy(
            query_ref.at[2 * flow + half],
            own.at[flow, 0, body, pl.ds(128 * half, 128)],
            load_sem.at[flow, half])
        for flow in range(2) for half in range(2)
    ]
    for copy in loads:
        copy.start()
    for copy in key_copies(0, 0):
        copy.start()

    row = lax.broadcasted_iota(jnp.int32, (16, 256), 0)
    step = lax.broadcasted_iota(jnp.int32, (16, 256), 1) // 128
    for flow in range(2):
        hot = jnp.where(row == step + 2 * flow, 1.0, 0.0).astype(jnp.bfloat16)

        def fill(slot, carry):
            own[flow, slot, 576:key_rows] = hot
            sib[flow, slot, 576:key_rows] = hot
            return carry

        lax.fori_loop(0, slots, fill, 0)
    for copy in loads:
        copy.wait()
    pl.semaphore_wait(barrier, len(partners))

    def combine(slot):
        for flow in range(2):
            part_copy(flow, slot).wait_recv()

        @pl.when(slot < 8)
        def _():
            for flow in range(2):
                merge([kept.at[flow, slot], from_sib.at[flow, slot]], kept.at[flow, slot])
                ring_copy(flow, slot).start()

        @pl.when(slot >= 8)
        def _():
            for flow in range(2):
                ring_copy(flow, slot - 4).wait_recv()
                merge([kept.at[flow, slot], from_sib.at[flow, slot], ring_in.at[flow, slot - 8]],
                      kept.at[flow, slot])
                ring_copy(flow, slot).start()

    def iteration(slot, carry):
        place = slot % 2

        @pl.when(slot > 0)
        def _():
            for flow in range(2):
                b_or_a = remote(own.at[flow, slot, body], own.at[flow, slot, body],
                                a_send.at[flow, 0], own_recv.at[flow, slot], sibling)
                b_or_a.wait_recv()

        @pl.when(slot < 3)
        def _():
            for flow in range(2):
                a_copy(flow, slot).start()

        @pl.when(slot < 12)
        def _():
            for flow in range(2):
                b_copy(flow, slot).start()

        for flow in range(2):
            sib_copy(flow, slot).start()

        @pl.when(slot < slots - 1)
        def _():
            for copy in key_copies(slot + 1, 1 - place):
                copy.start()

        for copy in key_copies(slot, place):
            copy.wait()

        for flow in range(2):
            mixed, stats = attend_unit(keys[place, flow], own[flow, slot])
            kept[flow, slot, 0:latent_rows] = mixed
            kept[flow, slot, latent_rows:part_rows] = stats

        for flow in range(2):
            sib_copy(flow, slot).wait_recv()
        results = [attend_unit(keys[place, 2 + flow], sib[flow, slot]) for flow in range(2)]
        for flow in range(2):
            mixed, stats = results[flow]
            sib[flow, slot, 0:latent_rows] = mixed
            sib[flow, slot, latent_rows:part_rows] = stats
            part_copy(flow, slot).start()

        @pl.when(slot > 4)
        def _():
            combine(slot - 1)

        return carry

    lax.fori_loop(0, slots, iteration, 0)
    combine(slots - 1)

    for da in (1, 2, 3, 0):
        for flow in range(2):
            part_copy(flow, da).wait_recv()
            ring_copy(flow, 12 + da).wait_recv()
            merge([kept.at[flow, da], from_sib.at[flow, da], ring_in.at[flow, 8 + da]],
                  kept.at[flow, da])
            if da:
                last_copy(flow, da).start()
    for flow in range(2):
        for da in (1, 2, 3):
            last_copy(flow, da).wait_recv()
        refs = [kept.at[flow, 0]] + [last_in.at[flow, i] for i in range(3)]
        top, factors, total = merge_weights(refs)
        scale = 1.0 / total
        for i in range(latent_rows // 128):
            rows = pl.ds(128 * i, 128)
            parts = [f * scale * ref[rows].astype(jnp.float32) for f, ref in zip(factors, refs)]
            final = sum(parts[1:], parts[0]).astype(jnp.bfloat16)
            out_ref[flow, :, 128 * i : 128 * (i + 1)] = jnp.swapaxes(final, 0, 1)

    for flow in range(2):
        def drain(slot, carry):
            sib_copy(flow, slot).wait_send()
            part_copy(flow, slot).wait_send()

            @pl.when(slot < 3)
            def _():
                a_copy(flow, slot).wait_send()

            @pl.when(slot < 12)
            def _():
                b_copy(flow, slot).wait_send()
                ring_copy(flow, slot + 4).wait_send()

            return carry

        lax.fori_loop(0, slots, drain, 0)
        for da in (1, 2, 3):
            last_copy(flow, da).wait_send()


def gather_attend(query_t, bias, cache_t):
    dma = pltpu.SemaphoreType.DMA
    bf16 = jnp.bfloat16
    return pl.pallas_call(
        gather_attend_kernel,
        in_specs=[pl.BlockSpec(memory_space=pl.ANY)] * 3,
        out_specs=pl.BlockSpec(memory_space=pltpu.VMEM),
        out_shape=jax.ShapeDtypeStruct((2, 256, latent_rows), bf16),
        scratch_shapes=[
            pltpu.VMEM((2, slots, key_rows, 256), bf16),
            pltpu.VMEM((2, slots, key_rows, 256), bf16),
            pltpu.VMEM((2, slots, part_rows, 256), bf16),
            pltpu.VMEM((2, slots, part_rows, 256), bf16),
            pltpu.VMEM((2, 12, part_rows, 256), bf16),
            pltpu.VMEM((2, 3, part_rows, 256), bf16),
            pltpu.VMEM((2, 4, key_rows, 512), bf16),
            dma((2, 2)),
            dma((2, 4, 2)),
            dma((2, slots)),
            dma((2, slots)),
            dma((2, 3)),
            dma((2, 12)),
            dma((2, slots)),
            dma((2, slots)),
            dma((2, slots)),
            dma((2, 12)),
            dma((2, 12)),
            dma((2, 3)),
            dma((2, 3)),
        ],
        compiler_params=pltpu.CompilerParams(
            collective_id=0, has_side_effects=True, vmem_limit_bytes=58 * 2**20
        ),
        cost_estimate=pl.CostEstimate(
            flops=18_000_000_000, bytes_accessed=40_000_000, transcendentals=8_000_000
        ),
    )(query_t, bias, cache_t)


def per_device(queries, top_rows, lengths, span_map, latent_cache, up_weight, out_weight):
    devices = lax.axis_size("ctx")
    groups = lax.axis_size("req")
    owned, steps, heads, depth = queries.shape
    latent = up_weight.shape[1]
    local_rows = latent_cache.shape[1]
    width = local_rows // 2
    ahead = jnp.arange(steps, dtype=jnp.int32) - steps + 1
    limits = lengths[:, None] + ahead[None, :]
    stored = stored_index(top_rows, limits, span_map, width)[0]
    bias = pl.pallas_call(
        mask_kernel,
        out_shape=jax.ShapeDtypeStruct((steps, 128, 128), jnp.bfloat16),
    )(stored)
    bias = bias.reshape(steps, devices, local_rows).transpose(1, 0, 2)
    bias = lax.all_to_all(bias, "ctx", split_axis=0, concat_axis=0, tiled=True)
    bias = jnp.pad(bias, ((0, 0), (0, 12), (0, 0)))

    query_t = jnp.swapaxes(queries, 2, 3)[0]
    cache_t = jnp.swapaxes(latent_cache, 1, 2)
    mixed = gather_attend(query_t, bias, cache_t)
    latent_out = mixed.reshape(1, steps, heads, latent)

    regrouped = lax.all_to_all(latent_out, "req", split_axis=2, concat_axis=0, tiled=True)
    head_values = jnp.einsum(
        "rshl,hle->rshe", regrouped, up_weight, preferred_element_type=jnp.float32
    ).astype(jnp.bfloat16)
    head_values = head_values.reshape(
        groups, owned * steps, head_values.shape[2] * head_values.shape[3]
    )
    terms = jnp.einsum(
        "gmf,fd->gmd",
        lax.all_gather(head_values, "ctx", axis=1, tiled=True),
        out_weight,
        preferred_element_type=jnp.float32,
    )
    summed = lax.psum_scatter(
        terms.astype(jnp.bfloat16), "req", scatter_dimension=0, tiled=True
    ).astype(jnp.float32)
    return summed.reshape(-1, steps, out_weight.shape[1]).astype(jnp.bfloat16)


def solution(mesh):
    return jax.shard_map(
        per_device,
        mesh=mesh,
        in_specs=(
            P(("req", "ctx"), None, None, None),
            P(("req", "ctx"), None, None),
            P(("req", "ctx")),
            P(),
            P("req", "ctx", None),
            P("req", None, None),
            P("req", "ctx"),
        ),
        out_specs=P("req", None, "ctx"),
        check_vma=False,
    )
```

time: 577 us -> 240 us (0.42)
  waiting for transfers between devices: 412 us -> 64.5 us
  Pallas kernels: 76.4 us -> 115 us
  other arithmetic: 20.5 us -> 3.32 us
  local copies, waits for them, and re-layouts: 12.9 us -> 5.71 us
    reduce_scatter x1 -> x0, waiting for transfers between devices: 117 us -> none  [per_device(): mixed = lax.psum_scatter(mixed, 'ctx', scatter_dimension=0, tiled=True)]
    pmax x1 -> x0, waiting for transfers between devices: 94.1 us -> none  [per_device(): top = lax.pmax(stats[:, :, 0], 'ctx')]
    unnamed x7 -> x2, waiting for transfers between devices: 80.3 us -> 0.03 us
    all_gather x1 -> x0, waiting for transfers between devices: 56.6 us -> none  [per_device(): query_t = lax.all_gather(query_t, 'ctx', axis=0, tiled=True)]
    pallas_call x1, Pallas kernels: 74.1 us -> 113 us  [gather_attend(): pl.pallas_call(gather_attend_kernel, in_specs=[pl.BlockSpec(memory_space=...]
    convert_element_type x2 -> x0, other arithmetic: 15.6 us -> none  [the longest x1 14.5 us: per_device(): (mixed.astype(jnp.float32) * factor[:, :, None, :]).astype(jnp.bfloat16)]
  transfers between devices with their start and end apart: 6 -> 2, of which waited for: 6 -> 2; matrix products, arithmetic and copies ran while one was open for 4% -> 0% of each run, Pallas kernels for 0% -> 0%
where the time goes in v2:
time: 240 us
  Pallas kernels  115 us (48%)
  waiting for transfers between devices  64.5 us (27%)
  blocking collectives  28.2 us (12%)
  between operations  14.2 us (6%)
  matrix products  8.42 us (4%)
  local copies, waits for them, and re-layouts  5.71 us (2%)
  other arithmetic  3.32 us (1%)
    pallas_call x1, Pallas kernels, gather_attend(): pl.pallas_call(gather_attend_kernel, in_specs=[pl.BlockSpec(memory_space=...  113 us
    all_gather x1, waiting for transfers between devices, per_device(): lax.all_gather(head_values, 'ctx', axis=1, tiled=True)  44.1 us
    reduce_scatter x1, waiting for transfers between devices, per_device(): lax.psum_scatter(terms.astype(jnp.bfloat16), 'req', scatter_dimension=0,...  20.4 us
    all_to_all x1, blocking collectives, per_device(): bias = lax.all_to_all(bias, 'ctx', split_axis=0, concat_axis=0, tiled=True)  15.1 us
    all_to_all x1, blocking collectives, per_device(): lax.all_to_all(latent_out, 'req', split_axis=2, concat_axis=0, tiled=True)  13.2 us
    dot_general x1, matrix products, per_device(): jnp.einsum('gmf,fd->gmd', lax.all_gather(head_values, 'ctx', axis=1, tile...  7.61 us
  transfers between devices with their start and end apart: 2, of which 2 were waited for; matrix products, arithmetic and copies ran while one was open for 0% of the time, Pallas kernels for 0%

profile of v2, /device:TPU:0, one launch (start us, length us, event | category | flops | bytes accessed | tf_op | source)
XLA Modules:
  0.0 239.6 jit_solution(10627695957880600357)
XLA Ops:
  6.5 0.0 copy-start
  6.5 0.0 all-gather.2.cloned.1.call-start
  7.3 0.8 fusion.24
  8.1 1.1 select_reduce_fusion
  9.2 1.5 fusion.21.stored_ref
  10.7 2.3 shard_map.73
  12.9 1.0 reshape.49
  13.9 0.1 copy.43
  14.0 15.1 %all_to_all.23 = bf16[32,4,512]{2,1,0:T(4,128)(2,1)S(1)} all-to-all(bf16[32,4,512]{2,1,0:T(4,128)(2,1)S(1)} %bitcast.44), channel_id=1, replica_groups=mesh['ctx'=32,'req'=4] {'ctx'}, dimensions={0} | all-to-all | bytes 262144 | tf_op jit(solution)/shard_map/all_to_all | solution.py:382
  29.1 0.9 pad.4.bias_ref
  30.0 0.0 copy-start.1
  30.0 112.7 %shard_map.74 = bf16[2,256,512]{2,1,0:T(8,128)(2,1)} custom-call(bf16[4,576,128]{2,1,0:T(8,128)(2,1)} %bitcast.46, bf16[32,16,512]{2,1,0:T(8,128)(2,1)} %pad.4.bias_ref, bf16[32,576,512]{2,1,0:T(8,128)(2,1)} %bitcast.45), custom_call_target="tpu_custom_call" | custom-call | flops 17999998976 | bytes 40000000 | tf_op jit(solution)/shard_map/pallas_call | solution.py:331
  142.7 1.4 copy.22
  144.1 13.2 %all_to_all.24 = bf16[1,4,128,512]{3,1,0,2:T(4,128)(2,1)S(1)} all-to-all(bf16[1,4,128,512]{3,1,0,2:T(4,128)(2,1)S(1)} %copy.22), channel_id=1, replica_groups=mesh['ctx'=32,'req'=4] {'req'}, dimensions={2} | all-to-all | bytes 1048576 | tf_op jit(solution)/shard_map/all_to_all | solution.py:390
  157.3 0.0 copy-done.1
  157.3 0.8 fusion.13
  158.1 0.7 reshape.54
  158.8 0.0 all-gather.2.cloned.1.call-update
  158.8 0.2 reduce-scatter.2.cloned.1.call-start
  159.1 44.1 %all-gather.2.cloned.1.call-done = bf16[4,128,4096]{2,0,1:T(4,128)(2,1)} async-done(((bf16[4,4,4096]{2,0,1:T(4,128)(2,1)}), bf16[4,128,4096]{2,0,1:T(4,128)(2,1)}) %all-gather.2.cloned.1.call-update) | async-done | bytes 4194320 | tf_op jit(solution)/shard_map/all_gather | solution.py:399
  203.2 0.0 copy-done
  203.2 7.6 %fusion.5 = bf16[4,128,224]{1,2,0:T(8,128)(2,1)} fusion(bf16[4096,224]{0,1:T(8,128)(2,1)S(1)} %copy-done, bf16[4,128,4096]{2,0,1:T(4,128)(2,1)} %all-gather.2.cloned.1.call-done), kind=kOutput, calls=%fused_computation.7 | convolution fusion | flops 939638784 | bytes 6258688 | tf_op jit(solution)/shard_map/gmf,fd->gmd/dot_general | solution.py:397
  210.8 0.0 reduce-scatter.2.cloned.1.call-update
  210.8 20.4 %reduce-scatter.2.cloned.1.call-done = bf16[1,128,224]{1,2,0:T(8,128)(2,1)} async-done(((bf16[4,128,224]{1,2,0:T(8,128)(2,1)}), bf16[1,128,224]{1,2,0:T(8,128)(2,1)}) %reduce-scatter.2.cloned.1.call-update) | async-done | bytes 57360 | tf_op jit(solution)/shard_map/reduce_scatter | solution.py:403
  231.2 0.9 copy.28
  232.1 0.7 convert_element_type.19
  (2 shorter events, 0.0 us)
Async XLA Ops:
  6.5 196.6 %copy-start = (bf16[4096,224]{0,1:T(8,128)(2,1)S(1)}, bf16[4096,224]{0,1:T(8,128)(2,1)}, u32[]{:S(2)}) copy-start(bf16[4096,224]{0,1:T(8,128)(2,1)} %param.13) | copy-start | bytes 5505028
  6.5 196.6 %all-gather.2.cloned.1.call-start = ((), (), s32[]{:S(2)}) async-start(), calls=%async_computation.3 | async-start | bytes 4325376 | tf_op jit(solution)/shard_map/all_gather | solution.py:399
  30.0 127.3 %copy-start.1 = (bf16[32,512,128]{2,1,0:T(8,128)(2,1)S(1)}, bf16[32,512,128]{2,1,0:T(8,128)(2,1)}, u32[]{:S(2)}) copy-start(bf16[32,512,128]{2,1,0:T(8,128)(2,1)} %param.12) | copy-start | bytes 12582916
  158.8 72.4 %reduce-scatter.2.cloned.1.call-start = ((), (), s32[]{:S(2)}) async-start(), calls=%async_computation.4 | async-start | bytes 286720 | tf_op jit(solution)/shard_map/reduce_scatter | solution.py:403
Sparse Core Ops, SparseCore 0:
  159.0 44.1 all-gather.1
  210.9 20.2 reduce-scatter.1

commit v3 on v2

--- a/solution.py
+++ b/solution.py
@@ -364,11 +364,199 @@
     )(query_t, bias, cache_t)
 
 
+def project_kernel(
+    mixed_ref, up_ref, out_weight_ref, out_ref,
+    taken, wide, up, weight, values, sums, give, get,
+    load_sem, take_send, take_recv, own_recv, sib_recv, a_send, b_send, sib_send,
+    give_send, give_recv,
+):
+    me = lax.axis_index("ctx")
+    group = lax.axis_index("req")
+    core = me % 2
+    chip = me // 2
+    a_step = 4 - 3 * core
+    b_step = 1 + 3 * core
+    a = (chip // a_step) % 4
+    b = (chip // b_step) % 4
+
+    def device(da, db):
+        return {"ctx": (((a + da) % 4) * a_step + ((b + db) % 4) * b_step) * 2 + core}
+
+    def plane(d):
+        return {"req": (group + d) % 4}
+
+    sibling = {"ctx": chip * 2 + 1 - core}
+    partners = [device(1, 0), device(3, 0), device(0, 1), device(0, 3), sibling]
+    partners += [plane(1), plane(2), plane(3)]
+    barrier = pltpu.get_barrier_semaphore()
+    for partner in partners:
+        pl.semaphore_signal(barrier, inc=1, device_id=partner, device_id_type=MESH)
+
+    def remote(src, dst, send, recv, target):
+        return pltpu.make_async_remote_copy(
+            src_ref=src, dst_ref=dst, send_sem=send, recv_sem=recv,
+            device_id=target, device_id_type=MESH)
+
+    def heads_of(z):
+        return mixed_ref.at[:, pl.ds(pl.multiple_of(z * 32, 32), 32)]
+
+    loads = [
+        pltpu.make_async_copy(heads_of(group), taken.at[0], load_sem.at[0]),
+        pltpu.make_async_copy(up_ref, up, load_sem.at[1]),
+        pltpu.make_async_copy(out_weight_ref, weight.at[pl.ds(0, 224)], load_sem.at[2]),
+    ]
+    for copy in loads:
+        copy.start()
+    pl.semaphore_wait(barrier, len(partners))
+    takes = [
+        remote(heads_of((group + d) % 4), taken.at[d], take_send.at[d - 1],
+               take_recv.at[d - 1], plane(d))
+        for d in (1, 2, 3)
+    ]
+    for copy in takes:
+        copy.start()
+
+    weight[224:256] = jnp.zeros((32, 4096), jnp.bfloat16)
+    sums[...] = jnp.zeros_like(sums)
+    loads[0].wait()
+    loads[1].wait()
+    for d in range(4):
+        if d:
+            takes[d - 1].wait_recv()
+        for s in range(4):
+            rows = taken[d, s].astype(jnp.float32)
+            for i in range(4):
+                wide[i, 128 * d + 32 * s : 128 * d + 32 * s + 32] = rows[:, 128 * i : 128 * i + 128]
+
+    def a_copy(flow, slot):
+        return remote(values.at[flow, slot, 0], values.at[flow, slot + 1, 0],
+                      a_send.at[flow, slot], own_recv.at[flow, slot + 1],
+                      device(1 if flow == 0 else 3, 0))
+
+    def b_copy(flow, slot):
+        return remote(values.at[flow, slot, 0], values.at[flow, slot + 4, 0],
+                      b_send.at[flow, slot], own_recv.at[flow, slot + 4],
+                      device(0, 1 if flow == 0 else 3))
+
+    def sib_copy(flow, slot):
+        return remote(values.at[flow, slot, 0], values.at[flow, slot, 1],
+                      sib_send.at[flow, slot], sib_recv.at[flow, slot], sibling)
+
+    def forward(flow, slot):
+        if slot < 3:
+            a_copy(flow, slot).start()
+        if slot < 12:
+            b_copy(flow, slot).start()
+        sib_copy(flow, slot).start()
+
+    for flow in range(2):
+        for i in range(16):
+            head = 16 * flow + i
+            rows = [wide[j, pl.ds(head, 16, stride=32), :] for j in range(4)]
+            rows = jnp.concatenate(rows, axis=1).astype(jnp.bfloat16)
+            value = jnp.dot(rows, up[head], preferred_element_type=jnp.float32)
+            values[flow, 0, 0, :, 128 * i : 128 * i + 128] = value.astype(jnp.bfloat16)
+        forward(flow, 0)
+
+    loads[2].wait()
+    for slot in range(slots):
+        for flow in range(2):
+            if slot:
+                (a_copy(flow, slot - 1) if slot < 4 else b_copy(flow, slot - 4)).wait_recv()
+                forward(flow, slot)
+        if slot % 4 != 3:
+            continue
+        db = slot // 4
+        for flow in range(2):
+            for da in range(4):
+                sib_copy(flow, 4 * db + da).wait_recv()
+            left = values[flow, 4 * db : 4 * db + 4].reshape(128, 2048)
+            term = lax.dot_general(
+                left, weight[:, 2048 * flow : 2048 * flow + 2048],
+                (((1,), (1,)), ((), ())), preferred_element_type=jnp.float32)
+            for da in range(4):
+                ua, ub = (4 - da, 4 - db) if flow == 0 else (da, db)
+                origins = (
+                    (((a + ua) % 4) * a_step + ((b + ub) % 4) * b_step) * 2 + core,
+                    (((b + ua) % 4) * b_step + ((a + ub) % 4) * a_step) * 2 + 1 - core,
+                )
+                for which, origin in enumerate(origins):
+                    at = 16 * (2 * da + which)
+                    place = pl.ds(pl.multiple_of(origin * 16, 16), 16)
+                    for i in range(2):
+                        sums[i, place] += term[at : at + 16, 128 * i : 128 * i + 128]
+
+    def share(d, s):
+        return jnp.concatenate(
+            [sums[i, pl.ds(4 * d + s, 32, stride=16), :] for i in range(2)], axis=1)
+
+    gives = []
+    for d in (1, 2, 3):
+        for s in range(4):
+            give[d - 1, s] = share(d, s).astype(jnp.bfloat16)
+        copy = remote(give.at[d - 1], get.at[d - 1], give_send.at[d - 1], give_recv.at[d - 1],
+                      plane(4 - d))
+        copy.start()
+        gives.append(copy)
+    for copy in gives:
+        copy.wait_recv()
+    for s in range(4):
+        total = share(0, s)
+        for i in range(3):
+            total = total + get[i, s].astype(jnp.float32)
+        out_ref[s] = total[:, :224].astype(jnp.bfloat16)
+
+    for copy in takes + gives:
+        copy.wait_send()
+    for flow in range(2):
+        for slot in range(slots):
+            sib_copy(flow, slot).wait_send()
+            if slot < 3:
+                a_copy(flow, slot).wait_send()
+            if slot < 12:
+                b_copy(flow, slot).wait_send()
+
+
+def project(mixed, up_weight, out_weight_t):
+    dma = pltpu.SemaphoreType.DMA
+    bf16, f32 = jnp.bfloat16, jnp.float32
+    return pl.pallas_call(
+        project_kernel,
+        in_specs=[pl.BlockSpec(memory_space=pl.ANY)] * 3,
+        out_specs=pl.BlockSpec(memory_space=pltpu.VMEM),
+        out_shape=jax.ShapeDtypeStruct((4, 32, 224), bf16),
+        scratch_shapes=[
+            pltpu.VMEM((4, 4, 32, 512), bf16),
+            pltpu.VMEM((4, 512, 128), f32),
+            pltpu.VMEM((32, 512, 128), bf16),
+            pltpu.VMEM((256, 4096), bf16),
+            pltpu.VMEM((2, slots, 2, 16, 2048), bf16),
+            pltpu.VMEM((2, 512, 128), f32),
+            pltpu.VMEM((3, 4, 32, 256), bf16),
+            pltpu.VMEM((3, 4, 32, 256), bf16),
+            dma((3,)),
+            dma((3,)),
+            dma((3,)),
+            dma((2, slots)),
+            dma((2, slots)),
+            dma((2, 3)),
+            dma((2, 12)),
+            dma((2, slots)),
+            dma((3,)),
+            dma((3,)),
+        ],
+        compiler_params=pltpu.CompilerParams(
+            collective_id=1, has_side_effects=True, vmem_limit_bytes=40 * 2**20
+        ),
+        cost_estimate=pl.CostEstimate(
+            flops=1_100_000_000, bytes_accessed=8_000_000, transcendentals=0
+        ),
+    )(mixed, up_weight, out_weight_t)
+
+
 def per_device(queries, top_rows, lengths, span_map, latent_cache, up_weight, out_weight):
     devices = lax.axis_size("ctx")
-    groups = lax.axis_size("req")
-    owned, steps, heads, depth = queries.shape
-    latent = up_weight.shape[1]
+    steps, heads = queries.shape[1:3]
     local_rows = latent_cache.shape[1]
     width = local_rows // 2
     ahead = jnp.arange(steps, dtype=jnp.int32) - steps + 1
@@ -385,25 +573,8 @@
     query_t = jnp.swapaxes(queries, 2, 3)[0]
     cache_t = jnp.swapaxes(latent_cache, 1, 2)
     mixed = gather_attend(query_t, bias, cache_t)
-    latent_out = mixed.reshape(1, steps, heads, latent)
-
-    regrouped = lax.all_to_all(latent_out, "req", split_axis=2, concat_axis=0, tiled=True)
-    head_values = jnp.einsum(
-        "rshl,hle->rshe", regrouped, up_weight, preferred_element_type=jnp.float32
-    ).astype(jnp.bfloat16)
-    head_values = head_values.reshape(
-        groups, owned * steps, head_values.shape[2] * head_values.shape[3]
-    )
-    terms = jnp.einsum(
-        "gmf,fd->gmd",
-        lax.all_gather(head_values, "ctx", axis=1, tiled=True),
-        out_weight,
-        preferred_element_type=jnp.float32,
-    )
-    summed = lax.psum_scatter(
-        terms.astype(jnp.bfloat16), "req", scatter_dimension=0, tiled=True
-    ).astype(jnp.float32)
-    return summed.reshape(-1, steps, out_weight.shape[1]).astype(jnp.bfloat16)
+    out = project(mixed.reshape(steps, heads, -1), up_weight, out_weight.T)
+    return jnp.swapaxes(out, 0, 1)
 
 
 def solution(mesh):

time: 240 us -> 182 us (0.76)
  waiting for transfers between devices: 64.5 us -> 0 us
  Pallas kernels: 115 us -> 158 us
  between operations: 14.2 us -> 0.72 us
  blocking collectives: 28.2 us -> 15.1 us
  matrix products: 8.42 us -> 0 us
    all_gather x1 -> x0, waiting for transfers between devices: 44.1 us -> none  [per_device(): lax.all_gather(head_values, 'ctx', axis=1, tiled=True)]
    pallas_call x0 -> x1, Pallas kernels: none -> 42.6 us  [project(): pl.pallas_call(project_kernel, in_specs=[pl.BlockSpec(memory_space=pl.ANY...]
    reduce_scatter x1 -> x0, waiting for transfers between devices: 20.4 us -> none  [per_device(): lax.psum_scatter(terms.astype(jnp.bfloat16), 'req', scatter_dimension=0,...]
    all_to_all x1 -> x0, blocking collectives: 13.2 us -> none  [per_device(): lax.all_to_all(latent_out, 'req', split_axis=2, concat_axis=0, tiled=True)]
    dot_general x2 -> x0, matrix products: 8.42 us -> none  [the longest x1 7.61 us: per_device(): jnp.einsum('gmf,fd->gmd', lax.all_gather(head_values, 'ctx', axis=1, tile...]
  transfers between devices with their start and end apart: 2 -> 0, of which waited for: 2 -> 0; matrix products, arithmetic and copies ran while one was open for 0% -> 0% of each run, Pallas kernels for 0% -> 0%
where the time goes in v3:
time: 182 us; the launch traced here: 180 us
  Pallas kernels  158 us (87%)
  blocking collectives  15.1 us (8%)
  local copies, waits for them, and re-layouts  3.68 us (2%)
  other arithmetic  3.32 us (2%)
    pallas_call x1, Pallas kernels, gather_attend(): pl.pallas_call(gather_attend_kernel, in_specs=[pl.BlockSpec(memory_space=...  113 us
    pallas_call x1, Pallas kernels, project(): pl.pallas_call(project_kernel, in_specs=[pl.BlockSpec(memory_space=pl.ANY...  42.6 us
    all_to_all x1, blocking collectives, per_device(): bias = lax.all_to_all(bias, 'ctx', split_axis=0, concat_axis=0, tiled=True)  15.1 us

profile of v3, /device:TPU:0, one launch (start us, length us, event | category | flops | bytes accessed | tf_op | source)
XLA Modules:
  0.0 180.5 jit_solution(14809997132001437058)
XLA Ops:
  0.7 0.8 fusion.6
  1.5 1.1 select_reduce_fusion
  2.5 1.5 fusion.3.stored_ref
  4.0 2.3 %shard_map.73 = bf16[4,128,128]{2,1,0:T(8,128)(2,1)} custom-call(s32[4,2048]{1,0:T(4,128)} %fusion.3.stored_ref), custom_call_target="tpu_custom_call" | custom-call | tf_op jit(solution)/shard_map/pallas_call | solution.py:565
  6.2 1.0 reshape.44
  7.2 0.1 copy.14
  7.4 15.1 %all_to_all.5 = bf16[32,4,512]{2,1,0:T(4,128)(2,1)S(1)} all-to-all(bf16[32,4,512]{2,1,0:T(4,128)(2,1)S(1)} %bitcast.21), channel_id=1, replica_groups=mesh['ctx'=32,'req'=4] {'ctx'}, dimensions={0} | all-to-all | bytes 262144 | tf_op jit(solution)/shard_map/all_to_all | solution.py:570
  22.4 0.9 pad.4.bias_ref
  23.3 0.0 copy-start
  23.3 0.0 copy-start.1
  23.3 112.8 %shard_map.74 = bf16[2,256,512]{2,1,0:T(8,128)(2,1)} custom-call(bf16[4,576,128]{2,1,0:T(8,128)(2,1)} %bitcast.23, bf16[32,16,512]{2,1,0:T(8,128)(2,1)} %pad.4.bias_ref, bf16[32,576,512]{2,1,0:T(8,128)(2,1)} %bitcast.22), custom_call_target="tpu_custom_call" | custom-call | flops 17999998976 | bytes 40000000 | tf_op jit(solution)/shard_map/pallas_call | solution.py:331
  136.1 0.0 copy-done
  136.1 0.0 copy-done.1
  136.1 0.0 copy-start.2
  136.1 1.0 copy-done.2
  137.2 42.6 %shard_map.75 = bf16[4,32,224]{2,1,0:T(8,128)(2,1)S(1)} custom-call(bf16[4,128,512]{2,1,0:T(8,128)(2,1)S(1)} %bitcast.19, bf16[32,512,128]{2,1,0:T(8,128)(2,1)S(1)} %copy-done, bf16[224,4096]{1,0:T(8,128)(2,1)S(1)} %bitcast.18), custom_call_target="tpu_custom_call" | custom-call | flops 1100000000 | bytes 8000000 | tf_op jit(solution)/shard_map/pallas_call | solution.py:523
  179.8 0.7 copy.12
  (1 shorter events, 0.0 us)
Async XLA Ops:
  23.3 112.8 %copy-start = (bf16[32,512,128]{2,1,0:T(8,128)(2,1)S(1)}, bf16[32,512,128]{2,1,0:T(8,128)(2,1)}, u32[]{:S(2)}) copy-start(bf16[32,512,128]{2,1,0:T(8,128)(2,1)} %up_ref.1) | copy-start | bytes 12582916
  23.3 112.8 %copy-start.1 = (bf16[4096,224]{0,1:T(8,128)(2,1)S(1)}, bf16[4096,224]{0,1:T(8,128)(2,1)}, u32[]{:S(2)}) copy-start(bf16[4096,224]{0,1:T(8,128)(2,1)} %param.13) | copy-start | bytes 5505028
  136.1 1.0 copy-start.2

commit v4 on v3

--- a/solution.py
+++ b/solution.py
@@ -13,40 +13,13 @@
 lowest = -16384.0
 
 
-def stored_index(top_rows, limits, span_map, width):
-    spans = span_map.shape[0]
-    blocks = top_rows // width
-    marks = blocks[..., None] == jnp.arange(spans, dtype=jnp.int32)
-    holder = jnp.sum(jnp.where(marks, span_map, 0), axis=-1)
-    local = jnp.where(blocks >= spans // 2, width, 0) + top_rows % width
-    stored = holder * (2 * width) + local
-    return jnp.where(top_rows < limits[..., None], stored, -1)
-
-
-def mask_kernel(stored_ref, bias_ref):
-    steps, picks = stored_ref.shape
-    rows, lanes = bias_ref.shape[1:]
-    for step in range(steps):
-        line = stored_ref[step : step + 1, :]
-        high = jnp.where(line < 0, -1, line // lanes)
-        low = line % lanes
-        row_hot = lax.broadcasted_iota(jnp.int32, (rows, picks), 0) == high
-        lane_hot = lax.broadcasted_iota(jnp.int32, (lanes, picks), 0) == low
-        count = lax.dot_general(
-            row_hot.astype(jnp.float32).astype(jnp.bfloat16),
-            lane_hot.astype(jnp.float32).astype(jnp.bfloat16),
-            (((1,), (1,)), ((), ())),
-            preferred_element_type=jnp.float32,
-        )
-        bias_ref[step] = jnp.where(count > 0.5, 0.0, masked).astype(jnp.bfloat16)
-
-
 MESH = pl.DeviceIdType.MESH
 side = 4
 slots = side * side
 key_rows = 592
 latent_rows = 512
 part_rows = 528
+ahead = 2
 
 
 def attend_unit(keys, query):
@@ -100,9 +73,42 @@
     )
 
 
+def make_mask(span_ref, length_ref, rows_ref, line, place_in, mask_one, core, a, b):
+    picks = rows_ref[...]
+    block = picks // 256
+    holder = jnp.zeros_like(block)
+    for c in range(64):
+        holder = jnp.where(block == c, span_ref[c], holder)
+    place_in[...] = jnp.where(block >= 32, 256, 0) + picks % 256
+    x, y = holder // 8, (holder // 2) % 4
+    ea = (x * (1 - core) + y * core - a + 4) % 4
+    eb = (y * (1 - core) + x * core - b + 4) % 4
+    ec = (holder + core) % 2
+    step = lax.broadcasted_iota(jnp.int32, picks.shape, 0)
+    limit = length_ref[0] - 3 + step
+    line[...] = jnp.where(picks < limit, 32 * ea + 16 * ec + 4 * eb + step, -1)
+
+    def chunk(i, count):
+        columns = pl.ds(pl.multiple_of(i * 512, 512), 512)
+        for s in range(4):
+            left = lax.broadcasted_iota(jnp.int32, (128, 512), 0) == line[s : s + 1, columns]
+            right = lax.broadcasted_iota(jnp.int32, (512, 512), 0) == place_in[s : s + 1, columns]
+            count += lax.dot_general(
+                left.astype(jnp.float32).astype(jnp.bfloat16),
+                right.astype(jnp.float32).astype(jnp.bfloat16),
+                (((1,), (1,)), ((), ())), preferred_element_type=jnp.float32)
+        return count
+
+    count = lax.fori_loop(0, 4, chunk, jnp.zeros((128, 512), jnp.float32))
+    bias = jnp.where(count > 0.5, 0.0, masked).astype(jnp.bfloat16)
+    mask_one[...] = bias.reshape(4, 2, 16, 512)
+
+
 def gather_attend_kernel(
-    query_ref, bias_ref, cache_ref, out_ref,
+    span_ref, length_ref, rows_ref, query_ref, cache_ref, out_ref,
     own, sib, kept, from_sib, ring_in, last_in, keys,
+    line, place_in, mask_one, mask_mid, mask_two, mask_got, mask_own, mask_sib,
+    one_send, one_recv, two_send, two_recv, three_send, three_recv,
     load_sem, key_sem, own_recv, sib_recv, a_send, b_send, sib_send,
     part_send, part_recv, ring_send, ring_recv, last_send, last_recv,
 ):
@@ -119,7 +125,7 @@
 
     sibling = chip * 2 + 1 - core
     barrier = pltpu.get_barrier_semaphore()
-    partners = [device(1, 0), device(3, 0), device(2, 0), device(0, 1), device(0, 3), sibling]
+    partners = [device(d, 0) for d in (1, 2, 3)] + [device(0, d) for d in (1, 2, 3)] + [sibling]
     for partner in partners:
         pl.semaphore_signal(barrier, inc=1, device_id={"ctx": partner}, device_id_type=MESH)
 
@@ -142,10 +148,7 @@
                 at = 2 * which + flow
                 copies.append(pltpu.make_async_copy(
                     cache_ref.at[request], keys.at[place, at, pl.ds(0, 576)],
-                    key_sem.at[place, at, 0]))
-                copies.append(pltpu.make_async_copy(
-                    bias_ref.at[request], keys.at[place, at, pl.ds(576, 16)],
-                    key_sem.at[place, at, 1]))
+                    key_sem.at[place, at]))
         return copies
 
     def remote(src, dst, send, recv, target):
@@ -155,10 +158,10 @@
 
     body = pl.ds(0, 576)
 
-    def a_copy(flow, slot):
-        return remote(own.at[flow, slot, body], own.at[flow, slot + 1, body],
-                      a_send.at[flow, slot], own_recv.at[flow, slot + 1],
-                      device(1 - 2 * flow, 0))
+    def a_copy(flow, da):
+        return remote(own.at[flow, 0, body], own.at[flow, da, body],
+                      a_send.at[flow, da - 1], own_recv.at[flow, da],
+                      device(da if flow == 0 else 4 - da, 0))
 
     def b_copy(flow, slot):
         return remote(own.at[flow, slot, body], own.at[flow, slot + 4, body],
@@ -169,10 +172,10 @@
         return remote(own.at[flow, slot, body], sib.at[flow, slot, body],
                       sib_send.at[flow, slot], sib_recv.at[flow, slot], sibling)
 
-    part = pl.ds(0, part_rows)
+    partial = pl.ds(0, part_rows)
 
     def part_copy(flow, slot):
-        return remote(sib.at[flow, slot, part], from_sib.at[flow, slot],
+        return remote(sib.at[flow, slot, partial], from_sib.at[flow, slot],
                       part_send.at[flow, slot], part_recv.at[flow, slot], sibling)
 
     def ring_copy(flow, slot):
@@ -197,12 +200,15 @@
     for copy in key_copies(0, 0):
         copy.start()
 
+    make_mask(span_ref, length_ref, rows_ref, line, place_in, mask_one, core, a, b)
+
     row = lax.broadcasted_iota(jnp.int32, (16, 256), 0)
     step = lax.broadcasted_iota(jnp.int32, (16, 256), 1) // 128
     for flow in range(2):
-        hot = jnp.where(row == step + 2 * flow, 1.0, 0.0).astype(jnp.bfloat16)
 
         def fill(slot, carry):
+            da = slot % 4 if flow == 0 else (4 - slot % 4) % 4
+            hot = jnp.where(row == step + 2 * flow + 4 * da, 1.0, 0.0).astype(jnp.bfloat16)
             own[flow, slot, 576:key_rows] = hot
             sib[flow, slot, 576:key_rows] = hot
             return carry
@@ -211,6 +217,43 @@
     for copy in loads:
         copy.wait()
     pl.semaphore_wait(barrier, len(partners))
+
+    ones = [remote(mask_one.at[d], mask_mid.at[d], one_send.at[d - 1], one_recv.at[d - 1],
+                   device(d, 0)) for d in (1, 2, 3)]
+    for copy in ones:
+        copy.start()
+    for flow in range(2):
+        b_copy(flow, 0).start()
+        for da in (1, 2, 3):
+            a_copy(flow, da).start()
+        sib_copy(flow, 0).start()
+    for copy in ones:
+        copy.wait_recv()
+    for which in range(2):
+        lists = [mask_one[0, which].astype(jnp.float32)]
+        lists += [mask_mid[d, which].astype(jnp.float32) for d in (1, 2, 3)]
+        for eb in range(4):
+            rows = [part[4 * eb : 4 * eb + 4] for part in lists]
+            mask_two[eb, which] = jnp.concatenate(rows, axis=0).astype(jnp.bfloat16)
+    twos = [remote(mask_two.at[d], mask_got.at[d], two_send.at[d - 1], two_recv.at[d - 1],
+                   device(0, d)) for d in (1, 2, 3)]
+    for copy in twos:
+        copy.start()
+    for slot in (1, 2, 3):
+        for flow in range(2):
+            a_copy(flow, slot).wait_recv()
+            b_copy(flow, slot).start()
+            sib_copy(flow, slot).start()
+    for copy in twos:
+        copy.wait_recv()
+    mask_own[0] = mask_two[0, 0]
+    mask_own[4] = mask_two[0, 1]
+    for d in (1, 2, 3):
+        mask_own[d] = mask_got[d, 0]
+        mask_own[4 + d] = mask_got[d, 1]
+    three = remote(mask_own.at[pl.ds(4, 4)], mask_sib, three_send, three_recv, sibling)
+    three.start()
+    three.wait_recv()
 
     def combine(slot):
         for flow in range(2):
@@ -233,25 +276,20 @@
     def iteration(slot, carry):
         place = slot % 2
 
-        @pl.when(slot > 0)
+        @pl.when((slot >= 4 - ahead) & (slot < slots - ahead))
         def _():
             for flow in range(2):
-                b_or_a = remote(own.at[flow, slot, body], own.at[flow, slot, body],
-                                a_send.at[flow, 0], own_recv.at[flow, slot], sibling)
-                b_or_a.wait_recv()
-
-        @pl.when(slot < 3)
+                b_copy(flow, slot + ahead - 4).wait_recv()
+
+        @pl.when((slot >= 4 - ahead) & (slot < 12 - ahead))
         def _():
             for flow in range(2):
-                a_copy(flow, slot).start()
-
-        @pl.when(slot < 12)
+                b_copy(flow, slot + ahead).start()
+
+        @pl.when((slot >= 4 - ahead) & (slot < slots - ahead))
         def _():
             for flow in range(2):
-                b_copy(flow, slot).start()
-
-        for flow in range(2):
-            sib_copy(flow, slot).start()
+                sib_copy(flow, slot + ahead).start()
 
         @pl.when(slot < slots - 1)
         def _():
@@ -260,6 +298,10 @@
 
         for copy in key_copies(slot, place):
             copy.wait()
+        for flow in range(2):
+            db = slot // 4 if flow == 0 else (4 - slot // 4) % 4
+            keys[place, flow, 576:key_rows] = mask_own[db]
+            keys[place, 2 + flow, 576:key_rows] = mask_sib[db]
 
         for flow in range(2):
             mixed, stats = attend_unit(keys[place, flow], own[flow, slot])
@@ -309,10 +351,6 @@
             sib_copy(flow, slot).wait_send()
             part_copy(flow, slot).wait_send()
 
-            @pl.when(slot < 3)
-            def _():
-                a_copy(flow, slot).wait_send()
-
             @pl.when(slot < 12)
             def _():
                 b_copy(flow, slot).wait_send()
@@ -322,15 +360,20 @@
 
         lax.fori_loop(0, slots, drain, 0)
         for da in (1, 2, 3):
+            a_copy(flow, da).wait_send()
             last_copy(flow, da).wait_send()
-
-
-def gather_attend(query_t, bias, cache_t):
+    for copy in ones + twos + [three]:
+        copy.wait_send()
+
+
+def gather_attend(span_map, lengths, top_rows, query_t, cache_t):
     dma = pltpu.SemaphoreType.DMA
     bf16 = jnp.bfloat16
     return pl.pallas_call(
         gather_attend_kernel,
-        in_specs=[pl.BlockSpec(memory_space=pl.ANY)] * 3,
+        in_specs=[pl.BlockSpec(memory_space=pltpu.SMEM)] * 2
+        + [pl.BlockSpec(memory_space=pltpu.VMEM)]
+        + [pl.BlockSpec(memory_space=pl.ANY)] * 2,
         out_specs=pl.BlockSpec(memory_space=pltpu.VMEM),
         out_shape=jax.ShapeDtypeStruct((2, 256, latent_rows), bf16),
         scratch_shapes=[
@@ -341,8 +384,22 @@
             pltpu.VMEM((2, 12, part_rows, 256), bf16),
             pltpu.VMEM((2, 3, part_rows, 256), bf16),
             pltpu.VMEM((2, 4, key_rows, 512), bf16),
+            pltpu.VMEM((4, 2048), jnp.int32),
+            pltpu.VMEM((4, 2048), jnp.int32),
+            pltpu.VMEM((4, 2, 16, 512), bf16),
+            pltpu.VMEM((4, 2, 16, 512), bf16),
+            pltpu.VMEM((4, 2, 16, 512), bf16),
+            pltpu.VMEM((4, 2, 16, 512), bf16),
+            pltpu.VMEM((8, 16, 512), bf16),
+            pltpu.VMEM((4, 16, 512), bf16),
+            dma((3,)),
+            dma((3,)),
+            dma((3,)),
+            dma((3,)),
+            dma,
+            dma,
             dma((2, 2)),
-            dma((2, 4, 2)),
+            dma((2, 4)),
             dma((2, slots)),
             dma((2, slots)),
             dma((2, 3)),
@@ -361,7 +418,7 @@
         cost_estimate=pl.CostEstimate(
             flops=18_000_000_000, bytes_accessed=40_000_000, transcendentals=8_000_000
         ),
-    )(query_t, bias, cache_t)
+    )(span_map, lengths, top_rows, query_t, cache_t)
 
 
 def project_kernel(
@@ -386,7 +443,7 @@
         return {"req": (group + d) % 4}
 
     sibling = {"ctx": chip * 2 + 1 - core}
-    partners = [device(1, 0), device(3, 0), device(0, 1), device(0, 3), sibling]
+    partners = [device(1, 0), device(2, 0), device(3, 0), device(0, 1), device(0, 3), sibling]
     partners += [plane(1), plane(2), plane(3)]
     barrier = pltpu.get_barrier_semaphore()
     for partner in partners:
@@ -428,10 +485,10 @@
             for i in range(4):
                 wide[i, 128 * d + 32 * s : 128 * d + 32 * s + 32] = rows[:, 128 * i : 128 * i + 128]
 
-    def a_copy(flow, slot):
-        return remote(values.at[flow, slot, 0], values.at[flow, slot + 1, 0],
-                      a_send.at[flow, slot], own_recv.at[flow, slot + 1],
-                      device(1 if flow == 0 else 3, 0))
+    def a_copy(flow, da):
+        return remote(values.at[flow, 0, 0], values.at[flow, da, 0],
+                      a_send.at[flow, da - 1], own_recv.at[flow, da],
+                      device(da if flow == 0 else 4 - da, 0))
 
     def b_copy(flow, slot):
         return remote(values.at[flow, slot, 0], values.at[flow, slot + 4, 0],
@@ -443,10 +500,11 @@
                       sib_send.at[flow, slot], sib_recv.at[flow, slot], sibling)
 
     def forward(flow, slot):
-        if slot < 3:
-            a_copy(flow, slot).start()
         if slot < 12:
             b_copy(flow, slot).start()
+        if slot == 0:
+            for da in (1, 2, 3):
+                a_copy(flow, da).start()
         sib_copy(flow, slot).start()
 
     for flow in range(2):
@@ -462,7 +520,7 @@
     for slot in range(slots):
         for flow in range(2):
             if slot:
-                (a_copy(flow, slot - 1) if slot < 4 else b_copy(flow, slot - 4)).wait_recv()
+                (a_copy(flow, slot) if slot < 4 else b_copy(flow, slot - 4)).wait_recv()
                 forward(flow, slot)
         if slot % 4 != 3:
             continue
@@ -511,7 +569,7 @@
     for flow in range(2):
         for slot in range(slots):
             sib_copy(flow, slot).wait_send()
-            if slot < 3:
+            if 0 < slot < 4:
                 a_copy(flow, slot).wait_send()
             if slot < 12:
                 b_copy(flow, slot).wait_send()
@@ -555,24 +613,10 @@
 
 
 def per_device(queries, top_rows, lengths, span_map, latent_cache, up_weight, out_weight):
-    devices = lax.axis_size("ctx")
     steps, heads = queries.shape[1:3]
-    local_rows = latent_cache.shape[1]
-    width = local_rows // 2
-    ahead = jnp.arange(steps, dtype=jnp.int32) - steps + 1
-    limits = lengths[:, None] + ahead[None, :]
-    stored = stored_index(top_rows, limits, span_map, width)[0]
-    bias = pl.pallas_call(
-        mask_kernel,
-        out_shape=jax.ShapeDtypeStruct((steps, 128, 128), jnp.bfloat16),
-    )(stored)
-    bias = bias.reshape(steps, devices, local_rows).transpose(1, 0, 2)
-    bias = lax.all_to_all(bias, "ctx", split_axis=0, concat_axis=0, tiled=True)
-    bias = jnp.pad(bias, ((0, 0), (0, 12), (0, 0)))
-
     query_t = jnp.swapaxes(queries, 2, 3)[0]
     cache_t = jnp.swapaxes(latent_cache, 1, 2)
-    mixed = gather_attend(query_t, bias, cache_t)
+    mixed = gather_attend(span_map, lengths, top_rows[0], query_t, cache_t)
     out = project(mixed.reshape(steps, heads, -1), up_weight, out_weight.T)
     return jnp.swapaxes(out, 0, 1)
 

time: 182 us -> 168 us (0.923)
  blocking collectives: 15.1 us -> 0 us
  Pallas kernels: 158 us -> 164 us
  other arithmetic: 3.32 us -> 0 us
  local copies, waits for them, and re-layouts: 3.68 us -> 1.73 us
    all_to_all x1 -> x0, blocking collectives: 15.1 us -> none  [per_device(): bias = lax.all_to_all(bias, 'ctx', split_axis=0, concat_axis=0, tiled=True)]
    pallas_call x1, Pallas kernels: 113 us -> 124 us  [gather_attend(): pl.pallas_call(gather_attend_kernel, in_specs=[pl.BlockSpec(memory_space=...]
    pallas_call x1, Pallas kernels: 42.6 us -> 40 us  [project(): pl.pallas_call(project_kernel, in_specs=[pl.BlockSpec(memory_space=pl.ANY...]
    pallas_call x1 -> x0, Pallas kernels: 2.26 us -> none  [per_device(): pl.pallas_call(mask_kernel, out_shape=jax.ShapeDtypeStruct((steps, 128, 1...]
where the time goes in v4:
time: 168 us; the launch traced here: 167 us
  Pallas kernels  164 us (98%)
  local copies, waits for them, and re-layouts  1.73 us (1%)
    pallas_call x1, Pallas kernels, gather_attend(): pl.pallas_call(gather_attend_kernel, in_specs=[pl.BlockSpec(memory_space=...  124 us
    pallas_call x1, Pallas kernels, project(): pl.pallas_call(project_kernel, in_specs=[pl.BlockSpec(memory_space=pl.ANY...  40 us

profile of v4, /device:TPU:0, one launch (start us, length us, event | category | flops | bytes accessed | tf_op | source)
XLA Modules:
  0.0 166.9 jit_solution(4918521639114769267)
XLA Ops:
  0.7 0.0 copy-start
  0.7 0.0 copy-start.1
  0.7 124.5 %shard_map.73 = bf16[2,256,512]{2,1,0:T(8,128)(2,1)} custom-call(s32[64]{0:T(128)} %span_ref.1, s32[1]{0:T(128)S(6)} %copy.9.length_ref, s32[4,2048]{1,0:T(4,128)} %bitcast.13, bf16[4,576,128]{2,1,0:T(8,128)(2,1)} %bitcast.12, bf16[32,576,512]{2,1,0:T(8,128)(2,1)} %bitcast.11), custom_call_target="tpu_custom_call" | custom-call | flops 17999998976 | bytes 40000000 | tf_op jit(solution)/shard_map/pallas_call | solution.py:372
  125.2 0.0 copy-done
  125.2 0.0 copy-done.1
  125.2 0.0 copy-start.2
  125.2 1.0 copy-done.2
  126.2 40.0 %shard_map.74 = bf16[4,32,224]{2,1,0:T(8,128)(2,1)S(1)} custom-call(bf16[4,128,512]{2,1,0:T(8,128)(2,1)S(1)} %bitcast.9, bf16[32,512,128]{2,1,0:T(8,128)(2,1)S(1)} %copy-done, bf16[224,4096]{1,0:T(8,128)(2,1)S(1)} %bitcast.8), custom_call_target="tpu_custom_call" | custom-call | flops 1100000000 | bytes 8000000 | tf_op jit(solution)/shard_map/pallas_call | solution.py:581
  166.2 0.7 copy.8
Async XLA Ops:
  0.7 124.5 %copy-start = (bf16[32,512,128]{2,1,0:T(8,128)(2,1)S(1)}, bf16[32,512,128]{2,1,0:T(8,128)(2,1)}, u32[]{:S(2)}) copy-start(bf16[32,512,128]{2,1,0:T(8,128)(2,1)} %up_ref.1) | copy-start | bytes 12582916
  0.7 124.5 %copy-start.1 = (bf16[4096,224]{0,1:T(8,128)(2,1)S(1)}, bf16[4096,224]{0,1:T(8,128)(2,1)}, u32[]{:S(2)}) copy-start(bf16[4096,224]{0,1:T(8,128)(2,1)} %param.13) | copy-start | bytes 5505028
  125.2 1.0 copy-start.2

commit v5 on v4

--- a/solution.py
+++ b/solution.py
@@ -18,7 +18,6 @@
 slots = side * side
 key_rows = 592
 latent_rows = 512
-part_rows = 528
 ahead = 2
 
 
@@ -36,41 +35,26 @@
         (((1,), (1,)), ((), ())),
         preferred_element_type=jnp.float32,
     )
-    mixed = jnp.swapaxes(mixed.astype(jnp.bfloat16), 0, 1)
-    top = jnp.swapaxes(jnp.broadcast_to(top, (256, 128)), 0, 1)[0:16]
-    total = jnp.swapaxes(jnp.broadcast_to(total, (256, 128)), 0, 1)[0:16]
-    return mixed, stat_rows(top, total)
-
-
-def stat_rows(top, total):
-    row = lax.broadcasted_iota(jnp.int32, (16, 256), 0)
+    return mixed.astype(jnp.bfloat16), top, total
+
+
+def pack_stats(top, total):
+    lane = lax.broadcasted_iota(jnp.int32, (256, 128), 1)
     high = total.astype(jnp.bfloat16).astype(jnp.float32)
-    rows = jnp.where(row == 0, top, jnp.where(row == 1, high, total - high))
-    return jnp.where(row < 3, rows, 0.0).astype(jnp.bfloat16)
-
-
-def merge_weights(refs):
-    stats = [ref[latent_rows:part_rows].astype(jnp.float32) for ref in refs]
-    top = functools.reduce(jnp.maximum, [stat[0:1] for stat in stats])
-    factors = [jnp.exp2(stat[0:1] - top) for stat in stats]
-    total = sum(f * (stat[1:2] + stat[2:3]) for f, stat in zip(factors, stats))
-    return top, factors, total
-
-
-def merge(refs, out):
-    top, factors, total = merge_weights(refs)
-
-    def chunk(i, carry):
-        rows = pl.ds(pl.multiple_of(i * 64, 64), 64)
-        parts = [f * ref[rows].astype(jnp.float32) for f, ref in zip(factors, refs)]
-        out[rows] = sum(parts[1:], parts[0]).astype(jnp.bfloat16)
-        return carry
-
-    lax.fori_loop(0, latent_rows // 64, chunk, 0)
-    shape = (16, 256)
-    out[latent_rows:part_rows] = stat_rows(
-        jnp.broadcast_to(top, shape), jnp.broadcast_to(total, shape)
-    )
+    packed = jnp.where(lane == 0, top, jnp.where(lane == 1, high, total - high))
+    return packed.astype(jnp.bfloat16)
+
+
+def merge_stats(stats):
+    top = functools.reduce(jnp.maximum, [t for t, _ in stats])
+    return top, sum(jnp.exp2(t - top) * l for t, l in stats)
+
+
+def roll_rows(block, count):
+    count = count % 8
+    if count == 0:
+        return block
+    return jnp.concatenate([block[8 - count :], block[: 8 - count]], axis=0)
 
 
 def make_mask(span_ref, length_ref, rows_ref, line, place_in, mask_one, core, a, b):
@@ -105,12 +89,15 @@
 
 
 def gather_attend_kernel(
-    span_ref, length_ref, rows_ref, query_ref, cache_ref, out_ref,
-    own, sib, kept, from_sib, ring_in, last_in, keys,
+    span_ref, length_ref, rows_ref, query_ref, cache_ref, up_ref, out_ref, far_up,
+    own, sib, kept, to_sib, from_sib, own_stat, keys,
     line, place_in, mask_one, mask_mid, mask_two, mask_got, mask_own, mask_sib,
+    stats, stats_a, stats_mid, stats_b, factor, up, wide, partial, ring_in, last_out, last_in,
     one_send, one_recv, two_send, two_recv, three_send, three_recv,
     load_sem, key_sem, own_recv, sib_recv, a_send, b_send, sib_send,
-    part_send, part_recv, ring_send, ring_recv, last_send, last_recv,
+    part_send, part_recv, credit, far_send, far_recv, pass_send, pass_recv, up_sem,
+    stat_a_send, stat_a_recv, stat_b_send, stat_b_recv,
+    ring_send, ring_recv, last_send, last_recv,
 ):
     me = lax.axis_index("ctx")
     core = me % 2
@@ -123,11 +110,14 @@
     def device(da, db):
         return (((a + da + 4) % 4) * a_step + ((b + db + 4) % 4) * b_step) * 2 + core
 
+    group = lax.axis_index("req")
     sibling = chip * 2 + 1 - core
     barrier = pltpu.get_barrier_semaphore()
     partners = [device(d, 0) for d in (1, 2, 3)] + [device(0, d) for d in (1, 2, 3)] + [sibling]
+    partners = [{"ctx": partner} for partner in partners]
+    partners += [{"req": (group + 1) % 4}, {"req": (group + 3) % 4}]
     for partner in partners:
-        pl.semaphore_signal(barrier, inc=1, device_id={"ctx": partner}, device_id_type=MESH)
+        pl.semaphore_signal(barrier, inc=1, device_id=partner, device_id_type=MESH)
 
     def own_request(flow, slot):
         da, db = slot % 4, slot // 4
@@ -172,19 +162,41 @@
         return remote(own.at[flow, slot, body], sib.at[flow, slot, body],
                       sib_send.at[flow, slot], sib_recv.at[flow, slot], sibling)
 
-    partial = pl.ds(0, part_rows)
-
     def part_copy(flow, slot):
-        return remote(sib.at[flow, slot, partial], from_sib.at[flow, slot],
-                      part_send.at[flow, slot], part_recv.at[flow, slot], sibling)
-
-    def ring_copy(flow, slot):
-        return remote(kept.at[flow, slot], ring_in.at[flow, slot - 4],
-                      ring_send.at[flow, slot - 4], ring_recv.at[flow, slot - 4],
+        return remote(to_sib.at[flow, slot % 2], from_sib.at[flow, slot % 4],
+                      part_send.at[flow, slot % 2], part_recv.at[flow, slot % 4], sibling)
+
+    def far_copy(piece):
+        quarter = pl.ds(16 * core + 8 * (piece % 2), 8)
+        if piece < 4:
+            src, ahead_z = up_ref.at[quarter], (1 if piece < 2 else 3)
+        else:
+            src = far_up.at[0 if piece == 4 else 1, quarter]
+            ahead_z = 1 if piece == 4 else 3
+        return pltpu.make_async_remote_copy(
+            src_ref=src, dst_ref=far_up.at[piece // 2, quarter],
+            send_sem=far_send.at[piece], recv_sem=far_recv.at[piece],
+            device_id={"req": (group + ahead_z) % 4}, device_id_type=MESH)
+
+    def pass_copy(piece):
+        quarter = far_up.at[piece // 2, pl.ds(16 * core + 8 * (piece % 2), 8)]
+        return remote(quarter, quarter, pass_send.at[piece], pass_recv.at[piece], sibling)
+
+    def stat_a_copy(d):
+        return remote(stats, stats_a.at[d - 1], stat_a_send.at[d - 1], stat_a_recv.at[d - 1],
+                      device(d, 0))
+
+    def stat_b_copy(d):
+        return remote(stats_mid, stats_b.at[d - 1], stat_b_send.at[d - 1],
+                      stat_b_recv.at[d - 1], device(0, d))
+
+    def ring_copy(flow, gi, db):
+        return remote(partial.at[flow, gi, db], ring_in.at[flow, gi, db - 1],
+                      ring_send.at[flow, gi, db - 1], ring_recv.at[flow, gi, db - 1],
                       device(0, 1 - 2 * flow))
 
     def last_copy(flow, da):
-        return remote(kept.at[flow, da], last_in.at[flow, da - 1],
+        return remote(last_out.at[flow, da - 1], last_in.at[flow, da - 1],
                       last_send.at[flow, da - 1], last_recv.at[flow, da - 1],
                       device(-da if flow == 0 else da - 4, 0))
 
@@ -222,6 +234,8 @@
                    device(d, 0)) for d in (1, 2, 3)]
     for copy in ones:
         copy.start()
+    for piece in (0, 3, 1, 2):
+        far_copy(piece).start()
     for flow in range(2):
         b_copy(flow, 0).start()
         for da in (1, 2, 3):
@@ -255,23 +269,33 @@
     three.start()
     three.wait_recv()
 
+    row8 = lax.broadcasted_iota(jnp.int32, (8, 128), 0)
+
     def combine(slot):
+        db, da = slot // 4, slot % 4
         for flow in range(2):
             part_copy(flow, slot).wait_recv()
-
-        @pl.when(slot < 8)
-        def _():
-            for flow in range(2):
-                merge([kept.at[flow, slot], from_sib.at[flow, slot]], kept.at[flow, slot])
-                ring_copy(flow, slot).start()
-
-        @pl.when(slot >= 8)
-        def _():
-            for flow in range(2):
-                ring_copy(flow, slot - 4).wait_recv()
-                merge([kept.at[flow, slot], from_sib.at[flow, slot], ring_in.at[flow, slot - 8]],
-                      kept.at[flow, slot])
-                ring_copy(flow, slot).start()
+            for half in range(2):
+                rows = slice(128 * half, 128 * half + 128)
+                got = from_sib[flow, slot % 4, rows, 512:640].astype(jnp.float32)
+                top_1, total_1 = own_stat[slot % 2, flow, 0, rows], own_stat[slot % 2, flow, 1, rows]
+                top_2 = jnp.broadcast_to(got[:, 0:1], (128, 128))
+                total_2 = jnp.broadcast_to(got[:, 1:2] + got[:, 2:3], (128, 128))
+                top = jnp.maximum(top_1, top_2)
+                factor_1, factor_2 = jnp.exp2(top_1 - top), jnp.exp2(top_2 - top)
+                total = factor_1 * total_1 + factor_2 * total_2
+                for i in range(4):
+                    lanes = slice(128 * i, 128 * i + 128)
+                    value = factor_1 * kept[flow, slot, rows, lanes].astype(jnp.float32)
+                    value += factor_2 * from_sib[flow, slot % 4, rows, lanes].astype(jnp.float32)
+                    kept[flow, slot, rows, lanes] = value.astype(jnp.bfloat16)
+                for i, value in enumerate((top, total)):
+                    value = jnp.swapaxes(value, 0, 1)[0:8]
+                    stats[i, flow, db] = jnp.where(
+                        row8 == 2 * da + half, value, stats[i, flow, db])
+
+    def give_credit():
+        pl.semaphore_signal(credit, inc=1, device_id={"ctx": sibling}, device_id_type=MESH)
 
     def iteration(slot, carry):
         place = slot % 2
@@ -303,86 +327,231 @@
             keys[place, flow, 576:key_rows] = mask_own[db]
             keys[place, 2 + flow, 576:key_rows] = mask_sib[db]
 
-        for flow in range(2):
-            mixed, stats = attend_unit(keys[place, flow], own[flow, slot])
-            kept[flow, slot, 0:latent_rows] = mixed
-            kept[flow, slot, latent_rows:part_rows] = stats
+        results = [attend_unit(keys[place, flow], own[flow, slot]) for flow in range(2)]
+        for flow in range(2):
+            mixed, top, total = results[flow]
+            kept[flow, slot] = mixed
+            own_stat[place, flow, 0] = jnp.broadcast_to(top, (256, 128))
+            own_stat[place, flow, 1] = jnp.broadcast_to(total, (256, 128))
 
         for flow in range(2):
             sib_copy(flow, slot).wait_recv()
+
+        @pl.when(slot >= 2)
+        def _():
+            for flow in range(2):
+                part_copy(flow, slot).wait_send()
+
         results = [attend_unit(keys[place, 2 + flow], sib[flow, slot]) for flow in range(2)]
         for flow in range(2):
-            mixed, stats = results[flow]
-            sib[flow, slot, 0:latent_rows] = mixed
-            sib[flow, slot, latent_rows:part_rows] = stats
+            mixed, top, total = results[flow]
+            to_sib[flow, place, :, 0:512] = mixed
+            to_sib[flow, place, :, 512:640] = pack_stats(top, total)
+
+        @pl.when(slot >= 4)
+        def _():
+            pl.semaphore_wait(credit, 1)
+
+        for flow in range(2):
             part_copy(flow, slot).start()
 
-        @pl.when(slot > 4)
+        @pl.when(slot > 0)
         def _():
             combine(slot - 1)
 
+        @pl.when((slot > 0) & (slot < 13))
+        def _():
+            give_credit()
+
+        @pl.when(slot == 8)
+        def _():
+            for piece in (0, 3):
+                far_copy(piece).wait_recv()
+                pass_copy(piece).start()
+            far_copy(4).start()
+            far_copy(5).start()
+
+        @pl.when(slot == 12)
+        def _():
+            for piece in (1, 2):
+                far_copy(piece).wait_recv()
+                pass_copy(piece).start()
+
         return carry
 
+    stats[...] = jnp.zeros_like(stats)
     lax.fori_loop(0, slots, iteration, 0)
+
+    def up_copy(gi):
+        src = up_ref if gi == 0 else far_up.at[gi - 1]
+        return pltpu.make_async_copy(src, up.at[gi % 2], up_sem.at[gi % 2])
+
+    up_copy(0).start()
     combine(slots - 1)
-
-    for da in (1, 2, 3, 0):
-        for flow in range(2):
-            part_copy(flow, da).wait_recv()
-            ring_copy(flow, 12 + da).wait_recv()
-            merge([kept.at[flow, da], from_sib.at[flow, da], ring_in.at[flow, 8 + da]],
-                  kept.at[flow, da])
-            if da:
-                last_copy(flow, da).start()
+    for d in (1, 2, 3):
+        stat_a_copy(d).start()
+    for piece in (0, 1):
+        pass_copy(piece).wait_recv()
+    up_copy(1).start()
+    for d in (1, 2, 3):
+        stat_a_copy(d).wait_recv()
+    for flow in range(2):
+        for db in range(4):
+            parts = [(stats[0, flow, db], stats[1, flow, db])]
+            for d in (1, 2, 3):
+                turn = 2 * d if flow == 0 else -2 * d
+                parts.append(tuple(roll_rows(stats_a[d - 1, i, flow, db], turn) for i in range(2)))
+            stats_mid[0, flow, db], stats_mid[1, flow, db] = merge_stats(parts)
+    for d in (1, 2, 3):
+        stat_b_copy(d).start()
+    for piece in (4, 5):
+        far_copy(piece).wait_recv()
+        pass_copy(piece).start()
+    for d in (1, 2, 3):
+        stat_b_copy(d).wait_recv()
+    for flow in range(2):
+        for db in range(4):
+            parts = [(stats_mid[0, flow, db], stats_mid[1, flow, db])]
+            for d in (1, 2, 3):
+                other = (db - d) % 4 if flow == 0 else (db + d) % 4
+                parts.append((stats_b[d - 1, 0, flow, other], stats_b[d - 1, 1, flow, other]))
+            top, total = merge_stats(parts)
+            value = jnp.exp2(stats[0, flow, db] - top) / total
+            turned = value
+            for z in (1, 2, 3):
+                shifted = jnp.concatenate([value[:, 32 * z :], value[:, : 32 * z]], axis=1)
+                turned = jnp.where(group == z, shifted, turned)
+            factor[32 * flow + 8 * db : 32 * flow + 8 * db + 8] = turned
+
+    def chain(gi, db):
+        for flow in range(2):
+            ring_copy(flow, gi, db - 1).wait_recv()
+            value = partial[flow, gi, db].astype(jnp.float32)
+            value += ring_in[flow, gi, db - 2].astype(jnp.float32)
+            partial[flow, gi, db] = value.astype(jnp.bfloat16)
+            ring_copy(flow, gi, db).start()
+
+    ahead_of = (0, 3, 1, 2)
+    for gi in range(4):
+        up_copy(gi).wait()
+        first_head = pl.multiple_of(32 * ((group + ahead_of[gi]) % 4), 32)
+        for flow in range(2):
+
+            def fill_wide(slot, carry):
+                for half in range(2):
+                    rows = pl.ds(pl.multiple_of(128 * half + first_head, 32), 32)
+                    value = kept[flow, slot, rows].astype(jnp.float32)
+                    at = pl.ds(pl.multiple_of(32 * (32 * flow + 2 * slot + half), 32), 32)
+                    for i in range(4):
+                        wide[i, at] = value[:, 128 * i : 128 * i + 128]
+                return carry
+
+            lax.fori_loop(0, slots, fill_wide, 0)
+        weight = factor[...]
+        for hj in range(16):
+            values = []
+            for head in (hj, 16 + hj):
+                rows = [wide[i, pl.ds(head, 64, stride=32), :] for i in range(4)]
+                rows = jnp.concatenate(rows, axis=1).astype(jnp.bfloat16)
+                value = jnp.dot(rows, up[gi % 2, head], preferred_element_type=jnp.float32)
+                lane = 32 * ahead_of[gi] + head
+                values.append(value * weight[:, lane : lane + 1])
+            for flow in range(2):
+                for db in range(4):
+                    at = 32 * flow + 8 * db
+                    both = jnp.concatenate([value[at : at + 8] for value in values], axis=0)
+                    partial[flow, gi, db, :, 128 * hj : 128 * hj + 128] = both.astype(jnp.bfloat16)
+        for flow in range(2):
+            ring_copy(flow, gi, 1).start()
+        if gi == 0:
+            for piece in (2, 3):
+                pass_copy(piece).wait_recv()
+            up_copy(2).start()
+        if gi == 1:
+            for piece in (4, 5):
+                pass_copy(piece).wait_recv()
+            up_copy(3).start()
+        if gi >= 1:
+            chain(gi - 1, 2)
+        if gi >= 2:
+            chain(gi - 2, 3)
+    chain(3, 2)
+    chain(2, 3)
+    chain(3, 3)
+
+    whole = []
+    for flow in range(2):
+        ends = []
+        for gi in range(4):
+            ring_copy(flow, gi, 3).wait_recv()
+            value = partial[flow, gi, 0].astype(jnp.float32)
+            ends.append(value + ring_in[flow, gi, 2].astype(jnp.float32))
+
+        def rows_of(da):
+            picked = [end[8 * c + 2 * da : 8 * c + 2 * da + 2] for end in ends for c in range(2)]
+            return jnp.concatenate(picked, axis=0)
+
+        for da in (1, 2, 3):
+            last_out[flow, da - 1] = rows_of(da).astype(jnp.bfloat16)
+            last_copy(flow, da).start()
+        whole.append(rows_of(0))
     for flow in range(2):
         for da in (1, 2, 3):
             last_copy(flow, da).wait_recv()
-        refs = [kept.at[flow, 0]] + [last_in.at[flow, i] for i in range(3)]
-        top, factors, total = merge_weights(refs)
-        scale = 1.0 / total
-        for i in range(latent_rows // 128):
-            rows = pl.ds(128 * i, 128)
-            parts = [f * scale * ref[rows].astype(jnp.float32) for f, ref in zip(factors, refs)]
-            final = sum(parts[1:], parts[0]).astype(jnp.bfloat16)
-            out_ref[flow, :, 128 * i : 128 * (i + 1)] = jnp.swapaxes(final, 0, 1)
+            whole[flow] = whole[flow] + last_in[flow, da - 1].astype(jnp.float32)
+    for gi in range(4):
+        picked = [whole[flow][4 * gi + 2 * c : 4 * gi + 2 * c + 2]
+                  for c in range(2) for flow in range(2)]
+        out_ref[gi] = jnp.concatenate(picked, axis=0)
 
     for flow in range(2):
         def drain(slot, carry):
             sib_copy(flow, slot).wait_send()
-            part_copy(flow, slot).wait_send()
 
             @pl.when(slot < 12)
             def _():
                 b_copy(flow, slot).wait_send()
-                ring_copy(flow, slot + 4).wait_send()
 
             return carry
 
         lax.fori_loop(0, slots, drain, 0)
+        for slot in (14, 15):
+            part_copy(flow, slot).wait_send()
         for da in (1, 2, 3):
             a_copy(flow, da).wait_send()
             last_copy(flow, da).wait_send()
+            for gi in range(4):
+                ring_copy(flow, gi, da).wait_send()
+    for piece in range(6):
+        far_copy(piece).wait_send()
+        pass_copy(piece).wait_send()
+    for d in (1, 2, 3):
+        stat_a_copy(d).wait_send()
+        stat_b_copy(d).wait_send()
     for copy in ones + twos + [three]:
         copy.wait_send()
 
 
-def gather_attend(span_map, lengths, top_rows, query_t, cache_t):
+def gather_attend(span_map, lengths, top_rows, query_t, cache_t, up_weight):
     dma = pltpu.SemaphoreType.DMA
-    bf16 = jnp.bfloat16
+    bf16, f32 = jnp.bfloat16, jnp.float32
     return pl.pallas_call(
         gather_attend_kernel,
         in_specs=[pl.BlockSpec(memory_space=pltpu.SMEM)] * 2
         + [pl.BlockSpec(memory_space=pltpu.VMEM)]
-        + [pl.BlockSpec(memory_space=pl.ANY)] * 2,
-        out_specs=pl.BlockSpec(memory_space=pltpu.VMEM),
-        out_shape=jax.ShapeDtypeStruct((2, 256, latent_rows), bf16),
+        + [pl.BlockSpec(memory_space=pl.ANY)] * 3,
+        out_specs=[pl.BlockSpec(memory_space=pltpu.VMEM), pl.BlockSpec(memory_space=pl.ANY)],
+        out_shape=[
+            jax.ShapeDtypeStruct((4, 8, 2048), f32),
+            jax.ShapeDtypeStruct((3,) + up_weight.shape, bf16),
+        ],
         scratch_shapes=[
             pltpu.VMEM((2, slots, key_rows, 256), bf16),
             pltpu.VMEM((2, slots, key_rows, 256), bf16),
-            pltpu.VMEM((2, slots, part_rows, 256), bf16),
-            pltpu.VMEM((2, slots, part_rows, 256), bf16),
-            pltpu.VMEM((2, 12, part_rows, 256), bf16),
-            pltpu.VMEM((2, 3, part_rows, 256), bf16),
+            pltpu.VMEM((2, slots, 256, 512), bf16),
+            pltpu.VMEM((2, 2, 256, 640), bf16),
+            pltpu.VMEM((2, 4, 256, 640), bf16),
+            pltpu.VMEM((2, 2, 2, 256, 128), f32),
             pltpu.VMEM((2, 4, key_rows, 512), bf16),
             pltpu.VMEM((4, 2048), jnp.int32),
             pltpu.VMEM((4, 2048), jnp.int32),
@@ -392,6 +561,17 @@
             pltpu.VMEM((4, 2, 16, 512), bf16),
             pltpu.VMEM((8, 16, 512), bf16),
             pltpu.VMEM((4, 16, 512), bf16),
+            pltpu.VMEM((2, 2, 4, 8, 128), f32),
+            pltpu.VMEM((3, 2, 2, 4, 8, 128), f32),
+            pltpu.VMEM((2, 2, 4, 8, 128), f32),
+            pltpu.VMEM((3, 2, 2, 4, 8, 128), f32),
+            pltpu.VMEM((64, 128), f32),
+            pltpu.VMEM((2, 32, 512, 128), bf16),
+            pltpu.VMEM((4, 2048, 128), f32),
+            pltpu.VMEM((2, 4, 4, 16, 2048), bf16),
+            pltpu.VMEM((2, 4, 3, 16, 2048), bf16),
+            pltpu.VMEM((2, 3, 16, 2048), bf16),
+            pltpu.VMEM((2, 3, 16, 2048), bf16),
             dma((3,)),
             dma((3,)),
             dma((3,)),
@@ -405,25 +585,35 @@
             dma((2, 3)),
             dma((2, 12)),
             dma((2, slots)),
-            dma((2, slots)),
-            dma((2, slots)),
-            dma((2, 12)),
-            dma((2, 12)),
+            dma((2, 2)),
+            dma((2, 4)),
+            pltpu.SemaphoreType.REGULAR,
+            dma((6,)),
+            dma((6,)),
+            dma((6,)),
+            dma((6,)),
+            dma((2,)),
+            dma((3,)),
+            dma((3,)),
+            dma((3,)),
+            dma((3,)),
+            dma((2, 4, 3)),
+            dma((2, 4, 3)),
             dma((2, 3)),
             dma((2, 3)),
         ],
         compiler_params=pltpu.CompilerParams(
-            collective_id=0, has_side_effects=True, vmem_limit_bytes=58 * 2**20
+            collective_id=0, has_side_effects=True, vmem_limit_bytes=60 * 2**20
         ),
         cost_estimate=pl.CostEstimate(
-            flops=18_000_000_000, bytes_accessed=40_000_000, transcendentals=8_000_000
+            flops=19_000_000_000, bytes_accessed=60_000_000, transcendentals=8_000_000
         ),
-    )(span_map, lengths, top_rows, query_t, cache_t)
+    )(span_map, lengths, top_rows, query_t, cache_t, up_weight)[0]
 
 
 def project_kernel(
-    mixed_ref, up_ref, out_weight_ref, out_ref,
-    taken, wide, up, weight, values, sums, give, get,
+    head_ref, out_weight_ref, out_ref,
+    taken, weight, values, sums, give, get,
     load_sem, take_send, take_recv, own_recv, sib_recv, a_send, b_send, sib_send,
     give_send, give_recv,
 ):
@@ -454,19 +644,15 @@
             src_ref=src, dst_ref=dst, send_sem=send, recv_sem=recv,
             device_id=target, device_id_type=MESH)
 
-    def heads_of(z):
-        return mixed_ref.at[:, pl.ds(pl.multiple_of(z * 32, 32), 32)]
-
     loads = [
-        pltpu.make_async_copy(heads_of(group), taken.at[0], load_sem.at[0]),
-        pltpu.make_async_copy(up_ref, up, load_sem.at[1]),
-        pltpu.make_async_copy(out_weight_ref, weight.at[pl.ds(0, 224)], load_sem.at[2]),
+        pltpu.make_async_copy(head_ref.at[0], taken.at[0], load_sem.at[0]),
+        pltpu.make_async_copy(out_weight_ref, weight.at[pl.ds(0, 224)], load_sem.at[1]),
     ]
     for copy in loads:
         copy.start()
     pl.semaphore_wait(barrier, len(partners))
     takes = [
-        remote(heads_of((group + d) % 4), taken.at[d], take_send.at[d - 1],
+        remote(head_ref.at[(0, 2, 3, 1)[d]], taken.at[d], take_send.at[d - 1],
                take_recv.at[d - 1], plane(d))
         for d in (1, 2, 3)
     ]
@@ -476,14 +662,8 @@
     weight[224:256] = jnp.zeros((32, 4096), jnp.bfloat16)
     sums[...] = jnp.zeros_like(sums)
     loads[0].wait()
-    loads[1].wait()
-    for d in range(4):
-        if d:
-            takes[d - 1].wait_recv()
-        for s in range(4):
-            rows = taken[d, s].astype(jnp.float32)
-            for i in range(4):
-                wide[i, 128 * d + 32 * s : 128 * d + 32 * s + 32] = rows[:, 128 * i : 128 * i + 128]
+    for copy in takes:
+        copy.wait_recv()
 
     def a_copy(flow, da):
         return remote(values.at[flow, 0, 0], values.at[flow, da, 0],
@@ -508,15 +688,11 @@
         sib_copy(flow, slot).start()
 
     for flow in range(2):
-        for i in range(16):
-            head = 16 * flow + i
-            rows = [wide[j, pl.ds(head, 16, stride=32), :] for j in range(4)]
-            rows = jnp.concatenate(rows, axis=1).astype(jnp.bfloat16)
-            value = jnp.dot(rows, up[head], preferred_element_type=jnp.float32)
-            values[flow, 0, 0, :, 128 * i : 128 * i + 128] = value.astype(jnp.bfloat16)
+        rows = [taken[d, 4 * flow : 4 * flow + 4] for d in range(4)]
+        values[flow, 0, 0] = jnp.concatenate(rows, axis=0).astype(jnp.bfloat16)
         forward(flow, 0)
 
-    loads[2].wait()
+    loads[1].wait()
     for slot in range(slots):
         for flow in range(2):
             if slot:
@@ -575,24 +751,22 @@
                 b_copy(flow, slot).wait_send()
 
 
-def project(mixed, up_weight, out_weight_t):
+def project(head_values, out_weight_t):
     dma = pltpu.SemaphoreType.DMA
     bf16, f32 = jnp.bfloat16, jnp.float32
     return pl.pallas_call(
         project_kernel,
-        in_specs=[pl.BlockSpec(memory_space=pl.ANY)] * 3,
+        in_specs=[pl.BlockSpec(memory_space=pl.ANY)] * 2,
         out_specs=pl.BlockSpec(memory_space=pltpu.VMEM),
         out_shape=jax.ShapeDtypeStruct((4, 32, 224), bf16),
         scratch_shapes=[
-            pltpu.VMEM((4, 4, 32, 512), bf16),
-            pltpu.VMEM((4, 512, 128), f32),
-            pltpu.VMEM((32, 512, 128), bf16),
+            pltpu.VMEM((4, 8, 2048), f32),
             pltpu.VMEM((256, 4096), bf16),
             pltpu.VMEM((2, slots, 2, 16, 2048), bf16),
             pltpu.VMEM((2, 512, 128), f32),
             pltpu.VMEM((3, 4, 32, 256), bf16),
             pltpu.VMEM((3, 4, 32, 256), bf16),
-            dma((3,)),
+            dma((2,)),
             dma((3,)),
             dma((3,)),
             dma((2, slots)),
@@ -609,15 +783,14 @@
         cost_estimate=pl.CostEstimate(
             flops=1_100_000_000, bytes_accessed=8_000_000, transcendentals=0
         ),
-    )(mixed, up_weight, out_weight_t)
+    )(head_values, out_weight_t)
 
 
 def per_device(queries, top_rows, lengths, span_map, latent_cache, up_weight, out_weight):
-    steps, heads = queries.shape[1:3]
     query_t = jnp.swapaxes(queries, 2, 3)[0]
     cache_t = jnp.swapaxes(latent_cache, 1, 2)
-    mixed = gather_attend(span_map, lengths, top_rows[0], query_t, cache_t)
-    out = project(mixed.reshape(steps, heads, -1), up_weight, out_weight.T)
+    head_values = gather_attend(span_map, lengths, top_rows[0], query_t, cache_t, up_weight)
+    out = project(head_values, out_weight.T)
     return jnp.swapaxes(out, 0, 1)
 
 

time: 168 us -> 176 us (1.048)
  Pallas kernels: 164 us -> 173 us
    pallas_call x1, Pallas kernels: 124 us -> 136 us  [gather_attend(): pl.pallas_call(gather_attend_kernel, in_specs=[pl.BlockSpec(memory_space=...]
    pallas_call x1, Pallas kernels: 40 us -> 36.9 us  [project(): pl.pallas_call(project_kernel, in_specs=[pl.BlockSpec(memory_space=pl.ANY...]
where the time goes in v5:
time: 176 us
  Pallas kernels  173 us (98%)
    pallas_call x1, Pallas kernels, gather_attend(): pl.pallas_call(gather_attend_kernel, in_specs=[pl.BlockSpec(memory_space=...  136 us
    pallas_call x1, Pallas kernels, project(): pl.pallas_call(project_kernel, in_specs=[pl.BlockSpec(memory_space=pl.ANY...  36.9 us

profile of v5, /device:TPU:0, one launch (start us, length us, event | category | flops | bytes accessed | tf_op | source)
XLA Modules:
  0.0 175.6 jit_solution(14796454184371096861)
XLA Ops:
  0.7 0.0 copy-start
  0.7 136.4 %shard_map.73 = (f32[4,8,2048]{2,1,0:T(8,128)}, bf16[3,32,512,128]{3,2,1,0:T(8,128)(2,1)}) custom-call(s32[64]{0:T(128)} %span_ref.1, s32[1]{0:T(128)S(6)} %copy.9.length_ref, s32[4,2048]{1,0:T(4,128)} %bitcast.11, bf16[4,576,128]{2,1,0:T(8,128)(2,1)} %bitcast.10, bf16[32,576,512]{2,1,0:T(8,128)(2,1)} %bitcast.9, bf16[32,512,128]{2,1,0:T(8,128)(2,1)} %up_ref.1), custom_call_target="tpu_custom_call" | custom-call | flops 19000000512 | bytes 60000000 | tf_op jit(solution)/shard_map/pallas_call | solution.py:538
  137.1 0.0 copy-done
  137.1 0.0 copy-start.1
  137.1 0.9 copy-done.1
  138.1 36.9 %shard_map.74 = bf16[4,32,224]{2,1,0:T(8,128)(2,1)S(1)} custom-call(f32[4,8,2048]{2,1,0:T(8,128)S(1)} %copy-done.1, bf16[224,4096]{1,0:T(8,128)(2,1)S(1)} %bitcast.8), custom_call_target="tpu_custom_call" | custom-call | flops 1100000000 | bytes 8000000 | tf_op jit(solution)/shard_map/pallas_call | solution.py:757
  175.0 0.7 copy.8
Async XLA Ops:
  0.7 136.5 %copy-start = (bf16[4096,224]{0,1:T(8,128)(2,1)S(1)}, bf16[4096,224]{0,1:T(8,128)(2,1)}, u32[]{:S(2)}) copy-start(bf16[4096,224]{0,1:T(8,128)(2,1)} %param.13) | copy-start | bytes 5505028
  137.1 1.0 copy-start.1

commit v6 on v5

--- a/solution.py
+++ b/solution.py
@@ -18,7 +18,6 @@
 slots = side * side
 key_rows = 592
 latent_rows = 512
-ahead = 2
 
 
 def attend_unit(keys, query):
@@ -45,6 +44,10 @@
     return packed.astype(jnp.bfloat16)
 
 
+def spread(i):
+    return i + (i // 2) * (5 - 2 * i)
+
+
 def merge_stats(stats):
     top = functools.reduce(jnp.maximum, [t for t, _ in stats])
     return top, sum(jnp.exp2(t - top) * l for t, l in stats)
@@ -92,7 +95,7 @@
     span_ref, length_ref, rows_ref, query_ref, cache_ref, up_ref, out_ref, far_up,
     own, sib, kept, to_sib, from_sib, own_stat, keys,
     line, place_in, mask_one, mask_mid, mask_two, mask_got, mask_own, mask_sib,
-    stats, stats_a, stats_mid, stats_b, factor, up, wide, partial, ring_in, last_out, last_in,
+    stats, stats_a, stats_mid, stats_b, factor, up, wide, raw, partial, ring_in, last_out, last_in,
     one_send, one_recv, two_send, two_recv, three_send, three_recv,
     load_sem, key_sem, own_recv, sib_recv, a_send, b_send, sib_send,
     part_send, part_recv, credit, far_send, far_recv, pass_send, pass_recv, up_sem,
@@ -120,13 +123,13 @@
         pl.semaphore_signal(barrier, inc=1, device_id=partner, device_id_type=MESH)
 
     def own_request(flow, slot):
-        da, db = slot % 4, slot // 4
+        da, db = spread(slot % 4), spread(slot // 4)
         if flow == 0:
             da, db = 4 - da, 4 - db
         return (((a + da) % 4) * a_step + ((b + db) % 4) * b_step) * 2 + core
 
     def sib_request(flow, slot):
-        da, db = slot % 4, slot // 4
+        da, db = spread(slot % 4), spread(slot // 4)
         if flow == 0:
             da, db = 4 - da, 4 - db
         return (((b + da) % 4) * b_step + ((a + db) % 4) * a_step) * 2 + 1 - core
@@ -148,15 +151,19 @@
 
     body = pl.ds(0, 576)
 
-    def a_copy(flow, da):
-        return remote(own.at[flow, 0, body], own.at[flow, da, body],
-                      a_send.at[flow, da - 1], own_recv.at[flow, da],
-                      device(da if flow == 0 else 4 - da, 0))
-
-    def b_copy(flow, slot):
-        return remote(own.at[flow, slot, body], own.at[flow, slot + 4, body],
-                      b_send.at[flow, slot], own_recv.at[flow, slot + 4],
-                      device(0, 1 - 2 * flow))
+    def a_copy(flow, slot):
+        side_step = 1 if (flow == 0) != (slot == 2) else 3
+        return remote(own.at[flow, 1 if slot == 3 else 0, body], own.at[flow, slot, body],
+                      a_send.at[flow, slot - 1], own_recv.at[flow, slot], device(side_step, 0))
+
+    def b_copy(flow, slot, row):
+        side_step = 1 if (flow == 0) != (row == 2) else 3
+        return remote(own.at[flow, slot - (4 if row == 1 else 8), body], own.at[flow, slot, body],
+                      b_send.at[flow, slot - 4], own_recv.at[flow, slot], device(0, side_step))
+
+    def arrive(flow, slot):
+        place = own.at[flow, slot, body]
+        remote(place, place, sib_send.at[flow, slot], own_recv.at[flow, slot], sibling).wait_recv()
 
     def sib_copy(flow, slot):
         return remote(own.at[flow, slot, body], sib.at[flow, slot, body],
@@ -191,9 +198,10 @@
                       stat_b_recv.at[d - 1], device(0, d))
 
     def ring_copy(flow, gi, db):
+        side_step = 1 if (flow == 0) != (db == 1) else 3
         return remote(partial.at[flow, gi, db], ring_in.at[flow, gi, db - 1],
                       ring_send.at[flow, gi, db - 1], ring_recv.at[flow, gi, db - 1],
-                      device(0, 1 - 2 * flow))
+                      device(0, side_step))
 
     def last_copy(flow, da):
         return remote(last_out.at[flow, da - 1], last_in.at[flow, da - 1],
@@ -219,7 +227,8 @@
     for flow in range(2):
 
         def fill(slot, carry):
-            da = slot % 4 if flow == 0 else (4 - slot % 4) % 4
+            da = spread(slot % 4)
+            da = da if flow == 0 else (4 - da) % 4
             hot = jnp.where(row == step + 2 * flow + 4 * da, 1.0, 0.0).astype(jnp.bfloat16)
             own[flow, slot, 576:key_rows] = hot
             sib[flow, slot, 576:key_rows] = hot
@@ -237,9 +246,10 @@
     for piece in (0, 3, 1, 2):
         far_copy(piece).start()
     for flow in range(2):
-        b_copy(flow, 0).start()
-        for da in (1, 2, 3):
-            a_copy(flow, da).start()
+        for slot in (1, 2):
+            a_copy(flow, slot).start()
+        b_copy(flow, 4, 1).start()
+        b_copy(flow, 8, 2).start()
         sib_copy(flow, 0).start()
     for copy in ones:
         copy.wait_recv()
@@ -253,11 +263,6 @@
                    device(0, d)) for d in (1, 2, 3)]
     for copy in twos:
         copy.start()
-    for slot in (1, 2, 3):
-        for flow in range(2):
-            a_copy(flow, slot).wait_recv()
-            b_copy(flow, slot).start()
-            sib_copy(flow, slot).start()
     for copy in twos:
         copy.wait_recv()
     mask_own[0] = mask_two[0, 0]
@@ -272,7 +277,7 @@
     row8 = lax.broadcasted_iota(jnp.int32, (8, 128), 0)
 
     def combine(slot):
-        db, da = slot // 4, slot % 4
+        db, da = spread(slot // 4), spread(slot % 4)
         for flow in range(2):
             part_copy(flow, slot).wait_recv()
             for half in range(2):
@@ -300,20 +305,39 @@
     def iteration(slot, carry):
         place = slot % 2
 
-        @pl.when((slot >= 4 - ahead) & (slot < slots - ahead))
-        def _():
+        def first_row(at):
             for flow in range(2):
-                b_copy(flow, slot + ahead - 4).wait_recv()
-
-        @pl.when((slot >= 4 - ahead) & (slot < 12 - ahead))
+                arrive(flow, at)
+                if at == 1:
+                    a_copy(flow, 3).start()
+                b_copy(flow, 4 + at, 1).start()
+                b_copy(flow, 8 + at, 2).start()
+                sib_copy(flow, at).start()
+
+        @pl.when(slot == 1)
+        def _():
+            first_row(1)
+            first_row(2)
+
+        @pl.when(slot == 2)
+        def _():
+            first_row(3)
+
+        @pl.when((slot >= 2) & (slot < 6))
         def _():
             for flow in range(2):
-                b_copy(flow, slot + ahead).start()
-
-        @pl.when((slot >= 4 - ahead) & (slot < slots - ahead))
+                arrive(flow, slot + 2)
+                b_copy(flow, slot + 10, 3).start()
+
+        @pl.when((slot >= 6) & (slot < 14))
         def _():
             for flow in range(2):
-                sib_copy(flow, slot + ahead).start()
+                arrive(flow, slot + 2)
+
+        @pl.when((slot >= 2) & (slot < 14))
+        def _():
+            for flow in range(2):
+                sib_copy(flow, slot + 2).start()
 
         @pl.when(slot < slots - 1)
         def _():
@@ -323,7 +347,8 @@
         for copy in key_copies(slot, place):
             copy.wait()
         for flow in range(2):
-            db = slot // 4 if flow == 0 else (4 - slot // 4) % 4
+            db = spread(slot // 4)
+            db = db if flow == 0 else (4 - db) % 4
             keys[place, flow, 576:key_rows] = mask_own[db]
             keys[place, 2 + flow, 576:key_rows] = mask_sib[db]
 
@@ -386,6 +411,39 @@
         src = up_ref if gi == 0 else far_up.at[gi - 1]
         return pltpu.make_async_copy(src, up.at[gi % 2], up_sem.at[gi % 2])
 
+    def fill_group(gi):
+        first_head = pl.multiple_of(32 * ((group + ahead_of[gi]) % 4), 32)
+        for flow in range(2):
+
+            def fill_wide(slot, carry):
+                place = 4 * spread(slot // 4) + spread(slot % 4)
+                for half in range(2):
+                    rows = pl.ds(pl.multiple_of(128 * half + first_head, 32), 32)
+                    value = kept[flow, slot, rows].astype(jnp.float32)
+                    at = pl.ds(pl.multiple_of(32 * (32 * flow + 2 * place + half), 32), 32)
+                    for i in range(4):
+                        wide[i, at] = value[:, 128 * i : 128 * i + 128]
+                return carry
+
+            lax.fori_loop(0, slots, fill_wide, 0)
+
+    def product(gi, head):
+        rows = [wide[i, pl.ds(head, 64, stride=32), :] for i in range(4)]
+        rows = jnp.concatenate(rows, axis=1).astype(jnp.bfloat16)
+        return jnp.dot(rows, up[gi % 2, head], preferred_element_type=jnp.float32)
+
+    def scaled(gi, head, value, weight):
+        lane = 32 * ahead_of[gi] + head
+        return value * weight[:, lane : lane + 1]
+
+    def store_pair(gi, hj, values):
+        for flow in range(2):
+            for db in range(4):
+                at = 32 * flow + 8 * db
+                both = jnp.concatenate([value[at : at + 8] for value in values], axis=0)
+                partial[flow, gi, db, :, 128 * hj : 128 * hj + 128] = both.astype(jnp.bfloat16)
+
+    ahead_of = (0, 3, 1, 2)
     up_copy(0).start()
     combine(slots - 1)
     for d in (1, 2, 3):
@@ -393,6 +451,8 @@
     for piece in (0, 1):
         pass_copy(piece).wait_recv()
     up_copy(1).start()
+    fill_group(0)
+    up_copy(0).wait()
     for d in (1, 2, 3):
         stat_a_copy(d).wait_recv()
     for flow in range(2):
@@ -404,6 +464,8 @@
             stats_mid[0, flow, db], stats_mid[1, flow, db] = merge_stats(parts)
     for d in (1, 2, 3):
         stat_b_copy(d).start()
+    for head in range(32):
+        raw[head] = product(0, head)
     for piece in (4, 5):
         far_copy(piece).wait_recv()
         pass_copy(piece).start()
@@ -423,46 +485,26 @@
                 turned = jnp.where(group == z, shifted, turned)
             factor[32 * flow + 8 * db : 32 * flow + 8 * db + 8] = turned
 
-    def chain(gi, db):
-        for flow in range(2):
-            ring_copy(flow, gi, db - 1).wait_recv()
-            value = partial[flow, gi, db].astype(jnp.float32)
-            value += ring_in[flow, gi, db - 2].astype(jnp.float32)
-            partial[flow, gi, db] = value.astype(jnp.bfloat16)
-            ring_copy(flow, gi, db).start()
-
-    ahead_of = (0, 3, 1, 2)
+    def chain(gi):
+        for flow in range(2):
+            ring_copy(flow, gi, 2).wait_recv()
+            value = partial[flow, gi, 3].astype(jnp.float32)
+            value += ring_in[flow, gi, 1].astype(jnp.float32)
+            partial[flow, gi, 3] = value.astype(jnp.bfloat16)
+            ring_copy(flow, gi, 3).start()
+
     for gi in range(4):
-        up_copy(gi).wait()
-        first_head = pl.multiple_of(32 * ((group + ahead_of[gi]) % 4), 32)
-        for flow in range(2):
-
-            def fill_wide(slot, carry):
-                for half in range(2):
-                    rows = pl.ds(pl.multiple_of(128 * half + first_head, 32), 32)
-                    value = kept[flow, slot, rows].astype(jnp.float32)
-                    at = pl.ds(pl.multiple_of(32 * (32 * flow + 2 * slot + half), 32), 32)
-                    for i in range(4):
-                        wide[i, at] = value[:, 128 * i : 128 * i + 128]
-                return carry
-
-            lax.fori_loop(0, slots, fill_wide, 0)
+        if gi:
+            up_copy(gi).wait()
+            fill_group(gi)
         weight = factor[...]
         for hj in range(16):
-            values = []
-            for head in (hj, 16 + hj):
-                rows = [wide[i, pl.ds(head, 64, stride=32), :] for i in range(4)]
-                rows = jnp.concatenate(rows, axis=1).astype(jnp.bfloat16)
-                value = jnp.dot(rows, up[gi % 2, head], preferred_element_type=jnp.float32)
-                lane = 32 * ahead_of[gi] + head
-                values.append(value * weight[:, lane : lane + 1])
+            values = [raw[head] if gi == 0 else product(gi, head) for head in (hj, 16 + hj)]
+            values = [scaled(gi, 16 * c + hj, value, weight) for c, value in enumerate(values)]
+            store_pair(gi, hj, values)
+        for db in (2, 1):
             for flow in range(2):
-                for db in range(4):
-                    at = 32 * flow + 8 * db
-                    both = jnp.concatenate([value[at : at + 8] for value in values], axis=0)
-                    partial[flow, gi, db, :, 128 * hj : 128 * hj + 128] = both.astype(jnp.bfloat16)
-        for flow in range(2):
-            ring_copy(flow, gi, 1).start()
+                ring_copy(flow, gi, db).start()
         if gi == 0:
             for piece in (2, 3):
                 pass_copy(piece).wait_recv()
@@ -472,19 +514,17 @@
                 pass_copy(piece).wait_recv()
             up_copy(3).start()
         if gi >= 1:
-            chain(gi - 1, 2)
-        if gi >= 2:
-            chain(gi - 2, 3)
-    chain(3, 2)
-    chain(2, 3)
-    chain(3, 3)
+            chain(gi - 1)
+    chain(3)
 
     whole = []
     for flow in range(2):
         ends = []
         for gi in range(4):
+            ring_copy(flow, gi, 1).wait_recv()
             ring_copy(flow, gi, 3).wait_recv()
             value = partial[flow, gi, 0].astype(jnp.float32)
+            value += ring_in[flow, gi, 0].astype(jnp.float32)
             ends.append(value + ring_in[flow, gi, 2].astype(jnp.float32))
 
         def rows_of(da):
@@ -507,16 +547,13 @@
     for flow in range(2):
         def drain(slot, carry):
             sib_copy(flow, slot).wait_send()
-
-            @pl.when(slot < 12)
-            def _():
-                b_copy(flow, slot).wait_send()
-
             return carry
 
         lax.fori_loop(0, slots, drain, 0)
         for slot in (14, 15):
             part_copy(flow, slot).wait_send()
+        for slot in range(4, 16):
+            b_copy(flow, slot, slot // 4).wait_send()
         for da in (1, 2, 3):
             a_copy(flow, da).wait_send()
             last_copy(flow, da).wait_send()
@@ -568,6 +605,7 @@
             pltpu.VMEM((64, 128), f32),
             pltpu.VMEM((2, 32, 512, 128), bf16),
             pltpu.VMEM((4, 2048, 128), f32),
+            pltpu.VMEM((32, 64, 128), f32),
             pltpu.VMEM((2, 4, 4, 16, 2048), bf16),
             pltpu.VMEM((2, 4, 3, 16, 2048), bf16),
             pltpu.VMEM((2, 3, 16, 2048), bf16),
@@ -633,7 +671,7 @@
         return {"req": (group + d) % 4}
 
     sibling = {"ctx": chip * 2 + 1 - core}
-    partners = [device(1, 0), device(2, 0), device(3, 0), device(0, 1), device(0, 3), sibling]
+    partners = [device(1, 0), device(3, 0), device(0, 1), device(0, 3), sibling]
     partners += [plane(1), plane(2), plane(3)]
     barrier = pltpu.get_barrier_semaphore()
     for partner in partners:
@@ -665,26 +703,31 @@
     for copy in takes:
         copy.wait_recv()
 
-    def a_copy(flow, da):
-        return remote(values.at[flow, 0, 0], values.at[flow, da, 0],
-                      a_send.at[flow, da - 1], own_recv.at[flow, da],
-                      device(da if flow == 0 else 4 - da, 0))
+    def a_copy(flow, slot):
+        side_step = 1 if (flow == 0) != (slot == 2) else 3
+        return remote(values.at[flow, 1 if slot == 3 else 0, 0], values.at[flow, slot, 0],
+                      a_send.at[flow, slot - 1], own_recv.at[flow, slot], device(side_step, 0))
 
     def b_copy(flow, slot):
-        return remote(values.at[flow, slot, 0], values.at[flow, slot + 4, 0],
-                      b_send.at[flow, slot], own_recv.at[flow, slot + 4],
-                      device(0, 1 if flow == 0 else 3))
+        side_step = 1 if (flow == 0) != (slot // 4 == 2) else 3
+        return remote(values.at[flow, slot - (4 if slot < 8 else 8), 0], values.at[flow, slot, 0],
+                      b_send.at[flow, slot - 4], own_recv.at[flow, slot], device(0, side_step))
 
     def sib_copy(flow, slot):
         return remote(values.at[flow, slot, 0], values.at[flow, slot, 1],
                       sib_send.at[flow, slot], sib_recv.at[flow, slot], sibling)
 
     def forward(flow, slot):
-        if slot < 12:
-            b_copy(flow, slot).start()
         if slot == 0:
-            for da in (1, 2, 3):
-                a_copy(flow, da).start()
+            a_copy(flow, 1).start()
+            a_copy(flow, 2).start()
+        if slot == 1:
+            a_copy(flow, 3).start()
+        if slot < 4:
+            b_copy(flow, slot + 4).start()
+            b_copy(flow, slot + 8).start()
+        elif slot < 8:
+            b_copy(flow, slot + 8).start()
         sib_copy(flow, slot).start()
 
     for flow in range(2):
@@ -696,29 +739,31 @@
     for slot in range(slots):
         for flow in range(2):
             if slot:
-                (a_copy(flow, slot) if slot < 4 else b_copy(flow, slot - 4)).wait_recv()
+                (a_copy if slot < 4 else b_copy)(flow, slot).wait_recv()
                 forward(flow, slot)
         if slot % 4 != 3:
             continue
-        db = slot // 4
+        row = slot // 4
+        db = spread(row)
         for flow in range(2):
             for da in range(4):
-                sib_copy(flow, 4 * db + da).wait_recv()
-            left = values[flow, 4 * db : 4 * db + 4].reshape(128, 2048)
+                sib_copy(flow, 4 * row + da).wait_recv()
+            left = values[flow, 4 * row : 4 * row + 4].reshape(128, 2048)
             term = lax.dot_general(
                 left, weight[:, 2048 * flow : 2048 * flow + 2048],
                 (((1,), (1,)), ((), ())), preferred_element_type=jnp.float32)
-            for da in range(4):
+            for i in range(4):
+                da = spread(i)
                 ua, ub = (4 - da, 4 - db) if flow == 0 else (da, db)
                 origins = (
                     (((a + ua) % 4) * a_step + ((b + ub) % 4) * b_step) * 2 + core,
                     (((b + ua) % 4) * b_step + ((a + ub) % 4) * a_step) * 2 + 1 - core,
                 )
                 for which, origin in enumerate(origins):
-                    at = 16 * (2 * da + which)
+                    at = 16 * (2 * i + which)
                     place = pl.ds(pl.multiple_of(origin * 16, 16), 16)
-                    for i in range(2):
-                        sums[i, place] += term[at : at + 16, 128 * i : 128 * i + 128]
+                    for half in range(2):
+                        sums[half, place] += term[at : at + 16, 128 * half : 128 * half + 128]
 
     def share(d, s):
         return jnp.concatenate(
@@ -747,7 +792,7 @@
             sib_copy(flow, slot).wait_send()
             if 0 < slot < 4:
                 a_copy(flow, slot).wait_send()
-            if slot < 12:
+            if slot >= 4:
                 b_copy(flow, slot).wait_send()
 
 

time: 176 us -> 170 us (0.966)
  Pallas kernels: 173 us -> 168 us
    pallas_call x1, Pallas kernels: 136 us -> 131 us  [gather_attend(): pl.pallas_call(gather_attend_kernel, in_specs=[pl.BlockSpec(memory_space=...]
where the time goes in v6:
time: 170 us
  Pallas kernels  168 us (99%)
    pallas_call x1, Pallas kernels, gather_attend(): pl.pallas_call(gather_attend_kernel, in_specs=[pl.BlockSpec(memory_space=...  131 us
    pallas_call x1, Pallas kernels, project(): pl.pallas_call(project_kernel, in_specs=[pl.BlockSpec(memory_space=pl.ANY...  36.6 us

profile of v6, /device:TPU:0, one launch (start us, length us, event | category | flops | bytes accessed | tf_op | source)
XLA Modules:
  0.0 169.8 jit_solution(3944364594472636263)
XLA Ops:
  0.7 0.0 copy-start
  0.7 130.9 %shard_map.73 = (f32[4,8,2048]{2,1,0:T(8,128)}, bf16[3,32,512,128]{3,2,1,0:T(8,128)(2,1)}) custom-call(s32[64]{0:T(128)} %span_ref.1, s32[1]{0:T(128)S(6)} %copy.9.length_ref, s32[4,2048]{1,0:T(4,128)} %bitcast.11, bf16[4,576,128]{2,1,0:T(8,128)(2,1)} %bitcast.10, bf16[32,576,512]{2,1,0:T(8,128)(2,1)} %bitcast.9, bf16[32,512,128]{2,1,0:T(8,128)(2,1)} %up_ref.1), custom_call_target="tpu_custom_call" | custom-call | flops 19000000512 | bytes 60000000 | tf_op jit(solution)/shard_map/pallas_call | solution.py:575
  131.6 0.0 copy-done
  131.6 0.0 copy-start.1
  131.6 0.9 copy-done.1
  132.6 36.6 %shard_map.74 = bf16[4,32,224]{2,1,0:T(8,128)(2,1)S(1)} custom-call(f32[4,8,2048]{2,1,0:T(8,128)S(1)} %copy-done.1, bf16[224,4096]{1,0:T(8,128)(2,1)S(1)} %bitcast.8), custom_call_target="tpu_custom_call" | custom-call | flops 1100000000 | bytes 8000000 | tf_op jit(solution)/shard_map/pallas_call | solution.py:802
  169.2 0.7 copy.8
Async XLA Ops:
  0.7 131.0 %copy-start = (bf16[4096,224]{0,1:T(8,128)(2,1)S(1)}, bf16[4096,224]{0,1:T(8,128)(2,1)}, u32[]{:S(2)}) copy-start(bf16[4096,224]{0,1:T(8,128)(2,1)} %param.13) | copy-start | bytes 5505028
  131.6 1.0 copy-start.1

commit v7 on v6

--- a/solution.py
+++ b/solution.py
@@ -38,7 +38,7 @@
 
 
 def pack_stats(top, total):
-    lane = lax.broadcasted_iota(jnp.int32, (256, 128), 1)
+    lane = lax.broadcasted_iota(jnp.int32, (top.shape[0], 128), 1)
     high = total.astype(jnp.bfloat16).astype(jnp.float32)
     packed = jnp.where(lane == 0, top, jnp.where(lane == 1, high, total - high))
     return packed.astype(jnp.bfloat16)
@@ -54,10 +54,8 @@
 
 
 def roll_rows(block, count):
-    count = count % 8
-    if count == 0:
-        return block
-    return jnp.concatenate([block[8 - count :], block[: 8 - count]], axis=0)
+    size = block.shape[0]
+    return jnp.concatenate([block[size - count :], block[: size - count]], axis=0)
 
 
 def make_mask(span_ref, length_ref, rows_ref, line, place_in, mask_one, core, a, b):
@@ -122,27 +120,20 @@
     for partner in partners:
         pl.semaphore_signal(barrier, inc=1, device_id=partner, device_id_type=MESH)
 
-    def own_request(flow, slot):
-        da, db = spread(slot % 4), spread(slot // 4)
-        if flow == 0:
-            da, db = 4 - da, 4 - db
-        return (((a + da) % 4) * a_step + ((b + db) % 4) * b_step) * 2 + core
-
-    def sib_request(flow, slot):
-        da, db = spread(slot % 4), spread(slot // 4)
-        if flow == 0:
-            da, db = 4 - da, 4 - db
-        return (((b + da) % 4) * b_step + ((a + db) % 4) * a_step) * 2 + 1 - core
+    def requests(slot):
+        ua, ub = 4 - spread(slot % 4), 4 - spread(slot // 4)
+        return (
+            (((a + ua) % 4) * a_step + ((b + ub) % 4) * b_step) * 2 + core,
+            (((b + ua) % 4) * b_step + ((a + ub) % 4) * a_step) * 2 + 1 - core,
+        )
 
     def key_copies(slot, place):
-        copies = []
-        for flow in range(2):
-            for which, request in ((0, own_request(flow, slot)), (1, sib_request(flow, slot))):
-                at = 2 * which + flow
-                copies.append(pltpu.make_async_copy(
-                    cache_ref.at[request], keys.at[place, at, pl.ds(0, 576)],
-                    key_sem.at[place, at]))
-        return copies
+        return [
+            pltpu.make_async_copy(
+                cache_ref.at[request], keys.at[place, which, pl.ds(0, 576)],
+                key_sem.at[place, which])
+            for which, request in enumerate(requests(slot))
+        ]
 
     def remote(src, dst, send, recv, target):
         return pltpu.make_async_remote_copy(
@@ -152,13 +143,13 @@
     body = pl.ds(0, 576)
 
     def a_copy(flow, slot):
-        side_step = 1 if (flow == 0) != (slot == 2) else 3
-        return remote(own.at[flow, 1 if slot == 3 else 0, body], own.at[flow, slot, body],
+        source, side_step = ((0, 1), (0, 3), (1, 1) if flow == 0 else (2, 3))[slot - 1]
+        return remote(own.at[flow, source, body], own.at[flow, slot, body],
                       a_send.at[flow, slot - 1], own_recv.at[flow, slot], device(side_step, 0))
 
     def b_copy(flow, slot, row):
-        side_step = 1 if (flow == 0) != (row == 2) else 3
-        return remote(own.at[flow, slot - (4 if row == 1 else 8), body], own.at[flow, slot, body],
+        back, side_step = ((4, 1), (8, 3), (8, 1) if flow == 0 else (4, 3))[row - 1]
+        return remote(own.at[flow, slot - back, body], own.at[flow, slot, body],
                       b_send.at[flow, slot - 4], own_recv.at[flow, slot], device(0, side_step))
 
     def arrive(flow, slot):
@@ -169,9 +160,9 @@
         return remote(own.at[flow, slot, body], sib.at[flow, slot, body],
                       sib_send.at[flow, slot], sib_recv.at[flow, slot], sibling)
 
-    def part_copy(flow, slot):
-        return remote(to_sib.at[flow, slot % 2], from_sib.at[flow, slot % 4],
-                      part_send.at[flow, slot % 2], part_recv.at[flow, slot % 4], sibling)
+    def part_copy(slot):
+        return remote(to_sib.at[slot % 2], from_sib.at[slot % 4],
+                      part_send.at[slot % 2], part_recv.at[slot % 4], sibling)
 
     def far_copy(piece):
         quarter = pl.ds(16 * core + 8 * (piece % 2), 8)
@@ -197,16 +188,15 @@
         return remote(stats_mid, stats_b.at[d - 1], stat_b_send.at[d - 1],
                       stat_b_recv.at[d - 1], device(0, d))
 
-    def ring_copy(flow, gi, db):
-        side_step = 1 if (flow == 0) != (db == 1) else 3
-        return remote(partial.at[flow, gi, db], ring_in.at[flow, gi, db - 1],
-                      ring_send.at[flow, gi, db - 1], ring_recv.at[flow, gi, db - 1],
+    def ring_copy(half, gi, db):
+        side_step = (3, 1 if half == 0 else 3, 1)[db - 1]
+        return remote(partial.at[half, gi, db], ring_in.at[half, gi, db - 1],
+                      ring_send.at[half, gi, db - 1], ring_recv.at[half, gi, db - 1],
                       device(0, side_step))
 
-    def last_copy(flow, da):
-        return remote(last_out.at[flow, da - 1], last_in.at[flow, da - 1],
-                      last_send.at[flow, da - 1], last_recv.at[flow, da - 1],
-                      device(-da if flow == 0 else da - 4, 0))
+    def last_copy(half, da):
+        return remote(last_out.at[half, da - 1], last_in.at[half, da - 1],
+                      last_send.at[half, da - 1], last_recv.at[half, da - 1], device(-da, 0))
 
     loads = [
         pltpu.make_async_copy(
@@ -228,7 +218,6 @@
 
         def fill(slot, carry):
             da = spread(slot % 4)
-            da = da if flow == 0 else (4 - da) % 4
             hot = jnp.where(row == step + 2 * flow + 4 * da, 1.0, 0.0).astype(jnp.bfloat16)
             own[flow, slot, 576:key_rows] = hot
             sib[flow, slot, 576:key_rows] = hot
@@ -274,30 +263,28 @@
     three.start()
     three.wait_recv()
 
-    row8 = lax.broadcasted_iota(jnp.int32, (8, 128), 0)
+    row16 = lax.broadcasted_iota(jnp.int32, (16, 128), 0)
 
     def combine(slot):
         db, da = spread(slot // 4), spread(slot % 4)
-        for flow in range(2):
-            part_copy(flow, slot).wait_recv()
-            for half in range(2):
-                rows = slice(128 * half, 128 * half + 128)
-                got = from_sib[flow, slot % 4, rows, 512:640].astype(jnp.float32)
-                top_1, total_1 = own_stat[slot % 2, flow, 0, rows], own_stat[slot % 2, flow, 1, rows]
-                top_2 = jnp.broadcast_to(got[:, 0:1], (128, 128))
-                total_2 = jnp.broadcast_to(got[:, 1:2] + got[:, 2:3], (128, 128))
-                top = jnp.maximum(top_1, top_2)
-                factor_1, factor_2 = jnp.exp2(top_1 - top), jnp.exp2(top_2 - top)
-                total = factor_1 * total_1 + factor_2 * total_2
-                for i in range(4):
-                    lanes = slice(128 * i, 128 * i + 128)
-                    value = factor_1 * kept[flow, slot, rows, lanes].astype(jnp.float32)
-                    value += factor_2 * from_sib[flow, slot % 4, rows, lanes].astype(jnp.float32)
-                    kept[flow, slot, rows, lanes] = value.astype(jnp.bfloat16)
-                for i, value in enumerate((top, total)):
-                    value = jnp.swapaxes(value, 0, 1)[0:8]
-                    stats[i, flow, db] = jnp.where(
-                        row8 == 2 * da + half, value, stats[i, flow, db])
+        part_copy(slot).wait_recv()
+        for s in range(4):
+            rows = slice(128 * s, 128 * s + 128)
+            got = from_sib[slot % 4, rows, 512:640].astype(jnp.float32)
+            top_1, total_1 = own_stat[slot % 2, 0, rows], own_stat[slot % 2, 1, rows]
+            top_2 = jnp.broadcast_to(got[:, 0:1], (128, 128))
+            total_2 = jnp.broadcast_to(got[:, 1:2] + got[:, 2:3], (128, 128))
+            top = jnp.maximum(top_1, top_2)
+            factor_1, factor_2 = jnp.exp2(top_1 - top), jnp.exp2(top_2 - top)
+            total = factor_1 * total_1 + factor_2 * total_2
+            for i in range(4):
+                lanes = slice(128 * i, 128 * i + 128)
+                value = factor_1 * kept[slot, rows, lanes].astype(jnp.float32)
+                value += factor_2 * from_sib[slot % 4, rows, lanes].astype(jnp.float32)
+                kept[slot, rows, lanes] = value.astype(jnp.bfloat16)
+            for i, value in enumerate((top, total)):
+                value = jnp.swapaxes(value, 0, 1)[0:16]
+                stats[i, db] = jnp.where(row16 == 4 * da + s, value, stats[i, db])
 
     def give_credit():
         pl.semaphore_signal(credit, inc=1, device_id={"ctx": sibling}, device_id_type=MESH)
@@ -308,7 +295,7 @@
         def first_row(at):
             for flow in range(2):
                 arrive(flow, at)
-                if at == 1:
+                if at == 1 + flow:
                     a_copy(flow, 3).start()
                 b_copy(flow, 4 + at, 1).start()
                 b_copy(flow, 8 + at, 2).start()
@@ -323,16 +310,18 @@
         def _():
             first_row(3)
 
-        @pl.when((slot >= 2) & (slot < 6))
+        @pl.when((slot >= 2) & (slot < 14))
         def _():
             for flow in range(2):
                 arrive(flow, slot + 2)
-                b_copy(flow, slot + 10, 3).start()
-
-        @pl.when((slot >= 6) & (slot < 14))
-        def _():
-            for flow in range(2):
-                arrive(flow, slot + 2)
+
+        @pl.when((slot >= 2) & (slot < 6))
+        def _():
+            b_copy(0, slot + 10, 3).start()
+
+        @pl.when((slot >= 6) & (slot < 10))
+        def _():
+            b_copy(1, slot + 6, 3).start()
 
         @pl.when((slot >= 2) & (slot < 14))
         def _():
@@ -346,39 +335,33 @@
 
         for copy in key_copies(slot, place):
             copy.wait()
-        for flow in range(2):
-            db = spread(slot // 4)
-            db = db if flow == 0 else (4 - db) % 4
-            keys[place, flow, 576:key_rows] = mask_own[db]
-            keys[place, 2 + flow, 576:key_rows] = mask_sib[db]
-
-        results = [attend_unit(keys[place, flow], own[flow, slot]) for flow in range(2)]
-        for flow in range(2):
-            mixed, top, total = results[flow]
-            kept[flow, slot] = mixed
-            own_stat[place, flow, 0] = jnp.broadcast_to(top, (256, 128))
-            own_stat[place, flow, 1] = jnp.broadcast_to(total, (256, 128))
+        db = spread(slot // 4)
+        keys[place, 0, 576:key_rows] = mask_own[db]
+        keys[place, 1, 576:key_rows] = mask_sib[db]
+
+        query = jnp.concatenate([own[0, slot], own[1, slot]], axis=1)
+        mixed, top, total = attend_unit(keys[place, 0], query)
+        kept[slot] = mixed
+        own_stat[place, 0] = jnp.broadcast_to(top, (512, 128))
+        own_stat[place, 1] = jnp.broadcast_to(total, (512, 128))
 
         for flow in range(2):
             sib_copy(flow, slot).wait_recv()
 
         @pl.when(slot >= 2)
         def _():
-            for flow in range(2):
-                part_copy(flow, slot).wait_send()
-
-        results = [attend_unit(keys[place, 2 + flow], sib[flow, slot]) for flow in range(2)]
-        for flow in range(2):
-            mixed, top, total = results[flow]
-            to_sib[flow, place, :, 0:512] = mixed
-            to_sib[flow, place, :, 512:640] = pack_stats(top, total)
+            part_copy(slot).wait_send()
+
+        query = jnp.concatenate([sib[0, slot], sib[1, slot]], axis=1)
+        mixed, top, total = attend_unit(keys[place, 1], query)
+        to_sib[place, :, 0:512] = mixed
+        to_sib[place, :, 512:640] = pack_stats(top, total)
 
         @pl.when(slot >= 4)
         def _():
             pl.semaphore_wait(credit, 1)
 
-        for flow in range(2):
-            part_copy(flow, slot).start()
+        part_copy(slot).start()
 
         @pl.when(slot > 0)
         def _():
@@ -413,19 +396,18 @@
 
     def fill_group(gi):
         first_head = pl.multiple_of(32 * ((group + ahead_of[gi]) % 4), 32)
-        for flow in range(2):
-
-            def fill_wide(slot, carry):
-                place = 4 * spread(slot // 4) + spread(slot % 4)
-                for half in range(2):
-                    rows = pl.ds(pl.multiple_of(128 * half + first_head, 32), 32)
-                    value = kept[flow, slot, rows].astype(jnp.float32)
-                    at = pl.ds(pl.multiple_of(32 * (32 * flow + 2 * place + half), 32), 32)
-                    for i in range(4):
-                        wide[i, at] = value[:, 128 * i : 128 * i + 128]
-                return carry
-
-            lax.fori_loop(0, slots, fill_wide, 0)
+
+        def fill_wide(slot, carry):
+            place = 4 * spread(slot // 4) + spread(slot % 4)
+            for s in range(4):
+                rows = pl.ds(pl.multiple_of(128 * s + first_head, 32), 32)
+                value = kept[slot, rows].astype(jnp.float32)
+                at = pl.ds(pl.multiple_of(32 * (4 * place + s), 32), 32)
+                for i in range(4):
+                    wide[i, at] = value[:, 128 * i : 128 * i + 128]
+            return carry
+
+        lax.fori_loop(0, slots, fill_wide, 0)
 
     def product(gi, head):
         rows = [wide[i, pl.ds(head, 64, stride=32), :] for i in range(4)]
@@ -436,12 +418,10 @@
         lane = 32 * ahead_of[gi] + head
         return value * weight[:, lane : lane + 1]
 
-    def store_pair(gi, hj, values):
-        for flow in range(2):
-            for db in range(4):
-                at = 32 * flow + 8 * db
-                both = jnp.concatenate([value[at : at + 8] for value in values], axis=0)
-                partial[flow, gi, db, :, 128 * hj : 128 * hj + 128] = both.astype(jnp.bfloat16)
+    def store(gi, head, value):
+        lanes = slice(128 * (head % 16), 128 * (head % 16) + 128)
+        for db in range(4):
+            partial[head // 16, gi, db, :, lanes] = value[16 * db : 16 * db + 16].astype(jnp.bfloat16)
 
     ahead_of = (0, 3, 1, 2)
     up_copy(0).start()
@@ -455,13 +435,11 @@
     up_copy(0).wait()
     for d in (1, 2, 3):
         stat_a_copy(d).wait_recv()
-    for flow in range(2):
-        for db in range(4):
-            parts = [(stats[0, flow, db], stats[1, flow, db])]
-            for d in (1, 2, 3):
-                turn = 2 * d if flow == 0 else -2 * d
-                parts.append(tuple(roll_rows(stats_a[d - 1, i, flow, db], turn) for i in range(2)))
-            stats_mid[0, flow, db], stats_mid[1, flow, db] = merge_stats(parts)
+    for db in range(4):
+        parts = [(stats[0, db], stats[1, db])]
+        for d in (1, 2, 3):
+            parts.append(tuple(roll_rows(stats_a[d - 1, i, db], 4 * d) for i in range(2)))
+        stats_mid[0, db], stats_mid[1, db] = merge_stats(parts)
     for d in (1, 2, 3):
         stat_b_copy(d).start()
     for head in range(32):
@@ -471,40 +449,39 @@
         pass_copy(piece).start()
     for d in (1, 2, 3):
         stat_b_copy(d).wait_recv()
-    for flow in range(2):
-        for db in range(4):
-            parts = [(stats_mid[0, flow, db], stats_mid[1, flow, db])]
-            for d in (1, 2, 3):
-                other = (db - d) % 4 if flow == 0 else (db + d) % 4
-                parts.append((stats_b[d - 1, 0, flow, other], stats_b[d - 1, 1, flow, other]))
-            top, total = merge_stats(parts)
-            value = jnp.exp2(stats[0, flow, db] - top) / total
-            turned = value
-            for z in (1, 2, 3):
-                shifted = jnp.concatenate([value[:, 32 * z :], value[:, : 32 * z]], axis=1)
-                turned = jnp.where(group == z, shifted, turned)
-            factor[32 * flow + 8 * db : 32 * flow + 8 * db + 8] = turned
+    for db in range(4):
+        parts = [(stats_mid[0, db], stats_mid[1, db])]
+        for d in (1, 2, 3):
+            parts.append((stats_b[d - 1, 0, (db - d) % 4], stats_b[d - 1, 1, (db - d) % 4]))
+        top, total = merge_stats(parts)
+        value = jnp.exp2(stats[0, db] - top) / total
+        turned = value
+        for z in (1, 2, 3):
+            shifted = jnp.concatenate([value[:, 32 * z :], value[:, : 32 * z]], axis=1)
+            turned = jnp.where(group == z, shifted, turned)
+        factor[16 * db : 16 * db + 16] = turned
 
     def chain(gi):
-        for flow in range(2):
-            ring_copy(flow, gi, 2).wait_recv()
-            value = partial[flow, gi, 3].astype(jnp.float32)
-            value += ring_in[flow, gi, 1].astype(jnp.float32)
-            partial[flow, gi, 3] = value.astype(jnp.bfloat16)
-            ring_copy(flow, gi, 3).start()
+        for half in range(2):
+            by = 3 if half == 0 else 1
+            ring_copy(half, gi, 2).wait_recv()
+            value = partial[half, gi, by].astype(jnp.float32)
+            value += ring_in[half, gi, 1].astype(jnp.float32)
+            partial[half, gi, by] = value.astype(jnp.bfloat16)
+            ring_copy(half, gi, by).start()
 
     for gi in range(4):
         if gi:
             up_copy(gi).wait()
             fill_group(gi)
         weight = factor[...]
-        for hj in range(16):
-            values = [raw[head] if gi == 0 else product(gi, head) for head in (hj, 16 + hj)]
-            values = [scaled(gi, 16 * c + hj, value, weight) for c, value in enumerate(values)]
-            store_pair(gi, hj, values)
-        for db in (2, 1):
-            for flow in range(2):
-                ring_copy(flow, gi, db).start()
+        for head in range(32):
+            value = raw[head] if gi == 0 else product(gi, head)
+            store(gi, head, scaled(gi, head, value, weight))
+            if head % 16 == 15:
+                half = head // 16
+                ring_copy(half, gi, 2).start()
+                ring_copy(half, gi, 1 if half == 0 else 3).start()
         if gi == 0:
             for piece in (2, 3):
                 pass_copy(piece).wait_recv()
@@ -518,30 +495,25 @@
     chain(3)
 
     whole = []
-    for flow in range(2):
+    for half in range(2):
         ends = []
         for gi in range(4):
-            ring_copy(flow, gi, 1).wait_recv()
-            ring_copy(flow, gi, 3).wait_recv()
-            value = partial[flow, gi, 0].astype(jnp.float32)
-            value += ring_in[flow, gi, 0].astype(jnp.float32)
-            ends.append(value + ring_in[flow, gi, 2].astype(jnp.float32))
-
-        def rows_of(da):
-            picked = [end[8 * c + 2 * da : 8 * c + 2 * da + 2] for end in ends for c in range(2)]
-            return jnp.concatenate(picked, axis=0)
-
+            ring_copy(half, gi, 1).wait_recv()
+            ring_copy(half, gi, 3).wait_recv()
+            value = partial[half, gi, 0].astype(jnp.float32)
+            value += ring_in[half, gi, 0].astype(jnp.float32)
+            ends.append(value + ring_in[half, gi, 2].astype(jnp.float32))
         for da in (1, 2, 3):
-            last_out[flow, da - 1] = rows_of(da).astype(jnp.bfloat16)
-            last_copy(flow, da).start()
-        whole.append(rows_of(0))
-    for flow in range(2):
+            rows = [end[4 * da : 4 * da + 4] for end in ends]
+            last_out[half, da - 1] = jnp.concatenate(rows, axis=0).astype(jnp.bfloat16)
+            last_copy(half, da).start()
+        whole.append(jnp.concatenate([end[0:4] for end in ends], axis=0))
+    for half in range(2):
         for da in (1, 2, 3):
-            last_copy(flow, da).wait_recv()
-            whole[flow] = whole[flow] + last_in[flow, da - 1].astype(jnp.float32)
+            last_copy(half, da).wait_recv()
+            whole[half] = whole[half] + last_in[half, da - 1].astype(jnp.float32)
     for gi in range(4):
-        picked = [whole[flow][4 * gi + 2 * c : 4 * gi + 2 * c + 2]
-                  for c in range(2) for flow in range(2)]
+        picked = [value[4 * gi : 4 * gi + 4] for value in whole]
         out_ref[gi] = jnp.concatenate(picked, axis=0)
 
     for flow in range(2):
@@ -550,8 +522,7 @@
             return carry
 
         lax.fori_loop(0, slots, drain, 0)
-        for slot in (14, 15):
-            part_copy(flow, slot).wait_send()
+        part_copy(14 + flow).wait_send()
         for slot in range(4, 16):
             b_copy(flow, slot, slot // 4).wait_send()
         for da in (1, 2, 3):
@@ -585,11 +556,11 @@
         scratch_shapes=[
             pltpu.VMEM((2, slots, key_rows, 256), bf16),
             pltpu.VMEM((2, slots, key_rows, 256), bf16),
-            pltpu.VMEM((2, slots, 256, 512), bf16),
-            pltpu.VMEM((2, 2, 256, 640), bf16),
-            pltpu.VMEM((2, 4, 256, 640), bf16),
-            pltpu.VMEM((2, 2, 2, 256, 128), f32),
-            pltpu.VMEM((2, 4, key_rows, 512), bf16),
+            pltpu.VMEM((slots, 512, 512), bf16),
+            pltpu.VMEM((2, 512, 640), bf16),
+            pltpu.VMEM((4, 512, 640), bf16),
+            pltpu.VMEM((2, 2, 512, 128), f32),
+            pltpu.VMEM((2, 2, key_rows, 512), bf16),
             pltpu.VMEM((4, 2048), jnp.int32),
             pltpu.VMEM((4, 2048), jnp.int32),
             pltpu.VMEM((4, 2, 16, 512), bf16),
@@ -598,10 +569,10 @@
             pltpu.VMEM((4, 2, 16, 512), bf16),
             pltpu.VMEM((8, 16, 512), bf16),
             pltpu.VMEM((4, 16, 512), bf16),
-            pltpu.VMEM((2, 2, 4, 8, 128), f32),
-            pltpu.VMEM((3, 2, 2, 4, 8, 128), f32),
-            pltpu.VMEM((2, 2, 4, 8, 128), f32),
-            pltpu.VMEM((3, 2, 2, 4, 8, 128), f32),
+            pltpu.VMEM((2, 4, 16, 128), f32),
+            pltpu.VMEM((3, 2, 4, 16, 128), f32),
+            pltpu.VMEM((2, 4, 16, 128), f32),
+            pltpu.VMEM((3, 2, 4, 16, 128), f32),
             pltpu.VMEM((64, 128), f32),
             pltpu.VMEM((2, 32, 512, 128), bf16),
             pltpu.VMEM((4, 2048, 128), f32),
@@ -617,14 +588,14 @@
             dma,
             dma,
             dma((2, 2)),
-            dma((2, 4)),
+            dma((2, 2)),
             dma((2, slots)),
             dma((2, slots)),
             dma((2, 3)),
             dma((2, 12)),
             dma((2, slots)),
-            dma((2, 2)),
-            dma((2, 4)),
+            dma((2,)),
+            dma((4,)),
             pltpu.SemaphoreType.REGULAR,
             dma((6,)),
             dma((6,)),
@@ -698,19 +669,18 @@
         copy.start()
 
     weight[224:256] = jnp.zeros((32, 4096), jnp.bfloat16)
-    sums[...] = jnp.zeros_like(sums)
     loads[0].wait()
     for copy in takes:
         copy.wait_recv()
 
     def a_copy(flow, slot):
-        side_step = 1 if (flow == 0) != (slot == 2) else 3
-        return remote(values.at[flow, 1 if slot == 3 else 0, 0], values.at[flow, slot, 0],
+        source, side_step = ((0, 1), (0, 3), (1, 1) if flow == 0 else (2, 3))[slot - 1]
+        return remote(values.at[flow, source, 0], values.at[flow, slot, 0],
                       a_send.at[flow, slot - 1], own_recv.at[flow, slot], device(side_step, 0))
 
     def b_copy(flow, slot):
-        side_step = 1 if (flow == 0) != (slot // 4 == 2) else 3
-        return remote(values.at[flow, slot - (4 if slot < 8 else 8), 0], values.at[flow, slot, 0],
+        back, side_step = ((4, 1), (8, 3), (8, 1) if flow == 0 else (4, 3))[slot // 4 - 1]
+        return remote(values.at[flow, slot - back, 0], values.at[flow, slot, 0],
                       b_send.at[flow, slot - 4], own_recv.at[flow, slot], device(0, side_step))
 
     def sib_copy(flow, slot):
@@ -721,13 +691,13 @@
         if slot == 0:
             a_copy(flow, 1).start()
             a_copy(flow, 2).start()
-        if slot == 1:
+        if slot == 1 + flow:
             a_copy(flow, 3).start()
         if slot < 4:
             b_copy(flow, slot + 4).start()
             b_copy(flow, slot + 8).start()
-        elif slot < 8:
-            b_copy(flow, slot + 8).start()
+        elif slot // 4 == 1 + flow:
+            b_copy(flow, slot + (4 if flow else 8)).start()
         sib_copy(flow, slot).start()
 
     for flow in range(2):
@@ -745,25 +715,25 @@
             continue
         row = slot // 4
         db = spread(row)
+        left = []
         for flow in range(2):
-            for da in range(4):
-                sib_copy(flow, 4 * row + da).wait_recv()
-            left = values[flow, 4 * row : 4 * row + 4].reshape(128, 2048)
-            term = lax.dot_general(
-                left, weight[:, 2048 * flow : 2048 * flow + 2048],
-                (((1,), (1,)), ((), ())), preferred_element_type=jnp.float32)
             for i in range(4):
-                da = spread(i)
-                ua, ub = (4 - da, 4 - db) if flow == 0 else (da, db)
-                origins = (
-                    (((a + ua) % 4) * a_step + ((b + ub) % 4) * b_step) * 2 + core,
-                    (((b + ua) % 4) * b_step + ((a + ub) % 4) * a_step) * 2 + 1 - core,
-                )
-                for which, origin in enumerate(origins):
-                    at = 16 * (2 * i + which)
-                    place = pl.ds(pl.multiple_of(origin * 16, 16), 16)
-                    for half in range(2):
-                        sums[half, place] += term[at : at + 16, 128 * half : 128 * half + 128]
+                sib_copy(flow, 4 * row + i).wait_recv()
+            left.append(values[flow, 4 * row : 4 * row + 4].reshape(128, 2048))
+        term = lax.dot_general(
+            jnp.concatenate(left, axis=1), weight[...],
+            (((1,), (1,)), ((), ())), preferred_element_type=jnp.float32)
+        for i in range(4):
+            ua, ub = 4 - spread(i), 4 - db
+            origins = (
+                (((a + ua) % 4) * a_step + ((b + ub) % 4) * b_step) * 2 + core,
+                (((b + ua) % 4) * b_step + ((a + ub) % 4) * a_step) * 2 + 1 - core,
+            )
+            for which, origin in enumerate(origins):
+                at = 16 * (2 * i + which)
+                place = pl.ds(pl.multiple_of(origin * 16, 16), 16)
+                for half in range(2):
+                    sums[half, place] = term[at : at + 16, 128 * half : 128 * half + 128]
 
     def share(d, s):
         return jnp.concatenate(

time: 170 us -> 165 us (0.971)
  Pallas kernels: 168 us -> 163 us
    pallas_call x1, Pallas kernels: 131 us -> 126 us  [gather_attend(): pl.pallas_call(gather_attend_kernel, in_specs=[pl.BlockSpec(memory_space=...]
where the time goes in v7:
time: 165 us
  Pallas kernels  163 us (99%)
    pallas_call x1, Pallas kernels, gather_attend(): pl.pallas_call(gather_attend_kernel, in_specs=[pl.BlockSpec(memory_space=...  126 us
    pallas_call x1, Pallas kernels, project(): pl.pallas_call(project_kernel, in_specs=[pl.BlockSpec(memory_space=pl.ANY...  37.2 us

profile of v7, /device:TPU:0, one launch (start us, length us, event | category | flops | bytes accessed | tf_op | source)
XLA Modules:
  0.0 165.2 jit_solution(13317004861790930864)
XLA Ops:
  0.7 0.0 copy-start
  0.7 125.6 %shard_map.73 = (f32[4,8,2048]{2,1,0:T(8,128)}, bf16[3,32,512,128]{3,2,1,0:T(8,128)(2,1)}) custom-call(s32[64]{0:T(128)} %span_ref.1, s32[1]{0:T(128)S(6)} %copy.9.length_ref, s32[4,2048]{1,0:T(4,128)} %bitcast.11, bf16[4,576,128]{2,1,0:T(8,128)(2,1)} %bitcast.10, bf16[32,576,512]{2,1,0:T(8,128)(2,1)} %bitcast.9, bf16[32,512,128]{2,1,0:T(8,128)(2,1)} %up_ref.1), custom_call_target="tpu_custom_call" | custom-call | flops 19000000512 | bytes 60000000 | tf_op jit(solution)/shard_map/pallas_call | solution.py:546
  126.3 0.0 copy-done
  126.3 0.0 copy-start.1
  126.3 0.9 copy-done.1
  127.3 37.2 %shard_map.74 = bf16[4,32,224]{2,1,0:T(8,128)(2,1)S(1)} custom-call(f32[4,8,2048]{2,1,0:T(8,128)S(1)} %copy-done.1, bf16[224,4096]{1,0:T(8,128)(2,1)S(1)} %bitcast.8), custom_call_target="tpu_custom_call" | custom-call | flops 1100000000 | bytes 8000000 | tf_op jit(solution)/shard_map/pallas_call | solution.py:772
  164.5 0.7 copy.8
Async XLA Ops:
  0.7 125.6 %copy-start = (bf16[4096,224]{0,1:T(8,128)(2,1)S(1)}, bf16[4096,224]{0,1:T(8,128)(2,1)}, u32[]{:S(2)}) copy-start(bf16[4096,224]{0,1:T(8,128)(2,1)} %param.13) | copy-start | bytes 5505028
  126.3 1.0 copy-start.1

commit v8 on v7

--- a/solution.py
+++ b/solution.py
@@ -46,6 +46,16 @@
 
 def spread(i):
     return i + (i // 2) * (5 - 2 * i)
+
+
+def row_of(slot):
+    middle = ((slot // 4) % 3 + 1) // 2
+    return (1 - middle) * (slot // 4) + middle * (1 + slot % 2)
+
+
+def column_of(slot):
+    middle = ((slot // 4) % 3 + 1) // 2
+    return (1 - middle) * (slot % 4) + middle * ((slot + 4) // 2 - 4)
 
 
 def merge_stats(stats):
@@ -121,7 +131,7 @@
         pl.semaphore_signal(barrier, inc=1, device_id=partner, device_id_type=MESH)
 
     def requests(slot):
-        ua, ub = 4 - spread(slot % 4), 4 - spread(slot // 4)
+        ua, ub = 4 - spread(column_of(slot)), 4 - spread(row_of(slot))
         return (
             (((a + ua) % 4) * a_step + ((b + ub) % 4) * b_step) * 2 + core,
             (((b + ua) % 4) * b_step + ((a + ub) % 4) * a_step) * 2 + 1 - core,
@@ -147,9 +157,8 @@
         return remote(own.at[flow, source, body], own.at[flow, slot, body],
                       a_send.at[flow, slot - 1], own_recv.at[flow, slot], device(side_step, 0))
 
-    def b_copy(flow, slot, row):
-        back, side_step = ((4, 1), (8, 3), (8, 1) if flow == 0 else (4, 3))[row - 1]
-        return remote(own.at[flow, slot - back, body], own.at[flow, slot, body],
+    def b_copy(flow, source, slot, side_step):
+        return remote(own.at[flow, source, body], own.at[flow, slot, body],
                       b_send.at[flow, slot - 4], own_recv.at[flow, slot], device(0, side_step))
 
     def arrive(flow, slot):
@@ -217,7 +226,7 @@
     for flow in range(2):
 
         def fill(slot, carry):
-            da = spread(slot % 4)
+            da = spread(column_of(slot))
             hot = jnp.where(row == step + 2 * flow + 4 * da, 1.0, 0.0).astype(jnp.bfloat16)
             own[flow, slot, 576:key_rows] = hot
             sib[flow, slot, 576:key_rows] = hot
@@ -237,8 +246,8 @@
     for flow in range(2):
         for slot in (1, 2):
             a_copy(flow, slot).start()
-        b_copy(flow, 4, 1).start()
-        b_copy(flow, 8, 2).start()
+        b_copy(flow, 0, 4, 1).start()
+        b_copy(flow, 0, 5, 3).start()
         sib_copy(flow, 0).start()
     for copy in ones:
         copy.wait_recv()
@@ -264,9 +273,10 @@
     three.wait_recv()
 
     row16 = lax.broadcasted_iota(jnp.int32, (16, 128), 0)
+    lane = lax.broadcasted_iota(jnp.int32, (128, 128), 1)
 
     def combine(slot):
-        db, da = spread(slot // 4), spread(slot % 4)
+        db, da = spread(row_of(slot)), spread(column_of(slot))
         part_copy(slot).wait_recv()
         for s in range(4):
             rows = slice(128 * s, 128 * s + 128)
@@ -282,8 +292,9 @@
                 value = factor_1 * kept[slot, rows, lanes].astype(jnp.float32)
                 value += factor_2 * from_sib[slot % 4, rows, lanes].astype(jnp.float32)
                 kept[slot, rows, lanes] = value.astype(jnp.bfloat16)
-            for i, value in enumerate((top, total)):
-                value = jnp.swapaxes(value, 0, 1)[0:16]
+            both = jnp.swapaxes(jnp.where(lane < 64, top, total), 0, 1)
+            for i in range(2):
+                value = both[64 * i : 64 * i + 16]
                 stats[i, db] = jnp.where(row16 == 4 * da + s, value, stats[i, db])
 
     def give_credit():
@@ -297,8 +308,8 @@
                 arrive(flow, at)
                 if at == 1 + flow:
                     a_copy(flow, 3).start()
-                b_copy(flow, 4 + at, 1).start()
-                b_copy(flow, 8 + at, 2).start()
+                b_copy(flow, at, 4 + 2 * at, 1).start()
+                b_copy(flow, at, 5 + 2 * at, 3).start()
                 sib_copy(flow, at).start()
 
         @pl.when(slot == 1)
@@ -310,24 +321,30 @@
         def _():
             first_row(3)
 
-        @pl.when((slot >= 2) & (slot < 14))
+        @pl.when((slot >= 2) & (slot < 10))
         def _():
             for flow in range(2):
                 arrive(flow, slot + 2)
 
-        @pl.when((slot >= 2) & (slot < 6))
-        def _():
-            b_copy(0, slot + 10, 3).start()
-
-        @pl.when((slot >= 6) & (slot < 10))
-        def _():
-            b_copy(1, slot + 6, 3).start()
-
-        @pl.when((slot >= 2) & (slot < 14))
+        @pl.when((slot >= 2) & (slot < 10) & (slot % 2 == 0))
+        def _():
+            b_copy(0, slot + 2, 11 + slot // 2, 1).start()
+
+        @pl.when((slot >= 2) & (slot < 10) & (slot % 2 == 1))
+        def _():
+            b_copy(1, slot + 2, 11 + slot // 2, 3).start()
+
+        @pl.when((slot >= 2) & (slot < 10))
         def _():
             for flow in range(2):
                 sib_copy(flow, slot + 2).start()
 
+        @pl.when(slot >= 12)
+        def _():
+            for flow in range(2):
+                arrive(flow, slot)
+                sib_copy(flow, slot).start()
+
         @pl.when(slot < slots - 1)
         def _():
             for copy in key_copies(slot + 1, 1 - place):
@@ -335,7 +352,7 @@
 
         for copy in key_copies(slot, place):
             copy.wait()
-        db = spread(slot // 4)
+        db = spread(row_of(slot))
         keys[place, 0, 576:key_rows] = mask_own[db]
         keys[place, 1, 576:key_rows] = mask_sib[db]
 
@@ -398,7 +415,7 @@
         first_head = pl.multiple_of(32 * ((group + ahead_of[gi]) % 4), 32)
 
         def fill_wide(slot, carry):
-            place = 4 * spread(slot // 4) + spread(slot % 4)
+            place = 4 * spread(row_of(slot)) + spread(column_of(slot))
             for s in range(4):
                 rows = pl.ds(pl.multiple_of(128 * s + first_head, 32), 32)
                 value = kept[slot, rows].astype(jnp.float32)
@@ -523,8 +540,10 @@
 
         lax.fori_loop(0, slots, drain, 0)
         part_copy(14 + flow).wait_send()
-        for slot in range(4, 16):
-            b_copy(flow, slot, slot // 4).wait_send()
+        for slot in range(4, 12):
+            b_copy(flow, slot // 2 - 2, slot, 3 if slot % 2 else 1).wait_send()
+        for slot in range(12, 16):
+            b_copy(flow, 2 * slot - 20 + flow, slot, 3 if flow else 1).wait_send()
         for da in (1, 2, 3):
             a_copy(flow, da).wait_send()
             last_copy(flow, da).wait_send()

time: 165 us -> 165 us (level)
  no operation moved by 1% of the time
where the time goes in v8:
time: 165 us
  Pallas kernels  162 us (98%)
    pallas_call x1, Pallas kernels, gather_attend(): pl.pallas_call(gather_attend_kernel, in_specs=[pl.BlockSpec(memory_space=...  124 us
    pallas_call x1, Pallas kernels, project(): pl.pallas_call(project_kernel, in_specs=[pl.BlockSpec(memory_space=pl.ANY...  37.9 us

profile of v8, /device:TPU:0, one launch (start us, length us, event | category | flops | bytes accessed | tf_op | source)
XLA Modules:
  0.0 164.8 jit_solution(16276729157116793117)
XLA Ops:
  0.7 0.0 copy-start
  0.7 124.5 %shard_map.73 = (f32[4,8,2048]{2,1,0:T(8,128)}, bf16[3,32,512,128]{3,2,1,0:T(8,128)(2,1)}) custom-call(s32[64]{0:T(128)} %span_ref.1, s32[1]{0:T(128)S(6)} %copy.9.length_ref, s32[4,2048]{1,0:T(4,128)} %bitcast.11, bf16[4,576,128]{2,1,0:T(8,128)(2,1)} %bitcast.10, bf16[32,576,512]{2,1,0:T(8,128)(2,1)} %bitcast.9, bf16[32,512,128]{2,1,0:T(8,128)(2,1)} %up_ref.1), custom_call_target="tpu_custom_call" | custom-call | flops 19000000512 | bytes 60000000 | tf_op jit(solution)/shard_map/pallas_call | solution.py:565
  125.2 0.0 copy-done
  125.2 0.0 copy-start.1
  125.2 0.9 copy-done.1
  126.1 37.9 %shard_map.74 = bf16[4,32,224]{2,1,0:T(8,128)(2,1)S(1)} custom-call(f32[4,8,2048]{2,1,0:T(8,128)S(1)} %copy-done.1, bf16[224,4096]{1,0:T(8,128)(2,1)S(1)} %bitcast.8), custom_call_target="tpu_custom_call" | custom-call | flops 1100000000 | bytes 8000000 | tf_op jit(solution)/shard_map/pallas_call | solution.py:791
  164.1 0.7 copy.8
Async XLA Ops:
  0.7 124.5 %copy-start = (bf16[4096,224]{0,1:T(8,128)(2,1)S(1)}, bf16[4096,224]{0,1:T(8,128)(2,1)}, u32[]{:S(2)}) copy-start(bf16[4096,224]{0,1:T(8,128)(2,1)} %param.13) | copy-start | bytes 5505028
  125.2 1.0 copy-start.1

commit v9 on v8

--- a/solution.py
+++ b/solution.py
@@ -278,8 +278,9 @@
     def combine(slot):
         db, da = spread(row_of(slot)), spread(column_of(slot))
         part_copy(slot).wait_recv()
-        for s in range(4):
-            rows = slice(128 * s, 128 * s + 128)
+
+        def one_step(s, carry):
+            rows = pl.ds(pl.multiple_of(128 * s, 128), 128)
             got = from_sib[slot % 4, rows, 512:640].astype(jnp.float32)
             top_1, total_1 = own_stat[slot % 2, 0, rows], own_stat[slot % 2, 1, rows]
             top_2 = jnp.broadcast_to(got[:, 0:1], (128, 128))
@@ -296,6 +297,9 @@
             for i in range(2):
                 value = both[64 * i : 64 * i + 16]
                 stats[i, db] = jnp.where(row16 == 4 * da + s, value, stats[i, db])
+            return carry
+
+        lax.fori_loop(0, 4, one_step, 0)
 
     def give_credit():
         pl.semaphore_signal(credit, inc=1, device_id={"ctx": sibling}, device_id_type=MESH)
@@ -408,11 +412,11 @@
     lax.fori_loop(0, slots, iteration, 0)
 
     def up_copy(gi):
-        src = up_ref if gi == 0 else far_up.at[gi - 1]
+        src = up_ref if gi == 0 else far_up.at[(1, 0, 2)[gi - 1]]
         return pltpu.make_async_copy(src, up.at[gi % 2], up_sem.at[gi % 2])
 
     def fill_group(gi):
-        first_head = pl.multiple_of(32 * ((group + ahead_of[gi]) % 4), 32)
+        first_head = pl.multiple_of(32 * ((group + spread(gi)) % 4), 32)
 
         def fill_wide(slot, carry):
             place = 4 * spread(row_of(slot)) + spread(column_of(slot))
@@ -431,25 +435,19 @@
         rows = jnp.concatenate(rows, axis=1).astype(jnp.bfloat16)
         return jnp.dot(rows, up[gi % 2, head], preferred_element_type=jnp.float32)
 
-    def scaled(gi, head, value, weight):
-        lane = 32 * ahead_of[gi] + head
-        return value * weight[:, lane : lane + 1]
-
     def store(gi, head, value):
         lanes = slice(128 * (head % 16), 128 * (head % 16) + 128)
         for db in range(4):
             partial[head // 16, gi, db, :, lanes] = value[16 * db : 16 * db + 16].astype(jnp.bfloat16)
 
-    ahead_of = (0, 3, 1, 2)
     up_copy(0).start()
     combine(slots - 1)
     for d in (1, 2, 3):
         stat_a_copy(d).start()
-    for piece in (0, 1):
+    for piece in (2, 3):
         pass_copy(piece).wait_recv()
     up_copy(1).start()
     fill_group(0)
-    up_copy(0).wait()
     for d in (1, 2, 3):
         stat_a_copy(d).wait_recv()
     for db in range(4):
@@ -459,24 +457,24 @@
         stats_mid[0, db], stats_mid[1, db] = merge_stats(parts)
     for d in (1, 2, 3):
         stat_b_copy(d).start()
-    for head in range(32):
-        raw[head] = product(0, head)
-    for piece in (4, 5):
-        far_copy(piece).wait_recv()
-        pass_copy(piece).start()
-    for d in (1, 2, 3):
-        stat_b_copy(d).wait_recv()
-    for db in range(4):
-        parts = [(stats_mid[0, db], stats_mid[1, db])]
+    def finish_stats():
         for d in (1, 2, 3):
-            parts.append((stats_b[d - 1, 0, (db - d) % 4], stats_b[d - 1, 1, (db - d) % 4]))
-        top, total = merge_stats(parts)
-        value = jnp.exp2(stats[0, db] - top) / total
-        turned = value
-        for z in (1, 2, 3):
-            shifted = jnp.concatenate([value[:, 32 * z :], value[:, : 32 * z]], axis=1)
-            turned = jnp.where(group == z, shifted, turned)
-        factor[16 * db : 16 * db + 16] = turned
+            stat_b_copy(d).wait_recv()
+        for db in range(4):
+            parts = [(stats_mid[0, db], stats_mid[1, db])]
+            for d in (1, 2, 3):
+                parts.append((stats_b[d - 1, 0, (db - d) % 4], stats_b[d - 1, 1, (db - d) % 4]))
+            top, total = merge_stats(parts)
+            value = jnp.exp2(stats[0, db] - top) / total
+            for z in range(4):
+                shifted = value
+                if z:
+                    shifted = jnp.concatenate([value[:, 32 * z :], value[:, : 32 * z]], axis=1)
+                for gi in range(4):
+
+                    @pl.when((group + spread(gi)) % 4 == z)
+                    def _():
+                        factor[gi, 16 * db : 16 * db + 16] = shifted
 
     def chain(gi):
         for half in range(2):
@@ -487,28 +485,47 @@
             partial[half, gi, by] = value.astype(jnp.bfloat16)
             ring_copy(half, gi, by).start()
 
-    for gi in range(4):
-        if gi:
-            up_copy(gi).wait()
+    def one_group(gi, carry):
+        pltpu.make_async_copy(up_ref, up.at[gi % 2], up_sem.at[gi % 2]).wait()
+
+        @pl.when(gi > 0)
+        def _():
             fill_group(gi)
-        weight = factor[...]
+
         for head in range(32):
-            value = raw[head] if gi == 0 else product(gi, head)
-            store(gi, head, scaled(gi, head, value, weight))
+            raw[head] = product(gi, head)
+
+        @pl.when(gi == 0)
+        def _():
+            for piece in (4, 5):
+                far_copy(piece).wait_recv()
+                pass_copy(piece).start()
+            for piece in (0, 1):
+                pass_copy(piece).wait_recv()
+            up_copy(2).start()
+            finish_stats()
+
+        @pl.when(gi == 1)
+        def _():
+            for piece in (4, 5):
+                pass_copy(piece).wait_recv()
+            up_copy(3).start()
+
+        weight = factor[gi]
+        for head in range(32):
+            store(gi, head, raw[head] * weight[:, head : head + 1])
             if head % 16 == 15:
                 half = head // 16
                 ring_copy(half, gi, 2).start()
                 ring_copy(half, gi, 1 if half == 0 else 3).start()
-        if gi == 0:
-            for piece in (2, 3):
-                pass_copy(piece).wait_recv()
-            up_copy(2).start()
-        if gi == 1:
-            for piece in (4, 5):
-                pass_copy(piece).wait_recv()
-            up_copy(3).start()
-        if gi >= 1:
+
+        @pl.when(gi > 0)
+        def _():
             chain(gi - 1)
+
+        return carry
+
+    lax.fori_loop(0, 4, one_group, 0)
     chain(3)
 
     whole = []
@@ -592,7 +609,7 @@
             pltpu.VMEM((3, 2, 4, 16, 128), f32),
             pltpu.VMEM((2, 4, 16, 128), f32),
             pltpu.VMEM((3, 2, 4, 16, 128), f32),
-            pltpu.VMEM((64, 128), f32),
+            pltpu.VMEM((4, 64, 128), f32),
             pltpu.VMEM((2, 32, 512, 128), bf16),
             pltpu.VMEM((4, 2048, 128), f32),
             pltpu.VMEM((32, 64, 128), f32),
@@ -680,7 +697,7 @@
         copy.start()
     pl.semaphore_wait(barrier, len(partners))
     takes = [
-        remote(head_ref.at[(0, 2, 3, 1)[d]], taken.at[d], take_send.at[d - 1],
+        remote(head_ref.at[(0, 1, 3, 2)[d]], taken.at[d], take_send.at[d - 1],
                take_recv.at[d - 1], plane(d))
         for d in (1, 2, 3)
     ]
@@ -812,7 +829,7 @@
             dma((3,)),
         ],
         compiler_params=pltpu.CompilerParams(
-            collective_id=1, has_side_effects=True, vmem_limit_bytes=40 * 2**20
+            collective_id=1, has_side_effects=True, vmem_limit_bytes=60 * 2**20
         ),
         cost_estimate=pl.CostEstimate(
             flops=1_100_000_000, bytes_accessed=8_000_000, transcendentals=0

time: 165 us -> 173 us (1.048)
  Pallas kernels: 162 us -> 170 us
    pallas_call x1, Pallas kernels: 124 us -> 132 us  [gather_attend(): pl.pallas_call(gather_attend_kernel, in_specs=[pl.BlockSpec(memory_space=...]
where the time goes in v9:
time: 173 us; the launch traced here: 172 us
  Pallas kernels  170 us (98%)
    pallas_call x1, Pallas kernels, gather_attend(): pl.pallas_call(gather_attend_kernel, in_specs=[pl.BlockSpec(memory_space=...  132 us
    pallas_call x1, Pallas kernels, project(): pl.pallas_call(project_kernel, in_specs=[pl.BlockSpec(memory_space=pl.ANY...  38.2 us

profile of v9, /device:TPU:0, one launch (start us, length us, event | category | flops | bytes accessed | tf_op | source)
XLA Modules:
  0.0 172.4 jit_solution(9679161951665041966)
XLA Ops:
  0.7 132.1 %shard_map.73 = (f32[4,8,2048]{2,1,0:T(8,128)}, bf16[3,32,512,128]{3,2,1,0:T(8,128)(2,1)}) custom-call(s32[64]{0:T(128)} %span_ref.1, s32[1]{0:T(128)S(6)} %copy.9.length_ref, s32[4,2048]{1,0:T(4,128)} %bitcast.11, bf16[4,576,128]{2,1,0:T(8,128)(2,1)} %bitcast.10, bf16[32,576,512]{2,1,0:T(8,128)(2,1)} %bitcast.8, bf16[32,512,128]{2,1,0:T(8,128)(2,1)} %up_ref.1), custom_call_target="tpu_custom_call" | custom-call | flops 19000000512 | bytes 60000000 | tf_op jit(solution)/shard_map/pallas_call | solution.py:582
  132.7 38.2 %shard_map.74 = bf16[4,32,224]{2,1,0:T(8,128)(2,1)} custom-call(f32[4,8,2048]{2,1,0:T(8,128)} %get-tuple-element.6.head_ref, bf16[224,4096]{1,0:T(8,128)(2,1)} %bitcast.9), custom_call_target="tpu_custom_call" | custom-call | flops 1100000000 | bytes 8000000 | tf_op jit(solution)/shard_map/pallas_call | solution.py:808
  170.9 1.5 copy.8

commit v10 on v8

--- a/solution.py
+++ b/solution.py
@@ -339,11 +339,11 @@
             for flow in range(2):
                 sib_copy(flow, slot + 2).start()
 
-        @pl.when(slot >= 12)
+        @pl.when((slot >= 11) & (slot < 15))
         def _():
             for flow in range(2):
-                arrive(flow, slot)
-                sib_copy(flow, slot).start()
+                arrive(flow, slot + 1)
+                sib_copy(flow, slot + 1).start()
 
         @pl.when(slot < slots - 1)
         def _():
@@ -356,23 +356,22 @@
         keys[place, 0, 576:key_rows] = mask_own[db]
         keys[place, 1, 576:key_rows] = mask_sib[db]
 
+        for flow in range(2):
+            sib_copy(flow, slot).wait_recv()
+
+        @pl.when(slot >= 2)
+        def _():
+            part_copy(slot).wait_send()
+
         query = jnp.concatenate([own[0, slot], own[1, slot]], axis=1)
+        other = jnp.concatenate([sib[0, slot], sib[1, slot]], axis=1)
         mixed, top, total = attend_unit(keys[place, 0], query)
+        mixed_2, top_2, total_2 = attend_unit(keys[place, 1], other)
         kept[slot] = mixed
         own_stat[place, 0] = jnp.broadcast_to(top, (512, 128))
         own_stat[place, 1] = jnp.broadcast_to(total, (512, 128))
-
-        for flow in range(2):
-            sib_copy(flow, slot).wait_recv()
-
-        @pl.when(slot >= 2)
-        def _():
-            part_copy(slot).wait_send()
-
-        query = jnp.concatenate([sib[0, slot], sib[1, slot]], axis=1)
-        mixed, top, total = attend_unit(keys[place, 1], query)
-        to_sib[place, :, 0:512] = mixed
-        to_sib[place, :, 512:640] = pack_stats(top, total)
+        to_sib[place, :, 0:512] = mixed_2
+        to_sib[place, :, 512:640] = pack_stats(top_2, total_2)
 
         @pl.when(slot >= 4)
         def _():
@@ -725,14 +724,7 @@
         forward(flow, 0)
 
     loads[1].wait()
-    for slot in range(slots):
-        for flow in range(2):
-            if slot:
-                (a_copy if slot < 4 else b_copy)(flow, slot).wait_recv()
-                forward(flow, slot)
-        if slot % 4 != 3:
-            continue
-        row = slot // 4
+    def products(row):
         db = spread(row)
         left = []
         for flow in range(2):
@@ -754,6 +746,19 @@
                 for half in range(2):
                     sums[half, place] = term[at : at + 16, 128 * half : 128 * half + 128]
 
+    for slot in (0, 1, 2, 3, 4, 8, 5, 9, 6, 10, 7, 11):
+        for flow in range(2):
+            if slot:
+                (a_copy if slot < 4 else b_copy)(flow, slot).wait_recv()
+                forward(flow, slot)
+    for row in range(3):
+        products(row)
+    for slot in (12, 13, 14, 15):
+        for flow in range(2):
+            b_copy(flow, slot).wait_recv()
+            forward(flow, slot)
+    products(3)
+
     def share(d, s):
         return jnp.concatenate(
             [sums[i, pl.ds(4 * d + s, 32, stride=16), :] for i in range(2)], axis=1)

time: 165 us -> 159 us (0.964)
  Pallas kernels: 162 us -> 156 us
    pallas_call x1, Pallas kernels: 124 us -> 119 us  [gather_attend(): pl.pallas_call(gather_attend_kernel, in_specs=[pl.BlockSpec(memory_space=...]
where the time goes in v10:
time: 159 us; the launch traced here: 158 us
  Pallas kernels  156 us (98%)
  local copies, waits for them, and re-layouts  1.63 us (1%)
    pallas_call x1, Pallas kernels, gather_attend(): pl.pallas_call(gather_attend_kernel, in_specs=[pl.BlockSpec(memory_space=...  119 us
    pallas_call x1, Pallas kernels, project(): pl.pallas_call(project_kernel, in_specs=[pl.BlockSpec(memory_space=pl.ANY...  36.9 us

profile of v10, /device:TPU:0, one launch (start us, length us, event | category | flops | bytes accessed | tf_op | source)
XLA Modules:
  0.0 158.1 jit_solution(3655920511506008332)
XLA Ops:
  0.7 0.0 copy-start
  0.7 118.8 %shard_map.73 = (f32[4,8,2048]{2,1,0:T(8,128)}, bf16[3,32,512,128]{3,2,1,0:T(8,128)(2,1)}) custom-call(s32[64]{0:T(128)} %span_ref.1, s32[1]{0:T(128)S(6)} %copy.9.length_ref, s32[4,2048]{1,0:T(4,128)} %bitcast.11, bf16[4,576,128]{2,1,0:T(8,128)(2,1)} %bitcast.10, bf16[32,576,512]{2,1,0:T(8,128)(2,1)} %bitcast.9, bf16[32,512,128]{2,1,0:T(8,128)(2,1)} %up_ref.1), custom_call_target="tpu_custom_call" | custom-call | flops 19000000512 | bytes 60000000 | tf_op jit(solution)/shard_map/pallas_call | solution.py:564
  119.5 0.0 copy-done
  119.5 0.0 copy-start.1
  119.5 0.9 copy-done.1
  120.4 36.9 %shard_map.74 = bf16[4,32,224]{2,1,0:T(8,128)(2,1)S(1)} custom-call(f32[4,8,2048]{2,1,0:T(8,128)S(1)} %copy-done.1, bf16[224,4096]{1,0:T(8,128)(2,1)S(1)} %bitcast.8), custom_call_target="tpu_custom_call" | custom-call | flops 1100000000 | bytes 8000000 | tf_op jit(solution)/shard_map/pallas_call | solution.py:796
  157.4 0.7 copy.8
Async XLA Ops:
  0.7 118.8 %copy-start = (bf16[4096,224]{0,1:T(8,128)(2,1)S(1)}, bf16[4096,224]{0,1:T(8,128)(2,1)}, u32[]{:S(2)}) copy-start(bf16[4096,224]{0,1:T(8,128)(2,1)} %param.13) | copy-start | bytes 5505028
  119.5 1.0 copy-start.1
